TPU v7x, 32 devices: a whole 2x2x4 slice. The times are simulated.
32 devices in a mesh: res: 16 (over z, y, x), nbr: 2 (over core).
Axes of the slice: x: 2, y: 2, z: 4, core: 2. Of those that a mesh axis runs over, the one named last changes fastest.
Arguments:
- nodes: bfloat16 [16384, 512], P(('res', 'nbr')), may hold values from -6 to 6
- edges: bfloat16 [16384, 60, 192], P('res', 'nbr'), may hold values from -6 to 6
- neighbours: int32 [16384, 60], P('res', 'nbr'), may hold values from 0 to 16383, as said below
- lengths: int32 [16], replicated, may hold values from 60 to 1024, as said below
- message_receiver_weight: bfloat16 [512, 512], replicated, may hold values from -0.15625 to 0.15625
- message_neighbour_weight: bfloat16 [512, 512], replicated, may hold values from -0.15625 to 0.15625
- message_edge_weight: bfloat16 [192, 512], replicated, may hold values from -0.15625 to 0.15625
- message_hidden_bias: float32 [512], replicated, may hold values from -3 to 3
- message_output_weight: bfloat16 [512, 512], replicated, may hold values from -1 to 1
- gain_one: float32 [512], replicated, may hold values from 0.25 to 1.75
- ffn_in: bfloat16 [512, 2048], replicated, may hold values from -0.25 to 0.25
- ffn_bias: float32 [2048], replicated, may hold values from -3 to 3
- ffn_out: bfloat16 [2048, 512], replicated, may hold values from -0.125 to 0.125
- gain_two: float32 [512], replicated, may hold values from 0.25 to 1.75
- edge_update_residue_weight: bfloat16 [512, 192], replicated, may hold values from -0.15625 to 0.15625
- edge_update_neighbour_weight: bfloat16 [512, 192], replicated, may hold values from -0.15625 to 0.15625
- edge_update_edge_weight: bfloat16 [192, 192], replicated, may hold values from -0.15625 to 0.15625
- edge_update_bias: float32 [192], replicated, may hold values from -3 to 3
- edge_out: bfloat16 [192, 192], replicated, may hold values from -0.4375 to 0.4375
- gain_three: float32 [192], replicated, may hold values from 0.25 to 1.75
- node_cot: bfloat16 [16384, 512], P(('res', 'nbr')), may hold values from -6 to 6
- edge_cot: bfloat16 [16384, 60, 192], P('res', 'nbr'), may hold values from -6 to 6
Outputs:
- node_out: bfloat16 [16384, 512], P(('res', 'nbr'))
- edge_new: bfloat16 [16384, 60, 192], P('res', 'nbr')
- node_grad: float32 [16384, 512], P(('res', 'nbr'))
- edge_grad: float32 [16384, 60, 192], P('res', 'nbr')
- grad_msg_self: float32 [512, 512], replicated
- grad_msg_nbr: float32 [512, 512], replicated
- grad_msg_edge: float32 [192, 512], replicated
- grad_msg_bias: float32 [512], replicated
- grad_msg_out: float32 [512, 512], replicated
- grad_gain_one: float32 [512], replicated
- grad_ffn_in: float32 [512, 2048], replicated
- grad_ffn_bias: float32 [2048], replicated
- grad_ffn_out: float32 [2048, 512], replicated
- grad_gain_two: float32 [512], replicated
- grad_edge_self: float32 [512, 192], replicated
- grad_edge_nbr: float32 [512, 192], replicated
- grad_edge_edge: float32 [192, 192], replicated
- grad_edge_bias: float32 [192], replicated
- grad_edge_out: float32 [192, 192], replicated
- grad_gain_three: float32 [192], replicated
Inputs may be any that keep to these rules, and one draw needn't show every extreme that they name: `neighbours`: every entry names a slot of the residue's own bucket, slots b * 1024 to (b + 1) * 1024 - 1 for bucket b. Even-numbered entries lie within 30 positions of the residue, inside its protein where the residue is a real one; odd-numbered entries lie anywhere in the bucket, padding slots included. `lengths`: the last bucket holds a protein of 1024 residues; the others vary.
All inputs are finite; a program needn't handle non-finite values.
Results may differ from a plain program's by a relative error of at most 0.014.
Values may be sent and summed in bfloat16 or wider, within the bound.
No kernel may reach another device: no remote copies, remote signals or barrier semaphores. Data moves between devices by JAX's collectives and lax.ppermute only.
A program may use at most 576 MiB of HBM per device.

v0:
```python
import jax
import jax.numpy as jnp
from jax import lax
from jax.sharding import PartitionSpec as P

SPAN = 1024


epsilon = 1e-05
highest_precision = lax.Precision.HIGHEST
root_half = 0.7071067811865476
inv_root_two_pi = 0.3989422804014327


def swapped(value, axis, distance):
    mask = 2**distance
    pairs = [(source, source ^ mask) for source in range(lax.axis_size(axis))]
    return lax.ppermute(value, axis, pairs)


def gelu_slope(values):
    return (
        0.5 * (1.0 + lax.erf(values * root_half))
        + values * jnp.exp(-0.5 * values * values) * inv_root_two_pi
    )


def layer_norm(values, gain_vec):
    mean_val = jnp.mean(values, -1, keepdims=True)
    centered = values - mean_val
    variance = jnp.mean(centered * centered, -1, keepdims=True)
    return centered * lax.rsqrt(variance + epsilon) * gain_vec


def norm_back(values, gain_vec, grad_out):
    mean_val = jnp.mean(values, -1, keepdims=True)
    centered = values - mean_val
    inv_std = lax.rsqrt(jnp.mean(centered * centered, -1, keepdims=True) + epsilon)
    normed = centered * inv_std
    grad_gain = jnp.sum(grad_out * normed, axis=0)
    grad_normed = grad_out * gain_vec
    grad_in = inv_std * (
        grad_normed
        - jnp.mean(grad_normed, -1, keepdims=True)
        - normed * jnp.mean(grad_normed * normed, -1, keepdims=True)
    )
    return (grad_in, grad_gain)


def valid_of(slot_ids, lengths):
    buckets = lengths.shape[0]
    matches = (slot_ids // SPAN)[:, None] == jnp.arange(buckets, dtype=jnp.int32)[None, :]
    true_len = jnp.sum(jnp.where(matches, lengths[None, :], 0), axis=1)
    return (slot_ids % SPAN < true_len).astype(jnp.float32)


def product(left_op, right_op):
    return jnp.dot(left_op, right_op, preferred_element_type=jnp.float32)


def inner_rows(left_op, right_op):
    return lax.dot_general(
        left_op, right_op, (((0,), (0,)), ((), ())), preferred_element_type=jnp.float32
    )


def times_transposed(left_op, right_op):
    return lax.dot_general(
        left_op, right_op, (((1,), (1,)), ((), ())), preferred_element_type=jnp.float32
    )


def exact_inner(left_op, right_op):
    return lax.dot_general(
        left_op,
        right_op,
        (((0,), (0,)), ((), ())),
        precision=highest_precision,
        preferred_element_type=jnp.float32,
    )


def exact_transposed(left_op, right_op):
    return lax.dot_general(
        left_op,
        right_op,
        (((1,), (1,)), ((), ())),
        precision=highest_precision,
        preferred_element_type=jnp.float32,
    )


def joined(table, other, high_side):
    return jnp.where(
        high_side, jnp.concatenate([other, table], axis=0), jnp.concatenate([table, other], axis=0)
    )


def halves(table, high_side):
    half = table.shape[0] // 2
    lower, upper = (table[:half], table[half:])
    return (jnp.where(high_side, upper, lower), jnp.where(high_side, lower, upper))


def gather_nodes(table, dev_index, levels):
    for level in range(levels):
        other = swapped(table, ("res", "nbr"), level)
        table = joined(table, other, dev_index >> level & 1 == 1)
    return table


def gather_states(table, dev_index, levels):
    for level in range(levels):
        other = swapped(table, ("res", "nbr"), level)
        table = joined(table, other, dev_index >> level & 1 == 1)
    return table


def sum_state_grads(table, dev_index, levels):
    for level in reversed(range(levels)):
        keep, send = halves(table, dev_index >> level & 1 == 1)
        table = keep + swapped(send.astype(jnp.bfloat16), ("res", "nbr"), level).astype(send.dtype)
    return table


def sum_message_grads(table, dev_index, levels):
    for level in reversed(range(levels)):
        keep, send = halves(table, dev_index >> level & 1 == 1)
        table = keep + swapped(send.astype(jnp.bfloat16), ("res", "nbr"), level).astype(send.dtype)
    return table


def on_device(
    nodes,
    edges,
    neighbours,
    lengths,
    message_receiver_weight,
    message_neighbour_weight,
    message_edge_weight,
    message_hidden_bias,
    message_output_weight,
    gain_one,
    ffn_in,
    ffn_bias,
    ffn_out,
    gain_two,
    edge_update_residue_weight,
    edge_update_neighbour_weight,
    edge_update_edge_weight,
    edge_update_bias,
    edge_out,
    gain_three,
    node_cot,
    edge_cot,
):
    block_len, half_k, edge_width = edges.shape
    model_width = nodes.shape[1]
    group_size = SPAN // nodes.shape[0]
    levels = group_size.bit_length() - 1
    dev_index = lax.axis_index("res") * lax.axis_size("nbr") + lax.axis_index("nbr")
    first_row = lax.axis_index("res") * block_len
    group_start = first_row // SPAN * SPAN
    local_first = first_row - group_start
    own_ids = first_row + jnp.arange(block_len, dtype=jnp.int32)
    flat_ids = neighbours.reshape(-1)
    local_ids = flat_ids - group_start
    edge_flat = edges.reshape(-1, edge_width)
    edge_weight = valid_of(own_ids, lengths)[:, None] * valid_of(flat_ids, lengths).reshape(
        block_len, half_k
    )
    both_ids = jnp.concatenate([flat_ids, own_ids]) - group_start
    node_table = gather_nodes(nodes, dev_index, levels)
    block_nodes = lax.dynamic_slice_in_dim(node_table, local_first, block_len, 0)
    near_nodes = jnp.take(node_table, local_ids, axis=0)
    pre_msg = (
        product(block_nodes, message_receiver_weight)[:, None, :]
        + (
            product(near_nodes, message_neighbour_weight) + product(edge_flat, message_edge_weight)
        ).reshape(block_len, half_k, model_width)
        + message_hidden_bias
    ).reshape(-1, model_width)
    act_msg = jax.nn.gelu(pre_msg, approximate=False).astype(jnp.bfloat16)
    message_value = product(act_msg, message_output_weight).reshape(block_len, half_k, model_width)
    partial_value = jnp.sum(edge_weight[:, :, None] * message_value, axis=1)
    msg_sums, counts = (
        lax.psum_scatter(partial_value, "nbr", scatter_dimension=0, tiled=True),
        lax.psum_scatter(jnp.sum(edge_weight, axis=1), "nbr", scatter_dimension=0, tiled=True),
    )
    divisor = jnp.maximum(counts, 1.0)[:, None]
    first_sum = nodes.astype(jnp.float32) + msg_sums / divisor
    first_norm = layer_norm(first_sum, gain_one)
    ffn_input = first_norm.astype(jnp.bfloat16)
    pre_ffn = product(ffn_input, ffn_in) + ffn_bias
    act_ffn = jax.nn.gelu(pre_ffn, approximate=False).astype(jnp.bfloat16)
    second_sum = first_norm + product(act_ffn, ffn_out)
    node_state = layer_norm(second_sum, gain_two).astype(jnp.bfloat16)
    state_table = gather_states(node_state, dev_index, levels)
    block_state = lax.dynamic_slice_in_dim(state_table, local_first, block_len, 0)
    near_state = jnp.take(state_table, local_ids, axis=0)
    near_proj = product(near_state, edge_update_neighbour_weight)
    pre_edge = (
        product(block_state, edge_update_residue_weight)[:, None, :]
        + (near_proj + product(edge_flat, edge_update_edge_weight)).reshape(
            block_len, half_k, edge_width
        )
        + edge_update_bias
    ).reshape(-1, edge_width)
    act_edge = jax.nn.gelu(pre_edge, approximate=False).astype(jnp.bfloat16)
    third_sum = edge_flat.astype(jnp.float32) + product(act_edge, edge_out)
    new_edges = layer_norm(third_sum, gain_three).astype(jnp.bfloat16)
    grad_third, grad_gain_three = norm_back(
        third_sum, gain_three, edge_cot.reshape(-1, edge_width).astype(jnp.float32)
    )
    grad_branch = grad_third.astype(jnp.bfloat16)
    grad_edge_out = inner_rows(act_edge, grad_branch)
    grad_pre_edge = (times_transposed(grad_branch, edge_out) * gelu_slope(pre_edge)).astype(
        jnp.bfloat16
    )
    grad_pre_wide = grad_pre_edge.astype(jnp.float32)
    grad_edge_bias = jnp.sum(grad_pre_wide, axis=0)
    grad_edge_edge = inner_rows(edge_flat, grad_pre_edge)
    grad_edge_block = jnp.sum(grad_pre_wide.reshape(block_len, half_k, edge_width), axis=1)
    grad_edge_self = exact_inner(block_state.astype(jnp.float32), grad_edge_block)
    block_back = exact_transposed(grad_edge_block, edge_update_residue_weight.astype(jnp.float32))
    grad_edge_nbr = inner_rows(near_state, grad_pre_edge)
    grad_table = (
        jnp.zeros((SPAN, model_width), jnp.float32)
        .at[both_ids]
        .add(
            jnp.concatenate(
                [times_transposed(grad_pre_edge, edge_update_neighbour_weight), block_back], axis=0
            )
        )
    )
    state_grad = sum_state_grads(grad_table, dev_index, levels)
    state_total = node_cot.astype(jnp.float32) + state_grad
    grad_second, grad_gain_two = norm_back(second_sum, gain_two, state_total)
    grad_ffn_top = grad_second.astype(jnp.bfloat16)
    grad_ffn_out = inner_rows(act_ffn, grad_ffn_top)
    grad_pre_ffn = (times_transposed(grad_ffn_top, ffn_out) * gelu_slope(pre_ffn)).astype(
        jnp.bfloat16
    )
    grad_ffn_bias = jnp.sum(grad_pre_ffn.astype(jnp.float32), axis=0)
    grad_ffn_in = inner_rows(ffn_input, grad_pre_ffn)
    grad_first_norm = grad_second + times_transposed(grad_pre_ffn, ffn_in)
    grad_first, grad_gain_one = norm_back(first_sum, gain_one, grad_first_norm)
    scaled = lax.all_gather(
        (grad_first / divisor).astype(jnp.bfloat16), "nbr", axis=0, tiled=True
    ).astype(jnp.float32)
    grad_message = (
        (edge_weight[:, :, None] * scaled[:, None, :]).reshape(-1, model_width).astype(jnp.bfloat16)
    )
    grad_msg_out = inner_rows(act_msg, grad_message)
    grad_pre_msg = (
        times_transposed(grad_message, message_output_weight) * gelu_slope(pre_msg)
    ).astype(jnp.bfloat16)
    grad_msg_wide = grad_pre_msg.astype(jnp.float32)
    grad_msg_bias = jnp.sum(grad_msg_wide, axis=0)
    grad_msg_edge = inner_rows(edge_flat, grad_pre_msg)
    grad_msg_nbr = inner_rows(near_nodes, grad_pre_msg)
    grad_msg_block = jnp.sum(grad_msg_wide.reshape(block_len, half_k, model_width), axis=1)
    grad_msg_self = exact_inner(block_nodes.astype(jnp.float32), grad_msg_block)
    node_table_grad = (
        jnp.zeros((SPAN, model_width), jnp.float32)
        .at[both_ids]
        .add(
            jnp.concatenate(
                [
                    times_transposed(grad_pre_msg, message_neighbour_weight),
                    exact_transposed(grad_msg_block, message_receiver_weight.astype(jnp.float32)),
                ],
                axis=0,
            )
        )
    )
    node_grad = grad_first + sum_message_grads(node_table_grad, dev_index, levels)
    edge_grad = (
        grad_third
        + times_transposed(grad_pre_edge, edge_update_edge_weight)
        + times_transposed(grad_pre_msg, message_edge_weight)
    ).reshape(block_len, half_k, edge_width)
    (
        grad_msg_self,
        grad_msg_nbr,
        grad_msg_edge,
        grad_msg_bias,
        grad_msg_out,
        grad_gain_one,
        grad_ffn_in,
        grad_ffn_bias,
        grad_ffn_out,
        grad_gain_two,
        grad_edge_self,
        grad_edge_nbr,
        grad_edge_edge,
        grad_edge_bias,
        grad_edge_out,
        grad_gain_three,
    ) = lax.psum(
        (
            grad_msg_self,
            grad_msg_nbr,
            grad_msg_edge,
            grad_msg_bias,
            grad_msg_out,
            grad_gain_one,
            grad_ffn_in,
            grad_ffn_bias,
            grad_ffn_out,
            grad_gain_two,
            grad_edge_self,
            grad_edge_nbr,
            grad_edge_edge,
            grad_edge_bias,
            grad_edge_out,
            grad_gain_three,
        ),
        ("res", "nbr"),
    )
    return (
        node_state,
        new_edges.reshape(block_len, half_k, edge_width),
        node_grad,
        edge_grad,
        grad_msg_self,
        grad_msg_nbr,
        grad_msg_edge,
        grad_msg_bias,
        grad_msg_out,
        grad_gain_one,
        grad_ffn_in,
        grad_ffn_bias,
        grad_ffn_out,
        grad_gain_two,
        grad_edge_self,
        grad_edge_nbr,
        grad_edge_edge,
        grad_edge_bias,
        grad_edge_out,
        grad_gain_three,
    )


def solution(mesh):
    placed = (
        P(("res", "nbr"), None),
        P("res", "nbr", None),
        P("res", "nbr"),
        P(),
        P(),
        P(),
        P(),
        P(),
        P(),
        P(),
        P(),
        P(),
        P(),
        P(),
        P(),
        P(),
        P(),
        P(),
        P(),
        P(),
        P(("res", "nbr"), None),
        P("res", "nbr", None),
    )
    return jax.shard_map(
        on_device,
        mesh=mesh,
        in_specs=placed,
        out_specs=(
            P(("res", "nbr"), None),
            P("res", "nbr", None),
            P(("res", "nbr"), None),
            P("res", "nbr", None),
            P(),
            P(),
            P(),
            P(),
            P(),
            P(),
            P(),
            P(),
            P(),
            P(),
            P(),
            P(),
            P(),
            P(),
            P(),
            P(),
        ),
        check_vma=False,
    )
```

profile of v0, /device:TPU:0, one launch (start us, length us, event | category | flops | bytes accessed | tf_op | source)
XLA Modules:
  0.0 2301.8 jit_solution(11289769630775640089)
XLA Ops:
  19.2 23.7 %copy.142 = bf16[1024,30,192]{2,1,0:T(8,128)(2,1)} copy(bf16[1024,30,192]{0,2,1:T(8,128)(2,1)} %param.25) | data formatting | bytes 23592960 | tf_op args[1]
  43.0 24.3 %reshape.262 = bf16[30720,192]{1,0:T(8,128)(2,1)} reshape(bf16[1024,30,192]{2,1,0:T(8,128)(2,1)} %copy.142) | data formatting | bytes 23592960 | tf_op jit(solution)/shard_map/reshape | solution.py:168
  73.4 21.4 add.243
  94.8 63.1 %add.244 = f32[30720,512]{1,0:T(8,128)} reshape(f32[1024,30,512]{2,1,0:T(8,128)} %add.243) | data formatting | bytes 125829120 | tf_op jit(solution)/shard_map/add | solution.py:177
  158.0 123.1 %gather_fusion = bf16[30720,512]{1,0:T(8,128)(2,1)} fusion(bf16[1024,512]{1,0:T(8,128)(2,1)S(1)} %copy.141, s32[30720]{0:T(1024)S(1)} %get-tuple-element.136), kind=kCustom, calls=%fused_computation.clone | custom fusion | bytes 63037440 | tf_op jit(solution)/shard_map/jit(_take)/gather | solution.py:175
  281.1 34.4 %fusion.46 = f32[30720,512]{1,0:T(8,128)} fusion(bf16[512,512]{1,0:T(8,128)(2,1)} %param.29, bf16[30720,512]{1,0:T(8,128)(2,1)} %gather_fusion, pred[30720]{0:T(1024)(128)(4,1)S(1)} %compare_and_fusion), kind=kOutput, calls=%fused_computation.86 | convolution fusion | flops 16121856000 | bytes 94926848 | tf_op jit(solution)/shard_map/dot_general | solution.py:58
  315.5 149.2 %fusion.10 = (bf16[30720,512]{1,0:T(8,128)(2,1)}, f32[30720,512]{1,0:T(8,128)}) fusion(f32[512]{0:T(512)S(1)} %copy-done.76, f32[30720,512]{1,0:T(8,128)} %add.244, f32[30720,512]{1,0:T(8,128)} %fusion.46, bf16[30720,192]{1,0:T(8,128)(2,1)} %reshape.262, bf16[192,512]{1,0:T(8,128)(2,1)S(1)} %copy-done.32), kind=kOutput, calls=%fused_computation.16 | convolution fusion | flops 7109345280 | bytes 232196096 | tf_op jit(solution)/shard_map/dot_general | solution.py:58
  464.7 40.9 %dot_general.99 = bf16[1024,30,512]{2,1,0:T(8,128)(2,1)} reshape(bf16[30720,512]{1,0:T(8,128)(2,1)} %get-tuple-element.138) | data formatting | bytes 62914560 | tf_op jit(solution)/shard_map/dot_general | solution.py:58
  505.7 55.7 %multiply_reduce_fusion = f32[1024,512]{1,0:T(8,128)} fusion(f32[1024,30]{0,1:T(8,128)S(1)} %copy-done.35, bf16[1024,30,512]{2,1,0:T(8,128)(2,1)} %dot_general.99, bf16[512,512]{1,0:T(8,128)(2,1)S(1)} %copy-done.72), kind=kOutput, calls=%fused_computation.24 | convolution fusion | flops 16137060352 | bytes 34201600 | tf_op jit(solution)/shard_map/dot_general | solution.py:58
  564.4 14.6 fusion.102
  585.8 11.6 fusion.53
  600.5 7.7 multiply_reduce_fusion.3
  609.1 18.1 copy.145
  627.2 25.8 %copy.152 = f32[1024,30,192]{2,1,0:T(8,128)} copy(bf16[1024,30,192]{0,2,1:T(8,128)(2,1)} %param.45) | data formatting | bytes 35389440 | tf_op jit(solution)/shard_map/convert_element_type | solution.py:213
  656.4 33.2 %reshape.267 = f32[30720,192]{1,0:T(8,128)} reshape(f32[1024,30,192]{2,1,0:T(8,128)} %copy.152) | data formatting | bytes 47185920 | tf_op jit(solution)/shard_map/convert_element_type | solution.py:213
  689.6 28.1 %copy.153 = f32[30720,192]{0,1:T(8,128)} copy(f32[30720,192]{1,0:T(8,128)} %reshape.267) | data formatting | bytes 47185920 | tf_op jit(solution)/shard_map/convert_element_type | solution.py:213
  725.3 123.0 %gather_fusion.1 = bf16[30720,512]{1,0:T(8,128)(2,1)} fusion(bf16[1024,512]{1,0:T(8,128)(2,1)S(1)} %copy.147, s32[30720]{0:T(1024)S(1)} %copy-done.21), kind=kCustom, calls=%fused_computation.1.clone | custom fusion | bytes 63037440 | tf_op jit(solution)/shard_map/jit(_take)/gather | solution.py:200
  848.4 12.0 add.255
  860.4 33.2 %add.256 = f32[30720,192]{1,0:T(8,128)} reshape(f32[1024,30,192]{2,1,0:T(8,128)} %add.255) | data formatting | bytes 47185920 | tf_op jit(solution)/shard_map/add | solution.py:203
  893.6 28.1 %copy.148 = f32[30720,192]{0,1:T(8,128)} copy(f32[30720,192]{1,0:T(8,128)} %add.256) | data formatting | bytes 47185920 | tf_op jit(solution)/shard_map/add | solution.py:203
  921.7 73.8 %fusion.31 = (bf16[30720,192]{0,1:T(8,128)(2,1)}, f32[30720,192]{0,1:T(8,128)}) fusion(f32[192]{0:T(256)S(1)} %copy-done.77, f32[30720,192]{0,1:T(8,128)} %copy.148, f32[30720,192]{0,1:T(8,128)} %fusion.102, bf16[512,192]{0,1:T(8,128)(2,1)S(1)} %copy-done.30, bf16[30720,512]{1,0:T(8,128)(2,1)} %gather_fusion.1, pred[30720]{0:T(1024)(128)(4,1)S(1)} %copy-done.51), kind=kOutput, calls=%fused_computation.57 | convolution fusion | flops 6456606720 | bytes 114260736 | tf_op jit(solution)/shard_map/dot_general | solution.py:58
  995.5 15.0 fusion.99
  1010.5 10.7 multiply_reduce_fusion.4
  1021.3 3.7 copy-done.1
  1025.0 13.1 multiply_reduce_fusion.1
  1038.1 21.8 subtract_multiply_fusion
  1059.8 19.6 convert_reduce_fusion.1
  1079.4 4.3 copy-done.2
  1083.7 24.0 %fusion.47 = f32[512,192]{0,1:T(8,128)} fusion(bf16[30720,192]{0,1:T(8,128)(2,1)S(1)} %get-tuple-element.154, bf16[30720,512]{1,0:T(8,128)(2,1)} %gather_fusion.1, pred[30720]{0:T(1024)(128)(4,1)S(1)} %copy-done.51), kind=kOutput, calls=%fused_computation.87 | convolution fusion | flops 6055526400 | bytes 43677696 | tf_op jit(solution)/shard_map/dot_general | solution.py:62
  1107.8 22.3 convolution_add_fusion.3
  1130.1 12.7 convolution_bitcast_fusion.1
  1142.8 19.9 copy.155
  1162.7 26.3 %fusion.103 = f32[30720,512]{1,0:T(8,128)} fusion(bf16[30720,192]{0,1:T(8,128)(2,1)} %copy-done.2, bf16[512,192]{0,1:T(8,128)(2,1)S(1)} %copy-done.31), kind=kOutput, calls=%fused_computation.216 | convolution fusion | flops 6039797760 | bytes 74907648 | tf_op jit(solution)/shard_map/dot_general | solution.py:68
  1189.0 33.2 %reshape.264 = f32[1024,30,192]{2,1,0:T(8,128)} reshape(f32[30720,192]{1,0:T(8,128)} %copy.155) | data formatting | bytes 47185920 | tf_op jit(solution)/shard_map/reshape | solution.py:223
  1222.2 13.5 reduce_sum.255
  1238.1 197.4 %scatter_custom_fusion = f32[1024,512]{1,0:T(8,128)} fusion(s32[31744]{0:T(1024)} %bitcast.60, f32[1024,512]{1,0:T(8,128)} %fusion.104, f32[]{:T(128)} %constant.103, f32[30720,512]{1,0:T(8,128)} %fusion.103, f32[]{:T(128)} %constant.63.clone.1), kind=kCustom, calls=%fused_computation.6 | custom fusion | flops 32505856 | bytes 67109888 | tf_op jit(solution)/shard_map/scatter-add | solution.py:230
  1445.6 15.0 fusion.48
  1460.5 17.9 copy.149
  1478.4 24.2 %reshape.263 = bf16[1024,30,192]{2,1,0:T(8,128)(2,1)} reshape(bf16[30720,192]{1,0:T(8,128)(2,1)} %copy.149) | data formatting | bytes 23592960 | tf_op jit(solution)/shard_map/reshape | solution.py:323
  1502.7 22.4 copy.164
  1529.6 5.8 convert_reduce_fusion.2
  1539.8 3.3 fusion.108
  1543.1 5.2 fusion.73
  1548.3 5.1 fusion.90
  1556.1 22.5 mul.374
  1578.6 63.1 %mul.375 = f32[30720,512]{1,0:T(8,128)} reshape(f32[1024,30,512]{2,1,0:T(8,128)} %mul.374) | data formatting | bytes 125829120 | tf_op jit(solution)/shard_map/mul | solution.py:252
  1641.7 33.8 %fusion.92 = f32[512,512]{1,0:T(8,128)} fusion(bf16[30720,512]{1,0:T(8,128)(2,1)} %get-tuple-element.138, f32[30720,512]{1,0:T(8,128)} %mul.375, f32[30720]{0:T(1024)S(1)} %copy-done.24), kind=kOutput, calls=%fused_computation.206 | convolution fusion | flops 16137584640 | bytes 95543296 | tf_op jit(solution)/shard_map/dot_general | solution.py:62
  1675.5 60.9 %convert_reduce_fusion = (f32[512]{0:T(512)}, bf16[30720,512]{1,0:T(8,128)(2,1)}) fusion(f32[30720,512]{1,0:T(8,128)} %get-tuple-element.139, bf16[512,512]{1,0:T(8,128)(2,1)S(1)} %copy-done.73, f32[30720,512]{1,0:T(8,128)} %mul.375, f32[30720]{0:T(1024)S(1)} %copy-done.24), kind=kOutput, calls=%fused_computation.84 | convolution fusion | flops 16326328320 | bytes 157935616 | tf_op jit(solution)/shard_map/dot_general | solution.py:68
  1736.4 32.8 %fusion.45 = f32[512,512]{1,0:T(8,128)} fusion(bf16[30720,512]{1,0:T(8,128)(2,1)} %get-tuple-element.150, bf16[30720,512]{1,0:T(8,128)(2,1)} %gather_fusion, pred[30720]{0:T(1024)(128)(4,1)S(1)} %copy-done.52), kind=kOutput, calls=%fused_computation.85 | convolution fusion | flops 16121856000 | bytes 63993856 | tf_op jit(solution)/shard_map/dot_general | solution.py:62
  1769.2 17.8 convolution_bitcast_fusion
  1787.0 45.7 %reshape.265 = f32[1024,30,512]{2,1,0:T(8,128)} reshape(bf16[30720,512]{1,0:T(8,128)(2,1)} %get-tuple-element.150) | data formatting | bytes 94371840 | tf_op jit(solution)/shard_map/reshape | solution.py:262
  1832.7 22.3 reduce_sum.260
  1855.0 4.4 fusion.107
  1859.4 4.8 fusion.106
  1864.3 34.0 %fusion.105 = f32[30720,512]{1,0:T(8,128)} fusion(bf16[30720,512]{1,0:T(8,128)(2,1)} %get-tuple-element.150, bf16[512,512]{1,0:T(8,128)(2,1)} %param.29), kind=kOutput, calls=%fused_computation.218 | convolution fusion | flops 16106127360 | bytes 94896128 | tf_op jit(solution)/shard_map/dot_general | solution.py:68
  1898.3 197.3 %scatter_custom_fusion.1 = f32[1024,512]{1,0:T(8,128)} fusion(s32[31744]{0:T(1024)} %bitcast.61, f32[1024,512]{1,0:T(8,128)} %fusion.106, f32[]{:T(128)} %constant.103, f32[30720,512]{1,0:T(8,128)} %fusion.105, f32[]{:T(128)} %constant.63.clone.1), kind=kCustom, calls=%fused_computation.10 | custom fusion | flops 32505856 | bytes 67109888 | tf_op jit(solution)/shard_map/scatter-add | solution.py:267
  2105.5 29.3 %convolution_add_fusion.1 = f32[30720,192]{0,1:T(8,128)} fusion(f32[30720,192]{0,1:T(8,128)} %convolution_add_fusion.3, bf16[30720,512]{1,0:T(8,128)(2,1)} %get-tuple-element.150, bf16[192,512]{1,0:T(8,128)(2,1)S(1)} %copy-done.33), kind=kOutput, calls=%fused_computation.42 | convolution fusion | flops 6045696000 | bytes 78839808 | tf_op jit(solution)/shard_map/dot_general | solution.py:68
  2134.8 27.2 %copy.161 = f32[30720,192]{1,0:T(8,128)} copy(f32[30720,192]{0,1:T(8,128)} %convolution_add_fusion.1) | data formatting | bytes 47185920 | tf_op jit(solution)/shard_map/add | solution.py:279
  2162.0 33.2 %reshape.266 = f32[1024,30,192]{2,1,0:T(8,128)} reshape(f32[30720,192]{1,0:T(8,128)} %copy.161) | data formatting | bytes 47185920 | tf_op jit(solution)/shard_map/reshape | solution.py:282
  2195.3 30.2 %copy.166 = f32[1024,30,192]{0,2,1:T(8,128)} copy(f32[1024,30,192]{2,1,0:T(8,128)} %reshape.266) | data formatting | bytes 47185920
  2225.5 41.9 %all-reduce.1 = (f32[512]{0:T(512)}, f32[512]{0:T(512)}, f32[2048]{0:T(1024)}, f32[512]{0:T(512)}, f32[192]{0:T(256)}, /*index=5*/f32[192]{0:T(256)}) all-reduce(f32[512]{0:T(512)S(1)} %copy-done.69, f32[512]{0:T(512)S(1)} %copy-done.68, f32[2048]{0:T(1024)S(1)} %copy-done.66, ...), channel_id=1, replica_groups=mesh['res'=16,'nbr'=2] {'res','nbr'}, use_global_device_ids=true, to_apply=%region_26.28 | all-reduce | flops 3968 | bytes 31744 | tf_op jit(solution)/shard_map/psum | solution.py:300
  2267.5 3.1 add_add_fusion.1
  2283.5 4.7 copy.191
  2288.2 4.6 copy.192
  (242 shorter events, 91.2 us)
Async XLA Ops:
  7.2 578.6 %copy-start = (bf16[512,2048]{1,0:T(8,128)(2,1)S(1)}, bf16[512,2048]{1,0:T(8,128)(2,1)}, u32[]{:S(2)}) copy-start(bf16[512,2048]{1,0:T(8,128)(2,1)} %param.34) | copy-start | bytes 6291460
  7.2 576.9 %reduce-scatter.2.cloned.1.call-start = ((), (), s32[]{:S(2)}) async-start(), calls=%async_computation.1 | async-start | bytes 3145728 | tf_op jit(solution)/shard_map/reduce_scatter | solution.py:187
  8.6 58.6 %copy-start.13 = (bf16[512,512]{0,1:T(8,128)(2,1)}, bf16[512,512]{0,1:T(8,128)(2,1)S(1)}, u32[]{:S(2)}) copy-start(bf16[512,512]{0,1:T(8,128)(2,1)S(1)} %copy.132) | copy-start | bytes 1572868
  8.7 58.6 %collective-permute-start = (bf16[512,512]{0,1:T(8,128)(2,1)S(1)}, bf16[512,512]{0,1:T(8,128)(2,1)}, u32[]{:S(2)}, u32[]{:S(2)}) collective-permute-start(bf16[512,512]{0,1:T(8,128)(2,1)S(1)} %copy.132), channel_id=1, source_target_pairs={{0,1},{1,0},{2,3},{3,2},{4,5},{5,4},{6,7},{7,6},{8,9},{9,8},{10,11... | collective-permute-start | bytes 1572872 | tf_op jit(solution)/shard_map/ppermute | solution.py:18
  11.7 55.6 %copy-start.11 = (s32[1024,30]{1,0:T(8,128)}, s32[1024,30]{1,0:T(8,128)S(1)}, u32[]{:S(2)}) copy-start(s32[1024,30]{1,0:T(8,128)S(1)} %copy.133) | copy-start | bytes 368644
  12.1 145.8 %copy-start.20 = (s32[30720]{0:T(1024)}, s32[30720]{0:T(1024)S(1)}, u32[]{:S(2)}) copy-start(s32[30720]{0:T(1024)S(1)} %get-tuple-element.136) | copy-start | bytes 368644
  67.3 213.8 %copy-start.50 = (pred[30720]{0:T(1024)(128)(4,1)}, pred[30720]{0:T(1024)(128)(4,1)S(1)}, u32[]{:S(2)}) copy-start(pred[30720]{0:T(1024)(128)(4,1)S(1)} %compare_and_fusion) | copy-start | bytes 92164
  281.1 34.5 %copy-start.32 = (bf16[192,512]{1,0:T(8,128)(2,1)S(1)}, bf16[192,512]{1,0:T(8,128)(2,1)}, u32[]{:S(2)}) copy-start(bf16[192,512]{1,0:T(8,128)(2,1)} %param.30) | copy-start | bytes 589828
  281.1 34.5 %copy-start.76 = (f32[512]{0:T(512)S(1)}, f32[512]{0:T(512)}, u32[]{:S(2)}) copy-start(f32[512]{0:T(512)} %param.31) | copy-start | bytes 6148
  464.7 40.9 %copy-start.35 = (f32[1024,30]{0,1:T(8,128)S(1)}, f32[1024,30]{0,1:T(8,128)}, u32[]{:S(2)}) copy-start(f32[1024,30]{0,1:T(8,128)} %copy.137) | copy-start | bytes 368644
  464.7 40.9 %copy-start.72 = (bf16[512,512]{1,0:T(8,128)(2,1)S(1)}, bf16[512,512]{1,0:T(8,128)(2,1)}, u32[]{:S(2)}) copy-start(bf16[512,512]{1,0:T(8,128)(2,1)} %param.32) | copy-start | bytes 1572868
  505.7 58.7 %copy-start.25 = (bf16[192,192]{1,0:T(8,128)(2,1)S(1)}, bf16[192,192]{1,0:T(8,128)(2,1)}, u32[]{:S(2)}) copy-start(bf16[192,192]{1,0:T(8,128)(2,1)} %param.40) | copy-start | bytes 221188
  564.3 14.7 copy-start.12
  564.3 15.2 copy-start.78
  564.3 16.4 copy-start.62
  564.3 19.0 copy-start.61
  564.3 19.8 copy-start.14
  564.3 21.4 copy-start.40
  564.3 21.4 copy-start.74
  564.4 989.0 %all-gather.2.cloned.1.call-start = ((), (), s32[]{:S(2)}) async-start(), calls=%async_computation.2 | async-start | bytes 1572864 | tf_op jit(solution)/shard_map/all_gather | solution.py:248
  585.8 14.6 copy-start.63
  600.3 118.3 %collective-permute-start.1 = (bf16[512,512]{0,1:T(8,128)(2,1)S(1)}, bf16[512,512]{0,1:T(8,128)(2,1)}, u32[]{:S(2)}, u32[]{:S(2)}) collective-permute-start(bf16[512,512]{0,1:T(8,128)(2,1)S(1)} %multiply_convert_fusion.2), channel_id=1, source_target_pairs={{0,1},{1,0},{2,3},{3,2},{4,5},{5,4},{6,7},{7,6},{8,9},{9,8},{10,11... | collective-permute-start | bytes 1572872 | tf_op jit(solution)/shard_map/ppermute | solution.py:18
  689.6 33.1 %copy-start.22 = (bf16[512,192]{0,1:T(8,128)(2,1)S(1)}, bf16[512,192]{0,1:T(8,128)(2,1)}, u32[]{:S(2)}) copy-start(bf16[512,192]{0,1:T(8,128)(2,1)} %param.38) | copy-start | bytes 589828
  689.6 35.7 %copy-start.21 = (s32[30720]{0:T(1024)S(1)}, s32[30720]{0:T(1024)}, u32[]{:S(2)}) copy-start(s32[30720]{0:T(1024)} %copy-done.20) | copy-start | bytes 368644
  893.6 28.1 %copy-start.30 = (bf16[512,192]{0,1:T(8,128)(2,1)S(1)}, bf16[512,192]{0,1:T(8,128)(2,1)}, u32[]{:S(2)}) copy-start(bf16[512,192]{0,1:T(8,128)(2,1)} %param.39) | copy-start | bytes 589828
  893.6 28.1 %copy-start.51 = (pred[30720]{0:T(1024)(128)(4,1)S(1)}, pred[30720]{0:T(1024)(128)(4,1)}, u32[]{:S(2)}) copy-start(pred[30720]{0:T(1024)(128)(4,1)} %copy-done.50) | copy-start | bytes 92164
  893.6 28.1 %copy-start.77 = (f32[192]{0:T(256)S(1)}, f32[192]{0:T(256)}, u32[]{:S(2)}) copy-start(f32[192]{0:T(256)} %param.41) | copy-start | bytes 2308
  921.7 73.8 %copy-start.36 = (bf16[192,192]{1,0:T(8,128)(2,1)S(1)}, bf16[192,192]{1,0:T(8,128)(2,1)}, u32[]{:S(2)}) copy-start(bf16[192,192]{1,0:T(8,128)(2,1)} %param.42) | copy-start | bytes 221188
  1083.7 24.0 %copy-start.26 = (bf16[192,192]{1,0:T(8,128)(2,1)S(1)}, bf16[192,192]{1,0:T(8,128)(2,1)}, u32[]{:S(2)}) copy-start(bf16[192,192]{1,0:T(8,128)(2,1)} %param.40) | copy-start | bytes 221188
  1142.8 19.9 copy-start.31
  1235.8 199.8 %copy-start.8 = (f32[1024,192]{1,0:T(8,128)}, f32[1024,192]{1,0:T(8,128)S(1)}, u32[]{:S(2)}) copy-start(f32[1024,192]{1,0:T(8,128)S(1)} %reduce_sum.255) | copy-start | bytes 2359300
  1440.1 38.3 %copy-start.10 = (f32[512,512]{0,1:T(8,128)}, f32[512,512]{0,1:T(8,128)S(1)}, u32[]{:S(2)}) copy-start(f32[512,512]{0,1:T(8,128)S(1)} %copy.169) | copy-start | bytes 3145732
  1444.0 81.1 %collective-permute-start.2 = (bf16[512,512]{0,1:T(8,128)(2,1)}, bf16[512,512]{0,1:T(8,128)(2,1)}, u32[]{:S(2)}, u32[]{:S(2)}) collective-permute-start(bf16[512,512]{0,1:T(8,128)(2,1)} %select_convert_fusion.1), channel_id=1, source_target_pairs={{0,1},{1,0},{2,3},{3,2},{4,5},{5,4},{6,7},{7,6},{8,9},{9,8},{10,11... | collective-permute-start | bytes 1572872 | tf_op jit(solution)/shard_map/ppermute | solution.py:18
  1478.4 46.6 %copy-start.47 = (f32[512]{0:T(512)S(1)}, f32[512]{0:T(512)}, u32[]{:S(2)}) copy-start(f32[512]{0:T(512)} %copy-done.46) | copy-start | bytes 6148
  1478.4 46.6 %copy-start.49 = (f32[512]{0:T(512)S(1)}, f32[512]{0:T(512)}, u32[]{:S(2)}) copy-start(f32[512]{0:T(512)} %copy-done.48) | copy-start | bytes 6148
  1478.4 46.6 %copy-start.60 = (f32[512]{0:T(512)S(1)}, f32[512]{0:T(512)}, u32[]{:S(2)}) copy-start(f32[512]{0:T(512)} %param.37) | copy-start | bytes 6148
  1502.7 27.0 %copy-start.75 = (f32[2048]{0:T(1024)S(1)}, f32[2048]{0:T(1024)}, u32[]{:S(2)}) copy-start(f32[2048]{0:T(1024)} %param.35) | copy-start | bytes 24580
  1502.7 32.8 %copy-start.4 = (f32[512,512]{0,1:T(8,128)S(1)}, f32[512,512]{0,1:T(8,128)}, u32[]{:S(2)}) copy-start(f32[512,512]{0,1:T(8,128)} %copy-done.3) | copy-start | bytes 3145732
  1502.7 32.8 %copy-start.38 = (f32[512]{0:T(512)S(1)}, f32[512]{0:T(512)}, u32[]{:S(2)}) copy-start(f32[512]{0:T(512)} %copy-done.37) | copy-start | bytes 6148
  1502.7 32.8 %copy-start.41 = (f32[512]{0:T(512)S(1)}, f32[512]{0:T(512)}, u32[]{:S(2)}) copy-start(f32[512]{0:T(512)} %param.33) | copy-start | bytes 6148
  1502.7 32.8 %copy-start.44 = (f32[512]{0:T(512)S(1)}, f32[512]{0:T(512)}, u32[]{:S(2)}) copy-start(f32[512]{0:T(512)} %copy-done.43) | copy-start | bytes 6148
  1539.8 733.4 %all-reduce.5.cloned.1.call-start = ((), (), s32[]{:S(2)}) async-start(), calls=%async_computation.3 | async-start | bytes 26214400 | tf_op jit(solution)/shard_map/psum | solution.py:300
  1578.6 63.1 %copy-start.24 = (f32[30720]{0:T(1024)S(1)}, f32[30720]{0:T(1024)}, u32[]{:S(2)}) copy-start(f32[30720]{0:T(1024)} %mul.372) | copy-start | bytes 368644
  1641.7 33.8 %copy-start.73 = (bf16[512,512]{1,0:T(8,128)(2,1)S(1)}, bf16[512,512]{1,0:T(8,128)(2,1)}, u32[]{:S(2)}) copy-start(bf16[512,512]{1,0:T(8,128)(2,1)} %param.32) | copy-start | bytes 1572868
  1675.5 60.9 %copy-start.52 = (pred[30720]{0:T(1024)(128)(4,1)S(1)}, pred[30720]{0:T(1024)(128)(4,1)}, u32[]{:S(2)}) copy-start(pred[30720]{0:T(1024)(128)(4,1)} %copy-done.50) | copy-start | bytes 92164
  1832.7 22.3 copy-start.6
  1898.3 207.2 %copy-start.33 = (bf16[192,512]{1,0:T(8,128)(2,1)S(1)}, bf16[192,512]{1,0:T(8,128)(2,1)}, u32[]{:S(2)}) copy-start(bf16[192,512]{1,0:T(8,128)(2,1)} %param.30) | copy-start | bytes 589828
  2100.2 34.6 %copy-start.9 = (f32[512,512]{0,1:T(8,128)}, f32[512,512]{0,1:T(8,128)S(1)}, u32[]{:S(2)}) copy-start(f32[512,512]{0,1:T(8,128)S(1)} %copy.171) | copy-start | bytes 3145732
  2104.1 163.3 %collective-permute-start.3 = (bf16[512,512]{0,1:T(8,128)(2,1)}, bf16[512,512]{0,1:T(8,128)(2,1)}, u32[]{:S(2)}, u32[]{:S(2)}) collective-permute-start(bf16[512,512]{0,1:T(8,128)(2,1)} %select_convert_fusion), channel_id=1, source_target_pairs={{0,1},{1,0},{2,3},{3,2},{4,5},{5,4},{6,7},{7,6},{8,9},{9,8},{10,11... | collective-permute-start | bytes 1572872 | tf_op jit(solution)/shard_map/ppermute | solution.py:18
  2195.2 30.3 %copy-start.65 = (f32[512]{0:T(512)S(1)}, f32[512]{0:T(512)}, u32[]{:S(2)}) copy-start(f32[512]{0:T(512)} %get-tuple-element.103) | copy-start | bytes 6148
  2195.2 30.3 %copy-start.66 = (f32[2048]{0:T(1024)S(1)}, f32[2048]{0:T(1024)}, u32[]{:S(2)}) copy-start(f32[2048]{0:T(1024)} %get-tuple-element.151) | copy-start | bytes 24580
  2195.2 30.3 %copy-start.67 = (f32[192]{0:T(256)S(1)}, f32[192]{0:T(256)}, u32[]{:S(2)}) copy-start(f32[192]{0:T(256)} %get-tuple-element.101) | copy-start | bytes 2308
  2195.2 30.3 %copy-start.68 = (f32[512]{0:T(512)S(1)}, f32[512]{0:T(512)}, u32[]{:S(2)}) copy-start(f32[512]{0:T(512)} %get-tuple-element.105) | copy-start | bytes 6148
  2195.2 30.3 %copy-start.69 = (f32[512]{0:T(512)S(1)}, f32[512]{0:T(512)}, u32[]{:S(2)}) copy-start(f32[512]{0:T(512)} %get-tuple-element.149) | copy-start | bytes 6148
  2195.2 30.3 %copy-start.70 = (f32[192]{0:T(256)S(1)}, f32[192]{0:T(256)}, u32[]{:S(2)}) copy-start(f32[192]{0:T(256)} %get-tuple-element.153) | copy-start | bytes 2308
  2195.2 72.3 %copy-start.5 = (f32[512,512]{0,1:T(8,128)S(1)}, f32[512,512]{0,1:T(8,128)}, u32[]{:S(2)}) copy-start(f32[512,512]{0,1:T(8,128)} %copy-done.3) | copy-start | bytes 3145732
  2195.2 72.2 %copy-start.39 = (f32[512]{0:T(512)S(1)}, f32[512]{0:T(512)}, u32[]{:S(2)}) copy-start(f32[512]{0:T(512)} %copy-done.37) | copy-start | bytes 6148
  2195.2 72.2 %copy-start.42 = (f32[512]{0:T(512)S(1)}, f32[512]{0:T(512)}, u32[]{:S(2)}) copy-start(f32[512]{0:T(512)} %param.33) | copy-start | bytes 6148
  2195.3 72.2 %copy-start.45 = (f32[512]{0:T(512)S(1)}, f32[512]{0:T(512)}, u32[]{:S(2)}) copy-start(f32[512]{0:T(512)} %copy-done.43) | copy-start | bytes 6148
  2195.3 72.2 %copy-start.56 = (f32[512]{0:T(512)S(1)}, f32[512]{0:T(512)}, u32[]{:S(2)}) copy-start(f32[512]{0:T(512)} %copy-done.55) | copy-start | bytes 6148
  2195.3 72.2 %copy-start.58 = (f32[512]{0:T(512)S(1)}, f32[512]{0:T(512)}, u32[]{:S(2)}) copy-start(f32[512]{0:T(512)} %copy-done.57) | copy-start | bytes 6148
  2273.2 19.7 copy-start.29
  2273.2 20.5 copy-start.28
  2273.2 21.2 copy-start.34
  (22 other events, 163.6 us)
Sparse Core Ops, SparseCore 0:
  564.4 12.0 reduce-scatter.1
  1539.9 11.4 all-gather.1
  1864.4 252.9 all-reduce.4
where the time goes:
time: 2320 us; the launch traced here: 2300 us
  local copies, waits for them, and re-layouts  1010 us (44%)
  matrix products  722 us (31%)
  other arithmetic  508 us (22%)
  blocking collectives  44.4 us (2%)
    dot_general x10, matrix products, product(): return jnp.dot(left_op, right_op, preferred_element_type=jnp.float32)  360 us
    dot_general x8, matrix products, times_transposed(): lax.dot_general(left_op, right_op, (((1,), (1,)), ((), ())), preferred_el...  200 us
    scatter-add x1, other arithmetic, on_device(): grad_table = jnp.zeros((SPAN, model_width), jnp.float32).at[both_ids].add...  197 us
    scatter-add x1, other arithmetic, on_device(): node_table_grad = jnp.zeros((SPAN, model_width), jnp.float32).at[both_ids...  197 us
    dot_general x8, matrix products, inner_rows(): lax.dot_general(left_op, right_op, (((0,), (0,)), ((), ())), preferred_el...  146 us
    unnamed x181, local copies, waits for them, and re-layouts  126 us
    gather x1, local copies, waits for them, and re-layouts, on_device(): near_nodes = jnp.take(node_table, local_ids, axis=0)  123 us
    gather x1, local copies, waits for them, and re-layouts, on_device(): near_state = jnp.take(state_table, local_ids, axis=0)  123 us
  transfers between devices with their start and end apart: 7, of which 0 were waited for; matrix products, arithmetic and copies ran while one was open for 28% of the time, Pallas kernels for 0%

commit v1 on v0

v1 whole, which is shorter than its diff:
```python
import functools

import jax
import jax.numpy as jnp
from jax import lax
from jax.experimental import pallas as pl
from jax.experimental.pallas import tpu as pltpu
from jax.sharding import PartitionSpec as P

SPAN = 1024
REACH = 64
TILE = 128
WINDOW = TILE + 2 * REACH
VMEM_BYTES = 60 * 2**20

epsilon = 1e-05
root_half = 0.7071067811865476
inv_root_two_pi = 0.3989422804014327
half_log2_e = 0.7213475204444817

bf16 = jnp.bfloat16
f32 = jnp.float32


def swapped(value, level):
    mask = 2**level
    devices = lax.axis_size("res") * lax.axis_size("nbr")
    pairs = [(source, source ^ mask) for source in range(devices)]
    return lax.ppermute(value, ("res", "nbr"), pairs)


def nn(left_op, right_op):
    return jnp.dot(left_op, right_op, preferred_element_type=f32)


def nt(left_op, right_op):
    return lax.dot_general(
        left_op, right_op, (((1,), (1,)), ((), ())), preferred_element_type=f32
    )


def tn(left_op, right_op):
    return lax.dot_general(
        left_op, right_op, (((0,), (0,)), ((), ())), preferred_element_type=f32
    )


def split(values):
    high = values.astype(bf16)
    return high, (values - high.astype(f32)).astype(bf16)


def gelu_and_slope(values):
    below = 0.5 + 0.5 * lax.erf(values * root_half)
    density = jnp.exp2(values * values * -half_log2_e)
    return values * below, below + values * density * inv_root_two_pi


def selector(rows, ids):
    places = lax.broadcasted_iota(jnp.int32, (rows, ids.shape[1]), 0)
    return (places == ids).astype(bf16)


def near_selector(ids, tile, local_first):
    first = local_first + tile * TILE
    return selector(WINDOW, ids[:, tile * TILE : (tile + 1) * TILE] - (first - REACH))


def window_of(tile, local_first):
    return pl.ds(pl.multiple_of(local_first + tile * TILE, TILE), WINDOW)


def repeat_lanes(column, width):
    return jnp.concatenate([column] * (width // column.shape[1]), axis=1)


def padded_rows(table):
    zeros = jnp.zeros((REACH, table.shape[1]), table.dtype)
    return jnp.concatenate([zeros, table, zeros], axis=0)


def whole(shape):
    return pl.BlockSpec(shape, lambda *_: (0,) * len(shape))


def params():
    return pltpu.CompilerParams(vmem_limit_bytes=VMEM_BYTES)


smem = pl.BlockSpec(memory_space=pltpu.SMEM)


def message_forward_kernel(
    static_first,
    meta,
    own,
    other,
    ids,
    edges,
    receiver,
    neighbour,
    edge_weight_t,
    bias,
    out_weight,
    table,
    slope,
    sums,
    packed,
    far_table,
    near_table,
    base,
    counts,
):
    step = pl.program_id(0)
    rows = base.shape[1]
    half = own.shape[0]
    local_first = pl.multiple_of(meta[1], TILE) if static_first is None else static_first

    @pl.when(step == 0)
    def _():
        high = meta[0]
        table[pl.ds(pl.multiple_of(high * half, half), half), :] = own[...]
        table[pl.ds(pl.multiple_of((1 - high) * half, half), half), :] = other[...]
        neighbour_t = neighbour[...].T
        nodes = table[...]
        far_table[...] = nt(neighbour_t, nodes).astype(bf16)
        near_table[...] = nt(neighbour_t, padded_rows(nodes)).astype(bf16)
        block = table[pl.ds(local_first, rows), :]
        base[...] = nt(receiver[...].T, block) + repeat_lanes(bias[...], rows)
        sums[...] = jnp.zeros_like(sums)
        counts[...] = jnp.zeros_like(counts)

    positions = lax.broadcasted_iota(jnp.int32, (1, rows), 1) + local_first
    for side in range(2):
        near = ids[pl.ds(2 * step + side, 1), :] - meta[2]
        valid = ((near < meta[3]) & (positions < meta[3])).astype(f32)
        counts[...] += valid
        if side == 0:
            picked = jnp.concatenate(
                [
                    nn(near_table[:, window_of(tile, local_first)], near_selector(near, tile, local_first))
                    for tile in range(rows // TILE)
                ],
                axis=1,
            )
        else:
            picked = nn(far_table[...], selector(SPAN, near))
        value = picked + nn(edge_weight_t[...], edges[side]) + base[...]
        act, grad = gelu_and_slope(value)
        sums[...] += act * valid
        slope[side] = (grad * valid).astype(bf16)

    @pl.when(step == pl.num_programs(0) - 1)
    def _():
        high_part, low_part = split(sums[...])
        message = tn(high_part, out_weight[...]) + tn(low_part, out_weight[...])
        width = message.shape[1]
        packed[:, :width] = message.astype(bf16)
        packed[:, width:] = jnp.broadcast_to(counts[...], (128, rows)).T.astype(bf16)


def message_forward(meta, own, other, ids, edges, receiver, neighbour, edge_weight, bias, out_weight, local_first):
    pairs = edges.shape[0] // 2
    width, rows = edges.shape[1:]
    model = own.shape[1]
    return pl.pallas_call(
        functools.partial(message_forward_kernel, local_first),
        name="message_forward",
        grid=(pairs,),
        in_specs=[
            smem,
            whole(own.shape),
            whole(other.shape),
            whole(ids.shape),
            pl.BlockSpec((2, width, rows), lambda i: (i, 0, 0)),
            whole(receiver.shape),
            whole(neighbour.shape),
            whole((model, width)),
            whole((model, 128)),
            whole(out_weight.shape),
        ],
        out_specs=[
            whole((SPAN, model)),
            pl.BlockSpec((2, model, rows), lambda i: (i, 0, 0)),
            whole((model, rows)),
            whole((rows, model + 128)),
        ],
        out_shape=[
            jax.ShapeDtypeStruct((SPAN, model), bf16),
            jax.ShapeDtypeStruct((2 * pairs, model, rows), bf16),
            jax.ShapeDtypeStruct((model, rows), f32),
            jax.ShapeDtypeStruct((rows, model + 128), bf16),
        ],
        scratch_shapes=[
            pltpu.VMEM((model, SPAN), bf16),
            pltpu.VMEM((model, SPAN + 2 * REACH), bf16),
            pltpu.VMEM((model, rows), f32),
            pltpu.VMEM((1, rows), f32),
        ],
        compiler_params=params(),
    )(
        meta,
        own,
        other,
        ids,
        edges,
        receiver,
        neighbour,
        edge_weight.T,
        jnp.broadcast_to(bias[:, None], (model, 128)),
        out_weight,
    )


def normed(values):
    mean_val = jnp.mean(values, -1, keepdims=True)
    centered = values - mean_val
    inv_std = lax.rsqrt(jnp.mean(centered * centered, -1, keepdims=True) + epsilon)
    return centered * inv_std, inv_std


def node_forward_kernel(
    nodes, mine, theirs, gain_one, ffn_in, ffn_bias, ffn_out, gain_two, state, ffn_input, act, slope, first, second, stats
):
    width = nodes.shape[1]
    total = mine[...].astype(f32) + theirs[...].astype(f32)
    divisor = jnp.maximum(total[:, width:], 1.0)
    ratio = 1.0 / divisor
    first_sum = nodes[...].astype(f32) + total[:, :width] * repeat_lanes(ratio, width)
    first_unit, first_inv = normed(first_sum)
    first[...] = first_unit
    first_norm = first_unit * gain_one[...]
    low = first_norm.astype(bf16)
    ffn_input[...] = low
    hidden, grad = gelu_and_slope(nn(low, ffn_in[...]) + ffn_bias[...])
    hidden = hidden.astype(bf16)
    act[...] = hidden
    slope[...] = grad.astype(bf16)
    second_unit, second_inv = normed(first_norm + nn(hidden, ffn_out[...]))
    second[...] = second_unit
    state[...] = (second_unit * gain_two[...]).astype(bf16)
    stats[:, :128] = ratio
    stats[:, 128:256] = jnp.broadcast_to(first_inv, ratio.shape)
    stats[:, 256:] = jnp.broadcast_to(second_inv, ratio.shape)


def node_forward(nodes, mine, theirs, gain_one, ffn_in, ffn_bias, ffn_out, gain_two):
    rows, model = nodes.shape
    hidden = ffn_in.shape[1]
    chunk = min(rows, 256)

    def by_rows(width):
        return pl.BlockSpec((chunk, width), lambda i: (i, 0))

    return pl.pallas_call(
        node_forward_kernel,
        name="node_forward",
        grid=(rows // chunk,),
        in_specs=[
            by_rows(model),
            by_rows(model + 128),
            by_rows(model + 128),
            whole((1, model)),
            whole(ffn_in.shape),
            whole((1, hidden)),
            whole(ffn_out.shape),
            whole((1, model)),
        ],
        out_specs=[
            by_rows(model),
            by_rows(model),
            by_rows(hidden),
            by_rows(hidden),
            by_rows(model),
            by_rows(model),
            by_rows(384),
        ],
        out_shape=[
            jax.ShapeDtypeStruct((rows, model), bf16),
            jax.ShapeDtypeStruct((rows, model), bf16),
            jax.ShapeDtypeStruct((rows, hidden), bf16),
            jax.ShapeDtypeStruct((rows, hidden), bf16),
            jax.ShapeDtypeStruct((rows, model), f32),
            jax.ShapeDtypeStruct((rows, model), f32),
            jax.ShapeDtypeStruct((rows, 384), f32),
        ],
        compiler_params=params(),
    )(nodes, mine, theirs, gain_one[None], ffn_in, ffn_bias[None], ffn_out, gain_two[None])


def edge_kernel(
    static_first,
    meta,
    states,
    ids,
    edges,
    cots,
    residue_t,
    neighbour_t,
    edge_weight,
    edge_weight_t,
    bias,
    out_weight,
    out_weight_t,
    gain,
    new_edges,
    partial,
    back_table,
    grads,
    vectors,
    far_table,
    near_table,
    base,
    far_sum,
    near_sum,
    own_sum,
    gain_sum,
    grad_edge,
    grad_out,
):
    step = pl.program_id(0)
    width, rows = base.shape
    local_first = pl.multiple_of(meta[1], TILE) if static_first is None else static_first

    @pl.when(step == 0)
    def _():
        nodes = states[...]
        far_table[...] = nt(neighbour_t[...], nodes).astype(bf16)
        near_table[...] = nt(neighbour_t[...], padded_rows(nodes)).astype(bf16)
        block = states[pl.ds(local_first, rows), :]
        base[...] = nt(residue_t[...], block) + repeat_lanes(bias[...], rows)
        for total in (far_sum, near_sum, own_sum, gain_sum, grad_edge, grad_out):
            total[...] = jnp.zeros_like(total)

    gains = repeat_lanes(gain[...], rows)
    for side in range(2):
        near = ids[pl.ds(2 * step + side, 1), :] - meta[2]
        if side == 0:
            chosen = [near_selector(near, tile, local_first) for tile in range(rows // TILE)]
            picked = jnp.concatenate(
                [
                    nn(near_table[:, window_of(tile, local_first)], pick)
                    for tile, pick in enumerate(chosen)
                ],
                axis=1,
            )
        else:
            chosen = selector(SPAN, near)
            picked = nn(far_table[...], chosen)
        edge = edges[side]
        value = picked + nn(edge_weight_t[...], edge) + base[...]
        act, slope = gelu_and_slope(value)
        act = act.astype(bf16)
        third = edge.astype(f32) + nn(out_weight_t[...], act)
        centered = third - jnp.mean(third, 0, keepdims=True)
        inv_std = lax.rsqrt(jnp.mean(centered * centered, 0, keepdims=True) + epsilon)
        unit = centered * inv_std
        new_edges[side] = (unit * gains).astype(bf16)
        cot = cots[side].astype(f32)
        gain_sum[...] += cot * unit
        scaled = cot * gains
        grad_third = inv_std * (
            scaled
            - jnp.mean(scaled, 0, keepdims=True)
            - unit * jnp.mean(scaled * unit, 0, keepdims=True)
        )
        branch = grad_third.astype(bf16)
        grad_out[...] += nt(act, branch)
        grad_value = (nn(out_weight[...], branch) * slope).astype(bf16)
        own_sum[...] += grad_value.astype(f32)
        grad_edge[...] += nt(edge, grad_value)
        partial[side] = grad_third + nn(edge_weight[...], grad_value)
        if side == 0:
            for tile, pick in enumerate(chosen):
                near_sum[:, window_of(tile, local_first)] += nt(
                    grad_value[:, tile * TILE : (tile + 1) * TILE], pick
                )
        else:
            far_sum[...] += nt(grad_value, chosen)

    @pl.when(step == pl.num_programs(0) - 1)
    def _():
        shifted = pltpu.roll(near_sum[...], SPAN + REACH, 1)
        table_sum = far_sum[...] + shifted[:, :SPAN]
        table_high, table_low = split(table_sum)
        own_high, own_low = split(own_sum[...])
        back = tn(table_high, neighbour_t[...]) + tn(table_low, neighbour_t[...])
        own_back = tn(own_high, residue_t[...]) + tn(own_low, residue_t[...])
        if rows == SPAN:
            back_table[...] = (back + own_back).astype(bf16)
        else:
            near_sum_rows = pl.ds(pl.multiple_of(local_first, TILE), rows)
            back_table[...] = back.astype(bf16)
            back_table[near_sum_rows, :] = (
                back_table[near_sum_rows, :].astype(f32) + own_back
            ).astype(bf16)
        block = states[pl.ds(local_first, rows), :]
        grads[:width, :] = nn(own_high, block) + nn(own_low, block)
        grads[width : 2 * width, :] = nn(table_high, states[...]) + nn(table_low, states[...])
        grads[2 * width :, :width] = grad_edge[...]
        grads[2 * width :, 256 : 256 + width] = grad_out[...]
        vectors[:, :1] = jnp.sum(own_sum[...], axis=1, keepdims=True)
        vectors[:, 1:2] = jnp.sum(gain_sum[...], axis=1, keepdims=True)


def edge_layer(
    meta, states, ids, edges, cots, residue, neighbour, edge_weight, bias, out_weight, gain, local_first
):
    pairs = edges.shape[0] // 2
    width, rows = edges.shape[1:]
    model = states.shape[1]
    by_pair = pl.BlockSpec((2, width, rows), lambda i: (i, 0, 0))
    square = whole((width, width))
    return pl.pallas_call(
        functools.partial(edge_kernel, local_first),
        name="edge_layer",
        grid=(pairs,),
        in_specs=[
            smem,
            whole(states.shape),
            whole(ids.shape),
            by_pair,
            by_pair,
            whole((width, model)),
            whole((width, model)),
            square,
            square,
            whole((width, 128)),
            square,
            square,
            whole((width, 128)),
        ],
        out_specs=[
            by_pair,
            by_pair,
            whole((SPAN, model)),
            whole((3 * width, model)),
            whole((width, 128)),
        ],
        out_shape=[
            jax.ShapeDtypeStruct(edges.shape, bf16),
            jax.ShapeDtypeStruct(edges.shape, f32),
            jax.ShapeDtypeStruct((SPAN, model), bf16),
            jax.ShapeDtypeStruct((3 * width, model), f32),
            jax.ShapeDtypeStruct((width, 128), f32),
        ],
        scratch_shapes=[
            pltpu.VMEM((width, SPAN), bf16),
            pltpu.VMEM((width, SPAN + 2 * REACH), bf16),
            pltpu.VMEM((width, rows), f32),
            pltpu.VMEM((width, SPAN), f32),
            pltpu.VMEM((width, SPAN + 2 * REACH), f32),
            pltpu.VMEM((width, rows), f32),
            pltpu.VMEM((width, rows), f32),
            pltpu.VMEM((width, width), f32),
            pltpu.VMEM((width, width), f32),
        ],
        compiler_params=params(),
    )(
        meta,
        states,
        ids,
        edges,
        cots,
        residue.T,
        neighbour.T,
        edge_weight,
        edge_weight.T,
        jnp.broadcast_to(bias[:, None], (width, 128)),
        out_weight,
        out_weight.T,
        jnp.broadcast_to(gain[:, None], (width, 128)),
    )


def norm_back(unit, inv_std, gain, grad_out):
    grad_gain = jnp.sum(grad_out * unit, axis=0, keepdims=True)
    scaled = grad_out * gain
    grad_in = inv_std * (
        scaled
        - jnp.mean(scaled, -1, keepdims=True)
        - unit * jnp.mean(scaled * unit, -1, keepdims=True)
    )
    return grad_in, grad_gain


def node_backward_kernel(
    meta,
    own_cot,
    other_cot,
    mine,
    theirs,
    first,
    second,
    stats,
    ffn_input,
    act,
    slope,
    gain_one,
    ffn_in,
    ffn_out,
    gain_two,
    grad_first_ref,
    message_cot,
    weights,
    vectors,
    sum_out,
    sum_in,
):
    step = pl.program_id(0)
    chunk, model = first.shape
    hidden = act.shape[1]
    core = meta[4]
    half = own_cot.shape[0]

    @pl.when(step == 0)
    def _():
        vectors[...] = jnp.zeros_like(vectors)
        sum_out[...] = jnp.zeros_like(sum_out)
        sum_in[...] = jnp.zeros_like(sum_in)

    row = step * chunk
    inside = pl.ds(pl.multiple_of(lax.rem(row, half), chunk), chunk)
    cot = jnp.where(row // half == core, own_cot[inside, :], other_cot[inside, :])
    total = cot.astype(f32) + (mine[...].astype(f32) + theirs[...].astype(f32))
    second_inv = stats[:, 256:257]
    first_inv = stats[:, 128:129]
    grad_second, gain_two_part = norm_back(second[...], second_inv, gain_two[...], total)
    top = grad_second.astype(bf16)
    grad_hidden = (nt(top, ffn_out[...]) * slope[...].astype(f32)).astype(bf16)
    out_columns = pl.ds(pl.multiple_of(core * (hidden // 2), 128), hidden // 2)
    in_columns = pl.ds(pl.multiple_of(core * (model // 2), 128), model // 2)
    sum_out[...] += tn(act[:, out_columns], top)
    sum_in[...] += tn(ffn_input[:, in_columns], grad_hidden)
    bias_part = jnp.sum(grad_hidden.astype(f32), axis=0, keepdims=True)
    grad_norm = grad_second + nt(grad_hidden, ffn_in[...])
    grad_first, gain_one_part = norm_back(first[...], first_inv, gain_one[...], grad_norm)
    grad_first_ref[...] = grad_first
    message_cot[...] = (grad_first * stats[:, :1]).astype(bf16)
    vectors[0:1, :] += gain_one_part
    vectors[1:2, :] += gain_two_part
    for part in range(hidden // model):
        vectors[2 + part : 3 + part, :] += bias_part[:, part * model : (part + 1) * model]

    @pl.when(step == pl.num_programs(0) - 1)
    def _():
        weights[: hidden // 2, :] = sum_out[...].astype(bf16)
        for part in range(hidden // model):
            start = hidden // 2 + part * (model // 2)
            weights[start : start + model // 2, :] = sum_in[
                :, part * model : (part + 1) * model
            ].astype(bf16)


def node_backward(
    meta, own_cot, other_cot, mine, theirs, first, second, stats, ffn_input, act, slope, gain_one, ffn_in, ffn_out, gain_two
):
    rows, model = first.shape
    hidden = act.shape[1]
    chunk = min(own_cot.shape[0], 256)

    def by_rows(width):
        return pl.BlockSpec((chunk, width), lambda i: (i, 0))

    return pl.pallas_call(
        node_backward_kernel,
        name="node_backward",
        grid=(rows // chunk,),
        in_specs=[
            smem,
            whole(own_cot.shape),
            whole(other_cot.shape),
            by_rows(model),
            by_rows(model),
            by_rows(model),
            by_rows(model),
            by_rows(384),
            by_rows(model),
            by_rows(hidden),
            by_rows(hidden),
            whole((1, model)),
            whole(ffn_in.shape),
            whole(ffn_out.shape),
            whole((1, model)),
        ],
        out_specs=[by_rows(model), by_rows(model), whole((hidden, model)), whole((8, model))],
        out_shape=[
            jax.ShapeDtypeStruct((rows, model), f32),
            jax.ShapeDtypeStruct((rows, model), bf16),
            jax.ShapeDtypeStruct((hidden, model), bf16),
            jax.ShapeDtypeStruct((8, model), f32),
        ],
        scratch_shapes=[
            pltpu.VMEM((hidden // 2, model), f32),
            pltpu.VMEM((model // 2, hidden), f32),
        ],
        compiler_params=params(),
    )(
        meta,
        own_cot,
        other_cot,
        mine,
        theirs,
        first,
        second,
        stats,
        ffn_input,
        act,
        slope,
        gain_one[None],
        ffn_in,
        ffn_out,
        gain_two[None],
    )


def message_backward_kernel(
    static_first,
    meta,
    table,
    cot,
    sums,
    ids,
    edges,
    slope,
    receiver,
    neighbour,
    out_weight,
    keep,
    send,
    grad_self,
    grad_near,
    grad_edge,
    grad_out,
    grad_bias,
    spread,
    far_sum,
    near_sum,
    own_sum,
):
    step = pl.program_id(0)
    rows = spread.shape[1]
    half = keep.shape[0]
    local_first = pl.multiple_of(meta[1], TILE) if static_first is None else static_first

    @pl.when(step == 0)
    def _():
        spread[...] = nt(out_weight[...], cot[...])
        grad_out[...] = nn(sums[...].astype(bf16), cot[...])
        grad_edge[...] = jnp.zeros_like(grad_edge)
        for total in (far_sum, near_sum, own_sum):
            total[...] = jnp.zeros_like(total)

    for side in range(2):
        near = ids[pl.ds(2 * step + side, 1), :] - meta[2]
        grad_value = (spread[...] * slope[side].astype(f32)).astype(bf16)
        own_sum[...] += grad_value.astype(f32)
        grad_edge[...] += nt(edges[side], grad_value)
        if side == 0:
            for tile in range(rows // TILE):
                near_sum[:, window_of(tile, local_first)] += nt(
                    grad_value[:, tile * TILE : (tile + 1) * TILE],
                    near_selector(near, tile, local_first),
                )
        else:
            far_sum[...] += nt(grad_value, selector(SPAN, near))

    @pl.when(step == pl.num_programs(0) - 1)
    def _():
        shifted = pltpu.roll(near_sum[...], SPAN + REACH, 1)
        table_high, table_low = split(far_sum[...] + shifted[:, :SPAN])
        own_high, own_low = split(own_sum[...])
        nodes = table[...]
        block = table[pl.ds(local_first, rows), :]
        grad_near[...] = (nn(table_high, nodes) + nn(table_low, nodes)).T
        grad_self[...] = (nn(own_high, block) + nn(own_low, block)).T
        grad_bias[...] = jnp.sum(own_sum[...].T, axis=0, keepdims=True)
        back = nn(neighbour[...], table_high) + nn(neighbour[...], table_low)
        own_back = nn(receiver[...], own_high) + nn(receiver[...], own_low)
        if rows == SPAN:
            far_sum[...] = back + own_back
        else:
            far_sum[...] = back
            far_sum[:, pl.ds(pl.multiple_of(local_first, TILE), rows)] += own_back
        high = meta[0]
        keep[...] = far_sum[:, pl.ds(pl.multiple_of(high * half, half), half)].T
        send[...] = far_sum[:, pl.ds(pl.multiple_of((1 - high) * half, half), half)].T.astype(bf16)


def message_backward(meta, table, cot, sums, ids, edges, slope, receiver, neighbour, out_weight, local_first):
    pairs = edges.shape[0] // 2
    width, rows = edges.shape[1:]
    model = table.shape[1]
    square = whole((model, model))
    return pl.pallas_call(
        functools.partial(message_backward_kernel, local_first),
        name="message_backward",
        grid=(pairs,),
        in_specs=[
            smem,
            whole(table.shape),
            whole(cot.shape),
            whole(sums.shape),
            whole(ids.shape),
            pl.BlockSpec((2, width, rows), lambda i: (i, 0, 0)),
            pl.BlockSpec((2, model, rows), lambda i: (i, 0, 0)),
            square,
            square,
            square,
        ],
        out_specs=[
            whole((SPAN // 2, model)),
            whole((SPAN // 2, model)),
            square,
            square,
            whole((width, model)),
            square,
            whole((1, model)),
            whole((model, rows)),
        ],
        out_shape=[
            jax.ShapeDtypeStruct((SPAN // 2, model), f32),
            jax.ShapeDtypeStruct((SPAN // 2, model), bf16),
            jax.ShapeDtypeStruct((model, model), f32),
            jax.ShapeDtypeStruct((model, model), f32),
            jax.ShapeDtypeStruct((width, model), f32),
            jax.ShapeDtypeStruct((model, model), f32),
            jax.ShapeDtypeStruct((1, model), f32),
            jax.ShapeDtypeStruct((model, rows), f32),
        ],
        scratch_shapes=[
            pltpu.VMEM((model, SPAN), f32),
            pltpu.VMEM((model, SPAN + 2 * REACH), f32),
            pltpu.VMEM((model, rows), f32),
        ],
        compiler_params=params(),
    )(meta, table, cot, sums, ids, edges, slope, receiver, neighbour, out_weight)


def edge_gradient_kernel(partial, slope, spread, edge_weight, out):
    for side in range(partial.shape[0]):
        grad_value = (spread[...] * slope[side].astype(f32)).astype(bf16)
        out[side] = partial[side] + nn(edge_weight[...], grad_value)


def edge_gradient(partial, slope, spread, edge_weight):
    columns, width, rows = partial.shape
    model = spread.shape[0]
    by_pair = pl.BlockSpec((2, width, rows), lambda i: (i, 0, 0))
    return pl.pallas_call(
        edge_gradient_kernel,
        name="edge_gradient",
        grid=(columns // 2,),
        in_specs=[
            by_pair,
            pl.BlockSpec((2, model, rows), lambda i: (i, 0, 0)),
            whole(spread.shape),
            whole(edge_weight.shape),
        ],
        out_specs=by_pair,
        out_shape=jax.ShapeDtypeStruct(partial.shape, f32),
        compiler_params=params(),
    )(partial, slope, spread, edge_weight)


def joined(table, other, high_side):
    return jnp.where(
        high_side, jnp.concatenate([other, table], axis=0), jnp.concatenate([table, other], axis=0)
    )


def halves(table, high_side):
    half = table.shape[0] // 2
    lower, upper = (table[:half], table[half:])
    return (jnp.where(high_side, upper, lower), jnp.where(high_side, lower, upper))


def sum_blocks(table, device, level):
    keep, send = halves(table, device >> level & 1 == 1)
    return keep + swapped(send.astype(bf16), level).astype(keep.dtype)


def on_device(
    nodes,
    edges,
    neighbours,
    lengths,
    message_receiver_weight,
    message_neighbour_weight,
    message_edge_weight,
    message_hidden_bias,
    message_output_weight,
    gain_one,
    ffn_in,
    ffn_bias,
    ffn_out,
    gain_two,
    edge_update_residue_weight,
    edge_update_neighbour_weight,
    edge_update_edge_weight,
    edge_update_bias,
    edge_out,
    gain_three,
    node_cot,
    edge_cot,
):
    rows, half_k, edge_width = edges.shape
    own_rows, model = nodes.shape
    hidden = ffn_in.shape[1]
    levels = (SPAN // own_rows).bit_length() - 1
    core = lax.axis_index("nbr")
    device = lax.axis_index("res") * lax.axis_size("nbr") + core
    first_row = lax.axis_index("res") * rows
    bucket = first_row // SPAN
    group_start = bucket * SPAN
    local_first = 0 if rows == SPAN else None
    length = jnp.sum(jnp.where(jnp.arange(lengths.shape[0]) == bucket, lengths, 0))
    top = device >> (levels - 1) & 1
    meta = jnp.stack(
        [top, first_row - group_start, group_start, length, core, 0, 0, 0]
    ).astype(jnp.int32)

    ids = neighbours.T
    edges_t = edges.transpose(1, 2, 0)
    cot_t = edge_cot.transpose(1, 2, 0)

    table = nodes
    for level in range(levels - 1):
        table = joined(table, swapped(table, level), device >> level & 1 == 1)
    other_table = swapped(table, levels - 1)
    other_cot = swapped(node_cot, 0)

    node_table, slope, sums, packed = message_forward(
        meta,
        table,
        other_table,
        ids,
        edges_t,
        message_receiver_weight,
        message_neighbour_weight,
        message_edge_weight,
        message_hidden_bias,
        message_output_weight,
        local_first,
    )
    block = node_table
    if rows < SPAN:
        block = lax.dynamic_slice_in_dim(node_table, first_row - group_start, rows, 0)
    state, ffn_input, act, ffn_slope, first, second, stats = node_forward(
        block, packed, swapped(packed, 0), gain_one, ffn_in, ffn_bias, ffn_out, gain_two
    )
    states = state
    for level in range(1, levels):
        states = joined(states, swapped(states, level), device >> level & 1 == 1)
    new_edges, partial, back, edge_grads, edge_vectors = edge_layer(
        meta,
        states,
        ids,
        edges_t,
        cot_t,
        edge_update_residue_weight,
        edge_update_neighbour_weight,
        edge_update_edge_weight,
        edge_update_bias,
        edge_out,
        gain_three,
        local_first,
    )
    for level in reversed(range(1, levels)):
        back = sum_blocks(back, device, level)
    grad_first, message_cot, ffn_grads, node_vectors = node_backward(
        meta,
        node_cot,
        other_cot,
        back,
        swapped(back, 0),
        first,
        second,
        stats,
        ffn_input,
        act,
        ffn_slope,
        gain_one,
        ffn_in,
        ffn_out,
        gain_two,
    )
    (
        keep,
        send,
        grad_msg_self,
        grad_msg_nbr,
        grad_msg_edge,
        grad_msg_out,
        grad_msg_bias,
        spread,
    ) = message_backward(
        meta,
        node_table,
        message_cot,
        sums,
        ids,
        edges_t,
        slope,
        message_receiver_weight,
        message_neighbour_weight,
        message_output_weight,
        local_first,
    )
    edge_grad = edge_gradient(partial, slope, spread, message_edge_weight)
    kept = keep + swapped(send, levels - 1).astype(f32)
    for level in reversed(range(levels - 1)):
        kept = sum_blocks(kept, device, level)
    own_first = lax.dynamic_slice_in_dim(grad_first, core * own_rows, own_rows, 0)
    node_grad = own_first + kept
    node_out = lax.dynamic_slice_in_dim(state, core * own_rows, own_rows, 0)

    halved = node_vectors * 0.5
    small = lax.psum(
        (
            grad_msg_self,
            grad_msg_nbr,
            grad_msg_edge,
            grad_msg_bias,
            grad_msg_out,
            edge_grads,
            edge_vectors[:, :2],
            halved,
        ),
        ("res", "nbr"),
    )
    grad_msg_self, grad_msg_nbr, grad_msg_edge, grad_msg_bias, grad_msg_out, edge_grads, edge_vectors, vectors = small
    ffn_grads = lax.psum(ffn_grads.astype(f32), "res")
    both = lax.all_gather(ffn_grads, "nbr", axis=0)
    grad_ffn_out = jnp.concatenate([both[0, : hidden // 2], both[1, : hidden // 2]], axis=0)
    parts = [
        both[:, hidden // 2 + part * (model // 2) : hidden // 2 + (part + 1) * (model // 2)].reshape(model, model)
        for part in range(hidden // model)
    ]
    grad_ffn_in = jnp.concatenate(parts, axis=1)
    return (
        node_out,
        new_edges.transpose(2, 0, 1),
        node_grad,
        edge_grad.transpose(2, 0, 1),
        grad_msg_self,
        grad_msg_nbr,
        grad_msg_edge,
        grad_msg_bias[0],
        grad_msg_out,
        vectors[0],
        grad_ffn_in,
        vectors[2 : 2 + hidden // model].reshape(-1),
        grad_ffn_out,
        vectors[1],
        edge_grads[:edge_width].T,
        edge_grads[edge_width : 2 * edge_width].T,
        edge_grads[2 * edge_width :, :edge_width],
        edge_vectors[:, 0],
        edge_grads[2 * edge_width :, 256 : 256 + edge_width],
        edge_vectors[:, 1],
    )


def solution(mesh):
    rows = P(("res", "nbr"), None)
    pairs = P("res", "nbr", None)
    placed = (rows, pairs, P("res", "nbr")) + (P(),) * 17 + (rows, pairs)
    return jax.shard_map(
        on_device,
        mesh=mesh,
        in_specs=placed,
        out_specs=(rows, pairs, rows, pairs) + (P(),) * 16,
        check_vma=False,
    )
```

time: 2320 us -> 574 us (0.25)
  local copies, waits for them, and re-layouts: 1010 us -> 24.7 us
  matrix products: 722 us -> 0 us
  other arithmetic: 508 us -> 11.7 us
  Pallas kernels: 0 us -> 268 us
  waiting for transfers between devices: 0.06 us -> 212 us
    dot_general x30 -> x0, matrix products: 722 us -> none  [the longest x10 360 us: product(): return jnp.dot(left_op, right_op, preferred_element_type=jnp.float32)]
    scatter-add x2 -> x0, other arithmetic: 395 us -> none  [the longest x1 197 us: on_device(): grad_table = jnp.zeros((SPAN, model_width), jnp.float32).at[both_ids].add...]
    pallas_call x0 -> x6, Pallas kernels: none -> 268 us  [the longest x1 83.2 us: edge_layer(): pl.pallas_call(functools.partial(edge_kernel, local_first), name='edge_la...]
    gather x2 -> x0, local copies, waits for them, and re-layouts: 246 us -> none  [the longest x1 123 us: on_device(): near_nodes = jnp.take(node_table, local_ids, axis=0)]
    add x6 -> x0, local copies, waits for them, and re-layouts: 185 us -> none  [the longest x2 84.5 us: on_device(): product(block_nodes, message_receiver_weight)[:, None, :]]
    reshape x7 -> x0, local copies, waits for them, and re-layouts: 179 us -> none  [the longest x1 45.7 us: on_device(): grad_msg_wide.reshape(block_len, half_k, model_width)]
    convert_element_type x6 -> x0, local copies, waits for them, and re-layouts: 128 us -> none  [the longest x3 87.1 us: on_device(): edge_cot.reshape(-1, edge_width).astype(jnp.float32)]
    psum x0 -> x1, waiting for transfers between devices: none -> 115 us  [on_device(): ffn_grads = lax.psum(ffn_grads.astype(f32), 'res')]
  transfers between devices with their start and end apart: 7 -> 8, of which waited for: 0 -> 5; matrix products, arithmetic and copies ran while one was open for 28% -> 2% of each run, Pallas kernels for 0% -> 15%
where the time goes in v1:
time: 574 us
  Pallas kernels  268 us (47%)
  waiting for transfers between devices  212 us (37%)
  blocking collectives  41.1 us (7%)
  local copies, waits for them, and re-layouts  24.7 us (4%)
  between operations  13.9 us (2%)
  other arithmetic  11.7 us (2%)
    psum x1, waiting for transfers between devices, on_device(): ffn_grads = lax.psum(ffn_grads.astype(f32), 'res')  115 us
    pallas_call x1, Pallas kernels, edge_layer(): pl.pallas_call(functools.partial(edge_kernel, local_first), name='edge_la...  83.2 us
    psum x1, waiting for transfers between devices, on_device(): lax.psum((grad_msg_self, grad_msg_nbr, grad_msg_edge, grad_msg_bias, grad...  76.1 us
    pallas_call x1, Pallas kernels, message_forward(): pl.pallas_call(functools.partial(message_forward_kernel, local_first), na...  68.6 us
    pallas_call x1, Pallas kernels, message_backward(): pl.pallas_call(functools.partial(message_backward_kernel, local_first), n...  55.3 us
    psum x1, blocking collectives, on_device(): lax.psum((grad_msg_self, grad_msg_nbr, grad_msg_edge, grad_msg_bias, grad...  41.1 us
    pallas_call x1, Pallas kernels, edge_gradient(): pl.pallas_call(edge_gradient_kernel, name='edge_gradient', grid=(columns...  32.8 us
    all_gather x1, waiting for transfers between devices, on_device(): both = lax.all_gather(ffn_grads, 'nbr', axis=0)  16.3 us
  transfers between devices with their start and end apart: 8, of which 5 were waited for; matrix products, arithmetic and copies ran while one was open for 2% of the time, Pallas kernels for 15%

profile of v1, /device:TPU:0, one launch (start us, length us, event | category | flops | bytes accessed | tf_op | source)
XLA Modules:
  0.0 573.6 jit_solution(12750157022800855314)
XLA Ops:
  7.2 0.0 all-reduce.5.cloned.1.call-start
  7.2 0.5 collective-permute-start
  7.8 1.8 copy.48
  9.5 1.3 fusion
  10.8 1.2 stack.23.meta
  12.1 0.0 collective-permute-done.other
  12.1 1.5 broadcast_in_dim.17.bias
  13.6 0.0 copy-done.8
  13.6 68.6 %message_forward.1 = (bf16[1024,512]{1,0:T(8,128)(2,1)}, bf16[30,512,1024]{2,1,0:T(8,128)(2,1)}, f32[512,1024]{1,0:T(8,128)}, bf16[1024,640]{1,0:T(8,128)(2,1)}) custom-call(s32[8]{0:T(128)} %stack.23.meta, bf16[512,512]{1,0:T(8,128)(2,1)} %own.1, bf16[512,512]{1,0:T(8,128)(2,1)} %copy-done.8, s32[30,1024]{1,0:T(8,128)} %bitcast.51, ...), custom_call_target="tpu_custom_call" | custom-call | tf_op jit(solution)/shard_map/message_forward/pallas_call | solution.py:166
  82.2 0.0 copy-start.18
  82.2 0.1 collective-permute-start.1
  82.3 0.0 copy-done.11
  82.3 0.7 copy.49
  83.1 0.0 copy-done.12
  83.1 0.7 copy.50
  83.8 1.7 collective-permute-done.1.theirs
  85.5 1.1 copy-done.1
  86.7 12.8 %node_forward.1 = (bf16[1024,512]{1,0:T(8,128)(2,1)}, bf16[1024,512]{1,0:T(8,128)(2,1)}, bf16[1024,2048]{1,0:T(8,128)(2,1)}, bf16[1024,2048]{1,0:T(8,128)(2,1)},...) custom-call(bf16[1024,512]{1,0:T(8,128)(2,1)} %get-tuple-element.48.nodes.table, ...), custom_call_target="tpu_custom_call" | custom-call | tf_op jit(solution)/shard_map/node_forward/pallas_call | solution.py:255
  99.5 0.7 broadcast_in_dim.38.bias
  100.2 0.7 broadcast_in_dim.39.gain
  101.0 83.2 %edge_layer.1 = (bf16[30,192,1024]{2,1,0:T(8,128)(2,1)}, f32[30,192,1024]{2,1,0:T(8,128)}, bf16[1024,512]{1,0:T(8,128)(2,1)}, f32[576,512]{1,0:T(8,128)}, f32[192,128]{1,0:T(8,128)}) custom-call(s32[8]{0:T(128)} %stack.23.meta, bf16[1024,512]{1,0:T(8,128)(2,1)} %get-tuple-element.50.states, s32[30,1024]{1,0:T(8,128)} %bitcast.52, ...), custom_call_target="tpu_custom_call" | custom-call | tf_op jit(solution)/shard_map/edge_layer/pallas_call | solution.py:414
  184.2 0.2 collective-permute-start.3
  184.4 0.0 copy-done.7
  184.4 0.4 collective-permute-start.2
  184.8 2.9 collective-permute-done.2.other_cot
  187.7 0.0 collective-permute-done.3.theirs
  187.7 0.8 copy-done.9
  188.5 0.4 copy-done.6
  188.8 15.6 %node_backward.1 = (f32[1024,512]{1,0:T(8,128)}, bf16[1024,512]{1,0:T(8,128)(2,1)}, bf16[2048,512]{1,0:T(8,128)(2,1)}, f32[8,512]{1,0:T(8,128)}) custom-call(s32[8]{0:T(128)} %stack.23.meta, bf16[512,512]{1,0:T(8,128)(2,1)} %own_cot.1, bf16[512,512]{1,0:T(8,128)(2,1)} %copy-done.9, bf16[1024,512]{1,0:T(8,128)(2,1)} %get-tuple-element.52.mine, ...), custom_call_target="tpu_custom_call" | custom-call | tf_op jit(solution)/shard_map/node_backward/pallas_call | solution.py:565
  204.5 4.2 bitcast_convert_fusion
  208.7 0.0 all-reduce.5.cloned.1.call-update
  208.7 0.0 all-reduce.7.cloned.1.call-start
  208.8 55.3 %message_backward.1 = (f32[512,512]{1,0:T(8,128)}, bf16[512,512]{1,0:T(8,128)(2,1)}, f32[512,512]{1,0:T(8,128)}, f32[512,512]{1,0:T(8,128)}, f32[192,512]{1,0:T(...) custom-call(s32[8]{0:T(128)} %stack.23.meta, bf16[1024,512]{1,0:T(8,128)(2,1)} %get-tuple-element.48.nodes.table, ...), custom_call_target="tpu_custom_call" | custom-call | tf_op jit(solution)/shard_map/message_backward/pallas_call | solution.py:695
  264.1 0.0 copy-start.15
  264.1 0.0 copy-start.14
  264.1 0.0 copy-start.16
  264.1 0.0 all-reduce.7.cloned.1.call-update
  264.1 0.0 all-gather.2.cloned.1.call-start
  264.2 115.3 %all-reduce.5.cloned.1.call-done = f32[1,2048,512]{2,1,0:T(8,128)} async-done(((f32[1,2048,512]{2,1,0:T(8,128)}), f32[1,2048,512]{2,1,0:T(8,128)}) %all-reduce.5.cloned.1.call-update) | async-done | bytes 4194320 | tf_op jit(solution)/shard_map/psum | solution.py:933
  379.5 0.0 all-gather.2.cloned.1.call-update
  379.6 0.8 constant_dynamic-slice_fusion
  380.4 0.0 collective-permute-start.4
  380.4 41.1 %all-reduce = (f32[512]{0:T(512)}, f32[8,512]{1,0:T(8,128)S(1)}, f32[192,2]{1,0:T(8,128)S(1)}) all-reduce(f32[512]{0:T(512)S(1)} %bitcast.66, f32[8,512]{1,0:T(8,128)S(1)} %broadcast_multiply_fusion, f32[192,2]{1,0:T(8,128)S(1)} %bitcast.59), channel_id=1, replica_groups=mesh['res'=16,'nbr'=2] {'res','nbr'}, use_global_device_ids=true, to_apply=%region_4.5 | all-reduce | flops 4992 | bytes 39936 | tf_op jit(solution)/shard_map/psum | solution.py:919
  421.6 0.6 copy.51
  422.2 32.8 %edge_gradient.1 = f32[30,192,1024]{2,1,0:T(8,128)} custom-call(f32[30,192,1024]{2,1,0:T(8,128)} %get-tuple-element.65.partial, bf16[30,512,1024]{2,1,0:T(8,128)(2,1)} %get-tuple-element.62.slope, f32[512,1024]{1,0:T(8,128)} %get-tuple-element.66.spread, bf16[192,512]{1,0:T(8,128)(2,1)} %edge_weight.3), custom_call_target="tpu_custom_call" | custom-call | tf_op jit(solution)/shard_map/edge_gradient/pallas_call | solution.py:750
  454.9 0.8 slice_reduce_fusion
  455.7 0.6 fusion.3
  456.3 0.0 collective-permute-done.4
  456.3 0.0 copy-done.10
  456.3 1.2 add_add_fusion
  457.6 76.1 %all-reduce.7.cloned.1.call-done = (f32[512,512]{1,0:T(8,128)}, f32[512,512]{1,0:T(8,128)}, f32[192,512]{1,0:T(8,128)}, f32[512,512]{1,0:T(8,128)}, f32[576,512]{1,0:T(8,128)}) async-done(((f32[512,512]{1,0:T(8,128)}, f32[512,512]{1,0:T(8,128)}, f32[192,512]{1,0:T(8,128)}, f32[512,512]{1,0:T(8,128)}, f32[576,512]{1,0:T(8,128)}), (f32[512,512]{1,0:T(8,128)}, f32[512,512]{1,0:T(8,128)}, f32[192,512]{1,0:T(8,128)}, ...) | async-done | bytes 4718608 | tf_op jit(solution)/shard_map/psum | solution.py:919
  533.7 1.8 fusion.2
  535.5 2.0 slice_bitcast_fusion.2
  537.5 16.3 %all-gather.2.cloned.1.call-done = f32[2,2048,512]{2,1,0:T(8,128)} async-done(((f32[1,2048,512]{2,1,0:T(8,128)}), f32[2,2048,512]{2,1,0:T(8,128)}) %all-gather.2.cloned.1.call-update) | async-done | bytes 8388624 | tf_op jit(solution)/shard_map/all_gather | solution.py:934
  553.8 2.8 slice_bitcast_fusion.1
  556.7 0.0 slice-start.1
  556.7 2.6 pad_maximum_fusion.1
  559.3 1.3 slice-done.1
  560.5 0.4 fusion.1
  561.0 2.4 pad_maximum_fusion
  563.4 1.0 copy.58
  564.4 1.0 copy.59
  565.3 0.7 copy.60
  566.1 1.0 copy.61
  (32 shorter events, 0.1 us)
Async XLA Ops:
  7.2 372.3 %all-reduce.5.cloned.1.call-start = ((), (), s32[]{:S(2)}) async-start(), calls=%async_computation | async-start | bytes 8388608 | tf_op jit(solution)/shard_map/psum | solution.py:933
  7.2 4.8 collective-permute-start
  12.1 1.5 copy-start.8
  13.6 68.8 %copy-start.11 = (bf16[192,192]{1,0:T(8,128)(2,1)S(1)}, bf16[192,192]{1,0:T(8,128)(2,1)}, u32[]{:S(2)}) copy-start(bf16[192,192]{1,0:T(8,128)(2,1)} %edge_weight.2) | copy-start | bytes 221188
  13.6 69.5 %copy-start.12 = (bf16[192,192]{1,0:T(8,128)(2,1)S(1)}, bf16[192,192]{1,0:T(8,128)(2,1)}, u32[]{:S(2)}) copy-start(bf16[192,192]{1,0:T(8,128)(2,1)} %out_weight.4) | copy-start | bytes 221188
  82.2 17.3 %copy-start.17 = (f32[192]{0:T(256)S(1)}, f32[192]{0:T(256)}, u32[]{:S(2)}) copy-start(f32[192]{0:T(256)} %param.39) | copy-start | bytes 2308
  82.2 18.0 %copy-start.18 = (f32[192]{0:T(256)S(1)}, f32[192]{0:T(256)}, u32[]{:S(2)}) copy-start(f32[192]{0:T(256)} %param.41) | copy-start | bytes 2308
  82.2 3.3 collective-permute-start.1
  85.5 1.1 copy-start.1
  101.0 83.5 %copy-start.7 = (bf16[512,512]{1,0:T(8,128)(2,1)S(1)}, bf16[512,512]{1,0:T(8,128)(2,1)}, u32[]{:S(2)}) copy-start(bf16[512,512]{1,0:T(8,128)(2,1)} %own_cot.1) | copy-start | bytes 1572868
  184.2 3.5 collective-permute-start.3
  184.4 3.3 collective-permute-start.2
  187.7 0.8 copy-start.9
  187.7 1.2 copy-start.6
  208.7 325.0 %all-reduce.7.cloned.1.call-start = ((), (), s32[]{:S(2)}) async-start(), calls=%async_computation.2 | async-start | bytes 9437184 | tf_op jit(solution)/shard_map/psum | solution.py:919
  264.1 115.5 %copy-start = (bf16[1024,512]{1,0:T(8,128)(2,1)S(1)}, bf16[1024,512]{1,0:T(8,128)(2,1)}, u32[]{:S(2)}) copy-start(bf16[1024,512]{1,0:T(8,128)(2,1)} %get-tuple-element.50.states) | copy-start | bytes 3145732
  264.1 116.3 %copy-start.15 = (f32[8,512]{1,0:T(8,128)S(1)}, f32[8,512]{1,0:T(8,128)}, u32[]{:S(2)}) copy-start(f32[8,512]{1,0:T(8,128)} %get-tuple-element.72) | copy-start | bytes 49156
  264.1 116.3 %copy-start.14 = (f32[192,128]{1,0:T(8,128)S(1)}, f32[192,128]{1,0:T(8,128)}, u32[]{:S(2)}) copy-start(f32[192,128]{1,0:T(8,128)} %get-tuple-element.75) | copy-start | bytes 294916
  264.1 116.3 %copy-start.16 = (f32[1,512]{1,0:T(1,128)S(1)}, f32[1,512]{1,0:T(1,128)}, u32[]{:S(2)}) copy-start(f32[1,512]{1,0:T(1,128)} %get-tuple-element.70) | copy-start | bytes 6148
  264.1 289.7 %all-gather.2.cloned.1.call-start = ((), (), s32[]{:S(2)}) async-start(), calls=%async_computation.1 | async-start | bytes 12582912 | tf_op jit(solution)/shard_map/all_gather | solution.py:934
  380.4 75.9 %collective-permute-start.4 = (bf16[512,512]{1,0:T(8,128)(2,1)}, bf16[512,512]{1,0:T(8,128)(2,1)S(1)}, u32[]{:S(2)}, u32[]{:S(2)}) collective-permute-start(bf16[512,512]{1,0:T(8,128)(2,1)} %get-tuple-element.64), channel_id=1, source_target_pairs={{0,1},{1,0},{2,3},{3,2},{4,5},{5,4},{6,7},{7,6},{8,9},{9,8},{10,11... | collective-permute-start | bytes 1572872 | tf_op jit(solution)/shard_map/ppermute | solution.py:29
  422.2 34.1 %copy-start.5 = (f32[512,512]{1,0:T(8,128)S(1)}, f32[512,512]{1,0:T(8,128)}, u32[]{:S(2)}) copy-start(f32[512,512]{1,0:T(8,128)} %get-tuple-element.63) | copy-start | bytes 3145732
  422.2 34.1 %copy-start.10 = (f32[1024,512]{1,0:T(8,128)S(1)}, f32[1024,512]{1,0:T(8,128)}, u32[]{:S(2)}) copy-start(f32[1024,512]{1,0:T(8,128)} %get-tuple-element.59) | copy-start | bytes 6291460
  553.8 5.4 slice-start
  556.7 3.9 slice-start.1
  561.0 2.4 copy-start.4
  561.0 3.4 copy-start.3
  563.4 2.0 copy-start.13
  563.4 2.7 copy-start.2
Sparse Core Ops, SparseCore 0:
  208.8 170.6 all-reduce.4
  387.7 146.0 all-reduce.6
  535.3 18.5 all-gather.1

commit v2 on v1

v2 whole, which is shorter than its diff:
```python
import functools

import jax
import jax.numpy as jnp
from jax import lax
from jax.experimental import pallas as pl
from jax.experimental.pallas import tpu as pltpu
from jax.sharding import PartitionSpec as P

SPAN = 1024
REACH = 32
MASKED = -16384.0
VMEM_BYTES = 60 * 2**20

epsilon = 1e-05
root_half = 0.7071067811865476
inv_root_two_pi = 0.3989422804014327
half_log2_e = 0.7213475204444817

bf16 = jnp.bfloat16
f32 = jnp.float32


def swapped(value, level):
    mask = 2**level
    devices = lax.axis_size("res") * lax.axis_size("nbr")
    pairs = [(source, source ^ mask) for source in range(devices)]
    return lax.ppermute(value, ("res", "nbr"), pairs)


def nn(left_op, right_op):
    return jnp.dot(left_op, right_op, preferred_element_type=f32)


def nt(left_op, right_op):
    return lax.dot_general(
        left_op, right_op, (((1,), (1,)), ((), ())), preferred_element_type=f32
    )


def tn(left_op, right_op):
    return lax.dot_general(
        left_op, right_op, (((0,), (0,)), ((), ())), preferred_element_type=f32
    )


def split(values):
    high = values.astype(bf16)
    return high, (values - high.astype(f32)).astype(bf16)


def twice_gelu_and_slope(values):
    below = 1.0 + lax.erf(values * root_half)
    density = jnp.exp2(values * values * -half_log2_e)
    return values * below, below + values * density * (2.0 * inv_root_two_pi)


def selector(rows, ids):
    places = lax.broadcasted_iota(jnp.int32, (rows, ids.shape[1]), 0)
    return (places == ids).astype(bf16)


def tile_of(rows):
    return min(rows, 256)


def window_of(rows):
    return tile_of(rows) + 2 * REACH


def far_rows(ids, edge):
    return jnp.concatenate([selector(SPAN, ids), edge], axis=0)


def near_rows(ids, edge, first):
    return jnp.concatenate([selector(ids.shape[1] + 2 * REACH, ids - (first - REACH)), edge], axis=0)


def tiles(rows):
    width = tile_of(rows)
    return [(tile, slice(tile * width, (tile + 1) * width)) for tile in range(rows // width)]


def window_rows(local_first, rows, tile):
    start = local_first + tile * tile_of(rows)
    if not isinstance(start, int):
        start = pl.multiple_of(start, 128)
    return pl.ds(start, window_of(rows))


def repeat_lanes(column, width):
    return jnp.concatenate([column] * (width // column.shape[1]), axis=1)


def whole(shape):
    return pl.BlockSpec(shape, lambda *_: (0,) * len(shape))


def params():
    return pltpu.CompilerParams(vmem_limit_bytes=VMEM_BYTES)


smem = pl.BlockSpec(memory_space=pltpu.SMEM)


def message_forward_kernel(
    static_first,
    meta,
    own,
    other,
    ids,
    edges,
    receiver,
    neighbour,
    edge_weight,
    bias,
    table,
    slope,
    packed,
    padded,
    far_table,
    near_table,
    base,
    sums,
    counts,
):
    step = pl.program_id(0)
    rows = base.shape[1]
    half = own.shape[0]
    local_first = pl.multiple_of(meta[1], 128) if static_first is None else static_first

    @pl.when(step == 0)
    def _():
        high = meta[0]
        table[pl.ds(pl.multiple_of(high * half, half), half), :] = own[...]
        table[pl.ds(pl.multiple_of((1 - high) * half, half), half), :] = other[...]
        places = lax.broadcasted_iota(jnp.int32, (SPAN, 1), 0)
        hidden = jnp.where(places < meta[3], 0.0, MASKED)
        projected = (nn(table[...], neighbour[...]) + hidden).astype(bf16)
        far_table[...] = jnp.concatenate([projected, edge_weight[...]], axis=0).T
        padded[...] = jnp.zeros_like(padded)
        padded[REACH : REACH + SPAN, :] = projected
        for tile, _ in tiles(rows):
            window = padded[window_rows(local_first, rows, tile), :]
            near_table[tile] = jnp.concatenate([window, edge_weight[...]], axis=0).T
        block = table[pl.ds(local_first, rows), :]
        places = lax.broadcasted_iota(jnp.int32, (rows, 1), 0) + local_first
        hidden = jnp.where(places < meta[3], 0.0, MASKED)
        base[...] = (nn(block, receiver[...]) + (bias[...] + hidden)).T
        sums[...] = jnp.zeros_like(sums)
        counts[...] = jnp.zeros_like(counts)

    positions = lax.broadcasted_iota(jnp.int32, (1, rows), 1) + local_first
    near, far = (ids[pl.ds(2 * step + side, 1), :] - meta[2] for side in range(2))
    counts[...] += jnp.where(positions < meta[3], 1.0, 0.0) * (
        jnp.where(near < meta[3], 1.0, 0.0) + jnp.where(far < meta[3], 1.0, 0.0)
    )
    for tile, lanes in tiles(rows):
        near_part = near_rows(near[:, lanes], edges[0, :, lanes], local_first + lanes.start)
        far_part = far_rows(far[:, lanes], edges[1, :, lanes])
        far_value = nn(far_table[...], far_part)
        near_value = nn(near_table[tile], near_part)
        far_act, far_slope = twice_gelu_and_slope(far_value + base[:, lanes])
        slope[1, :, lanes] = far_slope.astype(bf16)
        near_act, near_slope = twice_gelu_and_slope(near_value + base[:, lanes])
        slope[0, :, lanes] = near_slope.astype(bf16)
        sums[:, lanes] += far_act + near_act

    @pl.when(step == pl.num_programs(0) - 1)
    def _():
        width = sums.shape[0]
        packed[:width, :] = (0.5 * sums[...]).astype(bf16)
        packed[width:, :] = jnp.broadcast_to(counts[...], (16, rows)).astype(bf16)


def message_forward(meta, own, other, ids, edges, receiver, neighbour, edge_weight, bias, local_first):
    pairs = edges.shape[0] // 2
    width, rows = edges.shape[1:]
    model = own.shape[1]
    return pl.pallas_call(
        functools.partial(message_forward_kernel, local_first),
        name="message_forward",
        grid=(pairs,),
        in_specs=[
            smem,
            whole(own.shape),
            whole(other.shape),
            whole(ids.shape),
            pl.BlockSpec((2, width, rows), lambda i: (i, 0, 0)),
            whole(receiver.shape),
            whole(neighbour.shape),
            whole(edge_weight.shape),
            whole((1, model)),
        ],
        out_specs=[
            whole((SPAN, model)),
            pl.BlockSpec((2, model, rows), lambda i: (i, 0, 0)),
            whole((model + 16, rows)),
        ],
        out_shape=[
            jax.ShapeDtypeStruct((SPAN, model), bf16),
            jax.ShapeDtypeStruct((2 * pairs, model, rows), bf16),
            jax.ShapeDtypeStruct((model + 16, rows), bf16),
        ],
        scratch_shapes=[
            pltpu.VMEM((SPAN + 2 * REACH, model), bf16),
            pltpu.VMEM((model, SPAN + width), bf16),
            pltpu.VMEM((rows // tile_of(rows), model, window_of(rows) + width), bf16),
            pltpu.VMEM((model, rows), f32),
            pltpu.VMEM((model, rows), f32),
            pltpu.VMEM((1, rows), f32),
        ],
        compiler_params=params(),
    )(meta, own, other, ids, edges, receiver, neighbour, edge_weight, bias[None])


def normed(values):
    mean_val = jnp.mean(values, -1, keepdims=True)
    centered = values - mean_val
    inv_std = lax.rsqrt(jnp.mean(centered * centered, -1, keepdims=True) + epsilon)
    return centered * inv_std, inv_std


def node_forward_kernel(
    nodes,
    mine,
    theirs,
    out_weight,
    gain_one,
    ffn_in,
    ffn_bias,
    ffn_out,
    gain_two,
    state,
    ffn_input,
    act,
    slope,
    first,
    second,
    stats,
    sums,
):
    rows, width = nodes.shape
    total = mine[...].astype(f32) + theirs[...].astype(f32)
    count = jnp.maximum(total[width : width + 1, :], 1.0)
    ratio = 1.0 / jnp.broadcast_to(count, (128, rows)).T
    high, low = split(total[:width, :])
    sums[...] = high
    message = tn(high, out_weight[...]) + tn(low, out_weight[...])
    first_sum = nodes[...].astype(f32) + message * repeat_lanes(ratio, width)
    first_unit, first_inv = normed(first_sum)
    first[...] = first_unit
    first_norm = first_unit * gain_one[...]
    low = first_norm.astype(bf16)
    ffn_input[...] = low
    hidden, grad = twice_gelu_and_slope(nn(low, ffn_in[...]) + ffn_bias[...])
    hidden = (0.5 * hidden).astype(bf16)
    act[...] = hidden
    slope[...] = (0.5 * grad).astype(bf16)
    second_unit, second_inv = normed(first_norm + nn(hidden, ffn_out[...]))
    second[...] = second_unit
    state[...] = (second_unit * gain_two[...]).astype(bf16)
    stats[:, :128] = ratio
    stats[:, 128:256] = jnp.broadcast_to(first_inv, ratio.shape)
    stats[:, 256:] = jnp.broadcast_to(second_inv, ratio.shape)


def node_forward(nodes, mine, theirs, out_weight, gain_one, ffn_in, ffn_bias, ffn_out, gain_two):
    rows, model = nodes.shape
    hidden = ffn_in.shape[1]
    chunk = min(rows, 256)

    def by_rows(width):
        return pl.BlockSpec((chunk, width), lambda i: (i, 0))

    return pl.pallas_call(
        node_forward_kernel,
        name="node_forward",
        grid=(rows // chunk,),
        in_specs=[
            by_rows(model),
            pl.BlockSpec((model + 16, chunk), lambda i: (0, i)),
            pl.BlockSpec((model + 16, chunk), lambda i: (0, i)),
            whole(out_weight.shape),
            whole((1, model)),
            whole(ffn_in.shape),
            whole((1, hidden)),
            whole(ffn_out.shape),
            whole((1, model)),
        ],
        out_specs=[
            by_rows(model),
            by_rows(model),
            by_rows(hidden),
            by_rows(hidden),
            by_rows(model),
            by_rows(model),
            by_rows(384),
            pl.BlockSpec((model, chunk), lambda i: (0, i)),
        ],
        out_shape=[
            jax.ShapeDtypeStruct((rows, model), bf16),
            jax.ShapeDtypeStruct((rows, model), bf16),
            jax.ShapeDtypeStruct((rows, hidden), bf16),
            jax.ShapeDtypeStruct((rows, hidden), bf16),
            jax.ShapeDtypeStruct((rows, model), f32),
            jax.ShapeDtypeStruct((rows, model), f32),
            jax.ShapeDtypeStruct((rows, 384), f32),
            jax.ShapeDtypeStruct((model, rows), bf16),
        ],
        compiler_params=params(),
    )(
        nodes, mine, theirs, out_weight, gain_one[None], ffn_in, ffn_bias[None], ffn_out, gain_two[None]
    )


def edge_kernel(
    static_first,
    meta,
    states,
    ids,
    edges,
    cots,
    residue_t,
    neighbour_t,
    edge_weight,
    bias,
    out_weight,
    out_weight_t,
    gain,
    new_edges,
    partial,
    back_table,
    grads,
    vectors,
    padded,
    far_table,
    near_table,
    base,
    gains,
    far_sum,
    near_sum,
    own_sum,
    gain_sum,
    grad_edge,
    grad_out,
):
    step = pl.program_id(0)
    width, rows = base.shape
    window = window_of(rows)
    local_first = pl.multiple_of(meta[1], 128) if static_first is None else static_first

    @pl.when(step == 0)
    def _():
        fill = jnp.zeros((width, 256 - width), bf16)
        weight = jnp.concatenate([edge_weight[...], fill], axis=1)
        projected = nt(states[...], neighbour_t[...]).astype(bf16)
        projected = jnp.concatenate([projected, jnp.zeros((SPAN, 256 - width), bf16)], axis=1)
        far_table[...] = jnp.concatenate([projected, weight], axis=0).T[:width, :]
        padded[...] = jnp.zeros_like(padded)
        padded[REACH : REACH + SPAN, :] = projected
        for tile, _ in tiles(rows):
            part = padded[window_rows(local_first, rows, tile), :]
            near_table[tile] = jnp.concatenate([part, weight], axis=0).T[:width, :]
        block = states[pl.ds(local_first, rows), :]
        base[...] = nt(residue_t[...], block) + repeat_lanes(bias[...], rows)
        gains[...] = repeat_lanes(gain[...], rows)
        for total in (far_sum, near_sum, own_sum, gain_sum, grad_edge, grad_out):
            total[...] = jnp.zeros_like(total)

    for side in range(2):
        near = ids[pl.ds(2 * step + side, 1), :] - meta[2]
        edge = edges[side]
        if side == 0:
            chosen = [
                near_rows(near[:, lanes], edges[0, :, lanes], local_first + lanes.start)
                for _, lanes in tiles(rows)
            ]
            value = jnp.concatenate(
                [nn(near_table[tile], part) for tile, part in enumerate(chosen)], axis=1
            )
        else:
            chosen = far_rows(near, edge)
            value = nn(far_table[...], chosen)
        act, slope = twice_gelu_and_slope(value + base[...])
        act = act.astype(bf16)
        third = edge.astype(f32) + nn(out_weight_t[...], act)
        centered = third - jnp.mean(third, 0, keepdims=True)
        inv_std = lax.rsqrt(jnp.mean(centered * centered, 0, keepdims=True) + epsilon)
        unit = centered * inv_std
        new_edges[side] = (unit * gains[...]).astype(bf16)
        cot = cots[side].astype(f32)
        gain_sum[...] += cot * unit
        scaled = cot * gains[...]
        grad_third = inv_std * (
            scaled
            - jnp.mean(scaled, 0, keepdims=True)
            - unit * jnp.mean(scaled * unit, 0, keepdims=True)
        )
        branch = grad_third.astype(bf16)
        grad_out[...] += nt(act, branch)
        grad_value = (nn(out_weight[...], branch) * slope).astype(bf16)
        own_sum[...] += grad_value.astype(f32)
        partial[side] = grad_third + nn(edge_weight[...], grad_value)
        if side == 0:
            for tile, lanes in tiles(rows):
                found = nt(chosen[tile], grad_value[:, lanes])
                near_sum[window_rows(local_first, rows, tile), :] += found[:window, :]
                grad_edge[...] += found[window:, :]
        else:
            far_sum[...] += nt(chosen, grad_value)

    @pl.when(step == pl.num_programs(0) - 1)
    def _():
        table_high, table_low = split(far_sum[:SPAN, :] + near_sum[REACH : REACH + SPAN, :])
        own_high, own_low = split(own_sum[...])
        back = nn(table_high, neighbour_t[...]) + nn(table_low, neighbour_t[...])
        own_back = tn(own_high, residue_t[...]) + tn(own_low, residue_t[...])
        if rows == SPAN:
            back_table[...] = (back + own_back).astype(bf16)
        else:
            own_rows = pl.ds(local_first, rows)
            back_table[...] = back.astype(bf16)
            back_table[own_rows, :] = (back_table[own_rows, :].astype(f32) + own_back).astype(bf16)
        block = states[pl.ds(local_first, rows), :]
        grads[:width, :] = nn(own_high, block) + nn(own_low, block)
        grads[width : 2 * width, :] = tn(table_high, states[...]) + tn(table_low, states[...])
        grads[2 * width :, :width] = grad_edge[...] + far_sum[SPAN:, :]
        grads[2 * width :, 256 : 256 + width] = 0.5 * grad_out[...]
        ones = jnp.ones((16, rows), bf16)
        gain_high, gain_low = split(gain_sum[...])
        vectors[0:1, :width] = (nt(ones, own_high) + nt(ones, own_low))[:1]
        vectors[1:2, :width] = (nt(ones, gain_high) + nt(ones, gain_low))[:1]


def edge_layer(
    meta, states, ids, edges, cots, residue, neighbour, edge_weight, bias, out_weight, gain, local_first
):
    pairs = edges.shape[0] // 2
    width, rows = edges.shape[1:]
    model = states.shape[1]
    by_pair = pl.BlockSpec((2, width, rows), lambda i: (i, 0, 0))
    square = whole((width, width))
    return pl.pallas_call(
        functools.partial(edge_kernel, local_first),
        name="edge_layer",
        grid=(pairs,),
        in_specs=[
            smem,
            whole(states.shape),
            whole(ids.shape),
            by_pair,
            by_pair,
            whole((width, model)),
            whole((width, model)),
            square,
            whole((width, 128)),
            square,
            square,
            whole((width, 128)),
        ],
        out_specs=[
            by_pair,
            by_pair,
            whole((SPAN, model)),
            whole((3 * width, model)),
            whole((8, model)),
        ],
        out_shape=[
            jax.ShapeDtypeStruct(edges.shape, bf16),
            jax.ShapeDtypeStruct(edges.shape, f32),
            jax.ShapeDtypeStruct((SPAN, model), bf16),
            jax.ShapeDtypeStruct((3 * width, model), f32),
            jax.ShapeDtypeStruct((8, model), f32),
        ],
        scratch_shapes=[
            pltpu.VMEM((SPAN + 2 * REACH, 256), bf16),
            pltpu.VMEM((width, SPAN + width), bf16),
            pltpu.VMEM((rows // tile_of(rows), width, window_of(rows) + width), bf16),
            pltpu.VMEM((width, rows), f32),
            pltpu.VMEM((width, rows), f32),
            pltpu.VMEM((SPAN + width, width), f32),
            pltpu.VMEM((SPAN + 2 * REACH, width), f32),
            pltpu.VMEM((width, rows), f32),
            pltpu.VMEM((width, rows), f32),
            pltpu.VMEM((width, width), f32),
            pltpu.VMEM((width, width), f32),
        ],
        compiler_params=params(),
    )(
        meta,
        states,
        ids,
        edges,
        cots,
        residue.T,
        neighbour.T,
        edge_weight,
        jnp.broadcast_to(bias[:, None], (width, 128)),
        out_weight * 0.5,
        out_weight.T * 0.5,
        jnp.broadcast_to(gain[:, None], (width, 128)),
    )


def norm_back(unit, inv_std, gain, grad_out):
    grad_gain = jnp.sum(grad_out * unit, axis=0, keepdims=True)
    scaled = grad_out * gain
    grad_in = inv_std * (
        scaled
        - jnp.mean(scaled, -1, keepdims=True)
        - unit * jnp.mean(scaled * unit, -1, keepdims=True)
    )
    return grad_in, grad_gain


def node_backward_kernel(
    meta,
    own_cot,
    other_cot,
    mine,
    theirs,
    first,
    second,
    stats,
    ffn_input,
    act,
    slope,
    sums,
    gain_one,
    ffn_in,
    ffn_out,
    gain_two,
    grad_first_ref,
    message_cot,
    weights,
    vectors,
    sum_out,
    sum_in,
    sum_message,
):
    step = pl.program_id(0)
    chunk, model = first.shape
    hidden = act.shape[1]
    core = meta[4]
    half = own_cot.shape[0]

    @pl.when(step == 0)
    def _():
        vectors[...] = jnp.zeros_like(vectors)
        sum_out[...] = jnp.zeros_like(sum_out)
        sum_in[...] = jnp.zeros_like(sum_in)
        sum_message[...] = jnp.zeros_like(sum_message)

    if chunk > half:
        mine_first = core == 0
        lower = jnp.where(mine_first, own_cot[...], other_cot[...])
        cot = jnp.concatenate([lower, jnp.where(mine_first, other_cot[...], own_cot[...])], axis=0)
    else:
        row = step * chunk
        inside = pl.ds(pl.multiple_of(lax.rem(row, half), chunk), chunk)
        cot = jnp.where(row // half == core, own_cot[inside, :], other_cot[inside, :])
    total = cot.astype(f32) + (mine[...].astype(f32) + theirs[...].astype(f32))
    second_inv = stats[:, 256:257]
    first_inv = stats[:, 128:129]
    grad_second, gain_two_part = norm_back(second[...], second_inv, gain_two[...], total)
    top = grad_second.astype(bf16)
    grad_hidden = (nt(top, ffn_out[...]) * slope[...].astype(f32)).astype(bf16)
    out_columns = pl.ds(pl.multiple_of(core * (hidden // 2), 128), hidden // 2)
    in_columns = pl.ds(pl.multiple_of(core * (model // 2), 128), model // 2)
    sum_out[...] += tn(act[:, out_columns], top)
    sum_in[...] += tn(ffn_input[:, in_columns], grad_hidden)
    bias_part = jnp.sum(grad_hidden.astype(f32), axis=0, keepdims=True)
    grad_norm = grad_second + nt(grad_hidden, ffn_in[...])
    grad_first, gain_one_part = norm_back(first[...], first_inv, gain_one[...], grad_norm)
    grad_first_ref[...] = grad_first
    spread = (grad_first * stats[:, :1]).astype(bf16)
    message_cot[...] = spread
    sum_message[...] += nn(sums[pl.ds(pl.multiple_of(core * (model // 2), 16), model // 2), :], spread)
    vectors[0:1, :] += gain_one_part
    vectors[1:2, :] += gain_two_part
    for part in range(hidden // model):
        vectors[2 + part : 3 + part, :] += bias_part[:, part * model : (part + 1) * model]

    @pl.when(step == pl.num_programs(0) - 1)
    def _():
        weights[: hidden // 2, :] = sum_out[...].astype(bf16)
        for part in range(hidden // model):
            start = hidden // 2 + part * (model // 2)
            weights[start : start + model // 2, :] = sum_in[
                :, part * model : (part + 1) * model
            ].astype(bf16)
        weights[hidden:, :] = sum_message[...].astype(bf16)


def node_backward(
    meta, own_cot, other_cot, mine, theirs, first, second, stats, ffn_input, act, slope, sums, gain_one, ffn_in, ffn_out, gain_two
):
    rows, model = first.shape
    hidden = act.shape[1]
    chunk = min(rows, 256)

    def by_rows(width):
        return pl.BlockSpec((chunk, width), lambda i: (i, 0))

    return pl.pallas_call(
        node_backward_kernel,
        name="node_backward",
        grid=(rows // chunk,),
        in_specs=[
            smem,
            whole(own_cot.shape),
            whole(other_cot.shape),
            by_rows(model),
            by_rows(model),
            by_rows(model),
            by_rows(model),
            by_rows(384),
            by_rows(model),
            by_rows(hidden),
            by_rows(hidden),
            pl.BlockSpec((model, chunk), lambda i: (0, i)),
            whole((1, model)),
            whole(ffn_in.shape),
            whole(ffn_out.shape),
            whole((1, model)),
        ],
        out_specs=[
            by_rows(model),
            by_rows(model),
            whole((hidden + model // 2, model)),
            whole((8, model)),
        ],
        out_shape=[
            jax.ShapeDtypeStruct((rows, model), f32),
            jax.ShapeDtypeStruct((rows, model), bf16),
            jax.ShapeDtypeStruct((hidden + model // 2, model), bf16),
            jax.ShapeDtypeStruct((8, model), f32),
        ],
        scratch_shapes=[
            pltpu.VMEM((hidden // 2, model), f32),
            pltpu.VMEM((model // 2, hidden), f32),
            pltpu.VMEM((model // 2, model), f32),
        ],
        compiler_params=params(),
    )(
        meta,
        own_cot,
        other_cot,
        mine,
        theirs,
        first,
        second,
        stats,
        ffn_input,
        act,
        slope,
        sums,
        gain_one[None],
        ffn_in,
        ffn_out,
        gain_two[None],
    )


def message_backward_kernel(
    static_first,
    meta,
    table,
    cot,
    ids,
    edges,
    slope,
    receiver,
    neighbour,
    out_weight,
    edge_grads,
    edge_vectors,
    node_vectors,
    keep,
    send,
    keep_weights,
    send_weights,
    spread,
    far_sum,
    near_sum,
    own_sum,
    weights,
):
    step = pl.program_id(0)
    model, rows = spread.shape
    width = edges.shape[1]
    half = keep.shape[0]
    local_first = pl.multiple_of(meta[1], 128) if static_first is None else static_first

    @pl.when(step == 0)
    def _():
        spread[...] = 0.5 * nt(out_weight[...], cot[...])
        for total in (far_sum, near_sum, own_sum, weights):
            total[...] = jnp.zeros_like(total)

    window = window_of(rows)
    edge_rows = slice(2 * model, 2 * model + width)
    near, far = (ids[pl.ds(2 * step + side, 1), :] - meta[2] for side in range(2))
    far_grad = (spread[...] * slope[1].astype(f32)).astype(bf16)
    near_grad = (spread[...] * slope[0].astype(f32)).astype(bf16)
    own_sum[...] += far_grad.astype(f32) + near_grad.astype(f32)
    far_sum[...] += nt(far_rows(far, edges[1]), far_grad)
    for tile, lanes in tiles(rows):
        part = near_rows(near[:, lanes], edges[0, :, lanes], local_first + lanes.start)
        found = nt(part, near_grad[:, lanes])
        near_sum[window_rows(local_first, rows, tile), :] += found[:window, :]
        weights[edge_rows, :] += found[window:, :]

    @pl.when(step == pl.num_programs(0) - 1)
    def _():
        table_sum = far_sum[:SPAN, :] + near_sum[REACH : REACH + SPAN, :]
        own_rows = own_sum[...].T
        table_high, table_low = split(table_sum)
        own_high, own_low = split(own_rows)
        nodes_t = table[...].T
        block_t = nodes_t
        if rows < SPAN:
            block_t = table[pl.ds(local_first, rows), :].T
        weights[:model, :] = nn(block_t, own_high) + nn(block_t, own_low)
        weights[model : 2 * model, :] = nn(nodes_t, table_high) + nn(nodes_t, table_low)
        weights[edge_rows, :] += far_sum[SPAN:, :]
        start = edge_rows.stop
        weights[start : start + 3 * width, :] = edge_grads[...]
        start += 3 * width
        weights[start : start + 8, :] = edge_vectors[...]
        weights[start + 8 : start + 16, :] = 0.5 * node_vectors[...]
        weights[start + 16 : start + 17, :] = jnp.sum(own_rows, axis=0, keepdims=True)
        core = meta[4]
        split_rows = keep_weights.shape[0]
        mine = pl.multiple_of(core * split_rows, split_rows)
        keep_weights[...] = weights[pl.ds(mine, split_rows), :]
        send_weights[...] = weights[pl.ds(split_rows - mine, split_rows), :].astype(bf16)
        back = nt(table_high, neighbour[...]) + nt(table_low, neighbour[...])
        own_back = nt(own_high, receiver[...]) + nt(own_low, receiver[...])
        if rows == SPAN:
            far_sum[:SPAN, :] = back + own_back
        else:
            far_sum[:SPAN, :] = back
            far_sum[pl.ds(local_first, rows), :] += own_back
        high = meta[0]
        keep[...] = far_sum[pl.ds(pl.multiple_of(high * half, half), half), :]
        send[...] = far_sum[pl.ds(pl.multiple_of((1 - high) * half, half), half), :].astype(bf16)


def message_backward(
    meta, table, cot, ids, edges, slope, receiver, neighbour, out_weight, edge_grads, edge_vectors, node_vectors, local_first
):
    pairs = edges.shape[0] // 2
    width, rows = edges.shape[1:]
    model = table.shape[1]
    square = whole((model, model))
    used = 2 * model + 4 * width + 24
    split_rows = -(-used // 512) * 256
    return pl.pallas_call(
        functools.partial(message_backward_kernel, local_first),
        name="message_backward",
        grid=(pairs,),
        in_specs=[
            smem,
            whole(table.shape),
            whole(cot.shape),
            whole(ids.shape),
            pl.BlockSpec((2, width, rows), lambda i: (i, 0, 0)),
            pl.BlockSpec((2, model, rows), lambda i: (i, 0, 0)),
            square,
            square,
            square,
            whole(edge_grads.shape),
            whole(edge_vectors.shape),
            whole(node_vectors.shape),
        ],
        out_specs=[
            whole((SPAN // 2, model)),
            whole((SPAN // 2, model)),
            whole((split_rows, model)),
            whole((split_rows, model)),
            whole((model, rows)),
        ],
        out_shape=[
            jax.ShapeDtypeStruct((SPAN // 2, model), f32),
            jax.ShapeDtypeStruct((SPAN // 2, model), bf16),
            jax.ShapeDtypeStruct((split_rows, model), f32),
            jax.ShapeDtypeStruct((split_rows, model), bf16),
            jax.ShapeDtypeStruct((model, rows), f32),
        ],
        scratch_shapes=[
            pltpu.VMEM((SPAN + width, model), f32),
            pltpu.VMEM((SPAN + 2 * REACH, model), f32),
            pltpu.VMEM((model, rows), f32),
            pltpu.VMEM((2 * split_rows, model), f32),
        ],
        compiler_params=params(),
    )(
        meta,
        table,
        cot,
        ids,
        edges,
        slope,
        receiver,
        neighbour,
        out_weight,
        edge_grads,
        edge_vectors,
        node_vectors,
    )


def edge_gradient_kernel(partial, slope, spread, edge_weight, out):
    for side in range(partial.shape[0]):
        grad_value = (spread[...] * slope[side].astype(f32)).astype(bf16)
        out[side] = partial[side] + nn(edge_weight[...], grad_value)


def edge_gradient(first, count, values, slope, spread, edge_weight):
    width, rows = values.shape[1:]
    model = spread.shape[0]
    by_pair = pl.BlockSpec((2, width, rows), lambda i: (first + i, 0, 0))
    return pl.pallas_call(
        edge_gradient_kernel,
        name="edge_gradient",
        grid=(count,),
        in_specs=[
            by_pair,
            pl.BlockSpec((2, model, rows), lambda i: (first + i, 0, 0)),
            whole(spread.shape),
            whole(edge_weight.shape),
        ],
        out_specs=by_pair,
        out_shape=jax.ShapeDtypeStruct(values.shape, f32),
        input_output_aliases={0: 0},
        compiler_params=params(),
    )(values, slope, spread, edge_weight)


def sum_to_slots_kernel(shift, meta, *refs):
    parts, outs, total = refs[:-5], refs[-5:-1], refs[-1]
    total[...] = parts[0][...].astype(f32)
    for part in parts[1:]:
        total[...] += part[...].astype(f32)
    place = meta[5] >> shift & 3
    rows = outs[0].shape[0]
    for slot, out in enumerate(outs):
        start = pl.multiple_of((place ^ slot) * rows, rows)
        out[...] = total[pl.ds(start, rows), :].astype(out.dtype)


def sum_to_slots(meta, shift, parts):
    rows, width = parts[0].shape
    out_types = (f32, bf16, bf16, bf16)
    return pl.pallas_call(
        functools.partial(sum_to_slots_kernel, shift),
        name="sum_to_slots",
        in_specs=[smem] + [whole(part.shape) for part in parts],
        out_specs=[whole((rows // 4, width))] * 4,
        out_shape=[jax.ShapeDtypeStruct((rows // 4, width), kind) for kind in out_types],
        scratch_shapes=[pltpu.VMEM((rows, width), f32)],
        compiler_params=params(),
    )(meta, *parts)


def sum_parts_kernel(*refs):
    total = refs[0][...].astype(f32)
    for part in refs[1:-1]:
        total = total + part[...].astype(f32)
    refs[-1][...] = total.astype(bf16)


def sum_parts(parts):
    return pl.pallas_call(
        sum_parts_kernel,
        name="sum_parts",
        in_specs=[whole(part.shape) for part in parts],
        out_specs=whole(parts[0].shape),
        out_shape=jax.ShapeDtypeStruct(parts[0].shape, bf16),
        compiler_params=params(),
    )(*parts)


def assemble_kernel(shift, meta, *refs):
    place = meta[5] >> shift & 3
    rows = refs[0].shape[0]
    for slot, part in enumerate(refs[:-1]):
        start = pl.multiple_of((place ^ slot) * rows, rows)
        refs[-1][pl.ds(start, rows), :] = part[...]


def assemble(meta, shift, parts):
    rows, width = parts[0].shape
    return pl.pallas_call(
        functools.partial(assemble_kernel, shift),
        name="assemble",
        in_specs=[smem] + [whole(part.shape) for part in parts],
        out_specs=whole((4 * rows, width)),
        out_shape=jax.ShapeDtypeStruct((4 * rows, width), bf16),
        compiler_params=params(),
    )(meta, *parts)


def sent_each_way(shift, slots):
    return [moved(slot, place << shift) for place, slot in enumerate(slots) if place > 0]


def moved(value, mask):
    devices = lax.axis_size("res") * lax.axis_size("nbr")
    cores = lax.axis_size("nbr")
    pairs = [(source, source ^ (mask * cores)) for source in range(devices)]
    return lax.ppermute(value, ("res", "nbr"), pairs)


def unpack_early_kernel(meta, own, other, grad_out, grad_in, message_out):
    core = meta[4]
    hidden, model = grad_out.shape
    half = model // 2
    for side, source in enumerate((own, other)):
        place = core if side == 0 else 1 - core
        grad_out[pl.ds(pl.multiple_of(place * (hidden // 2), 8), hidden // 2), :] = source[
            : hidden // 2, :
        ].astype(f32)
        rows = pl.ds(pl.multiple_of(place * half, 8), half)
        for part in range(hidden // model):
            start = hidden // 2 + part * half
            grad_in[rows, part * model : (part + 1) * model] = source[start : start + half, :].astype(f32)
        message_out[rows, :] = source[hidden:, :].astype(f32)


def unpack_early(meta, own, other, hidden):
    model = own.shape[1]
    return pl.pallas_call(
        unpack_early_kernel,
        name="unpack_early",
        in_specs=[smem, whole(own.shape), whole(other.shape)],
        out_specs=[whole((hidden, model)), whole((model, hidden)), whole((model, model))],
        out_shape=[
            jax.ShapeDtypeStruct((hidden, model), f32),
            jax.ShapeDtypeStruct((model, hidden), f32),
            jax.ShapeDtypeStruct((model, model), f32),
        ],
        compiler_params=params(),
    )(meta, own, other)


def unpack_late_kernel(
    meta, own, other, grad_self, grad_near, grad_edge, edge_self, edge_near, edge_edge, edge_out, vectors, weights
):
    core = meta[4]
    rows, model = own.shape
    width = edge_self.shape[0]
    mine = pl.multiple_of(core * rows, rows)
    weights[pl.ds(mine, rows), :] = own[...]
    weights[pl.ds(rows - mine, rows), :] = other[...]
    grad_self[...] = weights[:model, :].astype(f32)
    grad_near[...] = weights[model : 2 * model, :].astype(f32)
    start = 2 * model
    for out in (grad_edge, edge_self, edge_near):
        out[...] = weights[start : start + width, :].astype(f32)
        start += width
    edge_edge[...] = weights[start : start + width, :width].astype(f32)
    edge_out[...] = weights[start : start + width, 256 : 256 + width].astype(f32)
    start += width
    vectors[...] = weights[start : start + 32, :].astype(f32)


def unpack_late(meta, own, other, width):
    rows, model = own.shape
    shapes = [(model, model)] * 2 + [(width, model)] * 3 + [(width, width)] * 2 + [(32, model)]
    return pl.pallas_call(
        unpack_late_kernel,
        name="unpack_late",
        in_specs=[smem, whole(own.shape), whole(other.shape)],
        out_specs=[whole(shape) for shape in shapes],
        out_shape=[jax.ShapeDtypeStruct(shape, f32) for shape in shapes],
        scratch_shapes=[pltpu.VMEM((2 * rows, model), bf16)],
        compiler_params=params(),
    )(meta, own, other)


def planes(size):
    return [[4 * block + place for place in range(4)] for block in range(size // 4)]


def columns(size):
    return [[4 * block + place for block in range(size // 4)] for place in range(4)]


def tied(*arrays):
    return lax.optimization_barrier(arrays)


def early_parts(size):
    if size != 16:
        return (
            lambda value: lax.psum(value.astype(f32), "res").astype(bf16),
            lambda value: value,
            lambda value: value,
        )
    return (
        lambda value: lax.psum_scatter(value, "res", axis_index_groups=planes(size), tiled=True),
        lambda value: lax.psum(value, "res", axis_index_groups=columns(size)),
        lambda value: lax.all_gather(value, "res", axis_index_groups=planes(size), tiled=True),
    )


def late_sum(meta, kept, sent, size, value, pieces, early, early_steps):
    received = swapped(sent, 0)
    early = early_steps[1](early)
    value, received = tied(pieces[0](value), received)
    if size != 16:
        total = lax.psum(kept + received.astype(f32), "res").astype(bf16)
        for piece in pieces[1:]:
            value = piece(value)
        return total, value, early_steps[2](early)
    value, kept, *slots = tied(value, *sum_to_slots(meta, 0, [kept, received]))
    value, *received = tied(pieces[1](value), *sent_each_way(0, [kept, *slots]))
    value, kept, *slots = tied(value, *sum_to_slots(meta, 2, [kept, *received]))
    value, *received = tied(pieces[2](value), *sent_each_way(2, [kept, *slots]))
    value, early, mine = tied(value, early, sum_parts([kept, *received]))
    early = early_steps[2](early)
    value, *received = tied(pieces[3](value), *sent_each_way(2, [mine] * 4))
    value, mine = tied(value, assemble(meta, 2, [mine, *received]))
    value, early, *received = tied(pieces[4](value), early, *sent_each_way(0, [mine] * 4))
    return assemble(meta, 0, [mine, *received]), value, early


def joined(table, other, high_side):
    return jnp.where(
        high_side, jnp.concatenate([other, table], axis=0), jnp.concatenate([table, other], axis=0)
    )


def halves(table, high_side):
    half = table.shape[0] // 2
    lower, upper = (table[:half], table[half:])
    return (jnp.where(high_side, upper, lower), jnp.where(high_side, lower, upper))


def sum_blocks(table, device, level):
    keep, send = halves(table, device >> level & 1 == 1)
    return keep + swapped(send.astype(bf16), level).astype(keep.dtype)


def on_device(
    nodes,
    edges,
    neighbours,
    lengths,
    message_receiver_weight,
    message_neighbour_weight,
    message_edge_weight,
    message_hidden_bias,
    message_output_weight,
    gain_one,
    ffn_in,
    ffn_bias,
    ffn_out,
    gain_two,
    edge_update_residue_weight,
    edge_update_neighbour_weight,
    edge_update_edge_weight,
    edge_update_bias,
    edge_out,
    gain_three,
    node_cot,
    edge_cot,
):
    rows, half_k, edge_width = edges.shape
    own_rows, model = nodes.shape
    hidden = ffn_in.shape[1]
    levels = (SPAN // own_rows).bit_length() - 1
    core = lax.axis_index("nbr")
    device = lax.axis_index("res") * lax.axis_size("nbr") + core
    first_row = lax.axis_index("res") * rows
    bucket = first_row // SPAN
    group_start = bucket * SPAN
    local_first = 0 if rows == SPAN else None
    length = jnp.sum(jnp.where(jnp.arange(lengths.shape[0]) == bucket, lengths, 0))
    top = device >> (levels - 1) & 1
    meta = jnp.stack(
        [top, first_row - group_start, group_start, length, core, lax.axis_index("res"), 0, 0]
    ).astype(jnp.int32)

    ids = neighbours.T
    edges_t = edges.transpose(1, 2, 0)
    cot_t = edge_cot.transpose(1, 2, 0)

    table = nodes
    for level in range(levels - 1):
        table = joined(table, swapped(table, level), device >> level & 1 == 1)
    other_table = swapped(table, levels - 1)
    other_cot = swapped(node_cot, 0)

    node_table, slope, packed = message_forward(
        meta,
        table,
        other_table,
        ids,
        edges_t,
        message_receiver_weight,
        message_neighbour_weight,
        message_edge_weight,
        message_hidden_bias,
        local_first,
    )
    block = node_table
    if rows < SPAN:
        block = lax.dynamic_slice_in_dim(node_table, first_row - group_start, rows, 0)
    state, ffn_input, act, ffn_slope, first, second, stats, sums = node_forward(
        block,
        packed,
        swapped(packed, 0),
        message_output_weight,
        gain_one,
        ffn_in,
        ffn_bias,
        ffn_out,
        gain_two,
    )
    states = state
    for level in range(1, levels):
        states = joined(states, swapped(states, level), device >> level & 1 == 1)
    new_edges, partial, back, edge_grads, edge_vectors = edge_layer(
        meta,
        states,
        ids,
        edges_t,
        cot_t,
        edge_update_residue_weight,
        edge_update_neighbour_weight,
        edge_update_edge_weight,
        edge_update_bias,
        edge_out,
        gain_three,
        local_first,
    )
    for level in reversed(range(1, levels)):
        back = sum_blocks(back, device, level)
    grad_first, message_cot, early, node_vectors = node_backward(
        meta,
        node_cot,
        other_cot,
        back,
        swapped(back, 0),
        first,
        second,
        stats,
        ffn_input,
        act,
        ffn_slope,
        sums,
        gain_one,
        ffn_in,
        ffn_out,
        gain_two,
    )
    size = lax.axis_size("res")
    early_steps = early_parts(size)
    early = early_steps[0](early)
    keep, send, kept_weights, sent_weights, spread = message_backward(
        meta,
        node_table,
        message_cot,
        ids,
        edges_t,
        slope,
        message_receiver_weight,
        message_neighbour_weight,
        message_output_weight,
        edge_grads,
        edge_vectors,
        node_vectors,
        local_first,
    )
    early, kept_weights, sent_weights = tied(early, kept_weights, sent_weights)
    kept = keep + swapped(send, levels - 1).astype(f32)
    for level in reversed(range(levels - 1)):
        kept = sum_blocks(kept, device, level)
    pieces = 5 if half_k % 10 == 0 else 1
    count = half_k // 2 // pieces

    def piece(index):
        return lambda values: edge_gradient(index * count, count, values, slope, spread, message_edge_weight)

    late, edge_grad, early = late_sum(
        meta,
        kept_weights,
        sent_weights,
        size,
        partial,
        [piece(index) for index in range(pieces)],
        early,
        early_steps,
    )
    own_first = lax.dynamic_slice_in_dim(grad_first, core * own_rows, own_rows, 0)
    node_grad = own_first + kept
    node_out = lax.dynamic_slice_in_dim(state, core * own_rows, own_rows, 0)
    grad_ffn_out, grad_ffn_in, grad_msg_out = unpack_early(meta, early, swapped(early, 0), hidden)
    (
        grad_msg_self,
        grad_msg_nbr,
        grad_msg_edge,
        grad_edge_self,
        grad_edge_nbr,
        grad_edge_edge,
        grad_edge_out,
        vectors,
    ) = unpack_late(meta, late, swapped(late, 0), edge_width)
    return (
        node_out,
        new_edges.transpose(2, 0, 1),
        node_grad,
        edge_grad.transpose(2, 0, 1),
        grad_msg_self,
        grad_msg_nbr,
        grad_msg_edge,
        vectors[16],
        grad_msg_out,
        vectors[8],
        grad_ffn_in,
        vectors[10 : 10 + hidden // model].reshape(-1),
        grad_ffn_out,
        vectors[9],
        grad_edge_self.T,
        grad_edge_nbr.T,
        grad_edge_edge,
        vectors[0, :edge_width],
        grad_edge_out,
        vectors[1, :edge_width],
    )


def solution(mesh):
    rows = P(("res", "nbr"), None)
    pairs = P("res", "nbr", None)
    placed = (rows, pairs, P("res", "nbr")) + (P(),) * 17 + (rows, pairs)
    return jax.shard_map(
        on_device,
        mesh=mesh,
        in_specs=placed,
        out_specs=(rows, pairs, rows, pairs) + (P(),) * 16,
        check_vma=False,
    )
```

time: 574 us -> 358 us (0.62)
  waiting for transfers between devices: 212 us -> 25.7 us
  blocking collectives: 41.1 us -> 0 us
  starting transfers between devices: 1.35 us -> 18.8 us
  Pallas kernels: 268 us -> 276 us
  local copies, waits for them, and re-layouts: 24.7 us -> 17.6 us
  other arithmetic: 11.7 us -> 4.89 us
    psum x2 -> x1, waiting for transfers between devices: 191 us -> 0.01 us  [early_parts(): lax.psum(value, 'res', axis_index_groups=columns(size))]
    psum x1 -> x0, blocking collectives: 41.1 us -> none  [on_device(): lax.psum((grad_msg_self, grad_msg_nbr, grad_msg_edge, grad_msg_bias, grad...]
    pallas_call x1 -> x12, Pallas kernels: 32.8 us -> 64 us  [the longest x5 42.9 us: edge_gradient(): pl.pallas_call(edge_gradient_kernel, name='edge_gradient', grid=(count,),...]
    ppermute x0 -> x12, starting transfers between devices: none -> 16.7 us  [moved(): return lax.ppermute(value, ('res', 'nbr'), pairs)]
    pallas_call x1, Pallas kernels: 68.6 us -> 53.1 us  [message_forward(): pl.pallas_call(functools.partial(message_forward_kernel, local_first), na...]
    ppermute x0 -> x12, waiting for transfers between devices: none -> 9.51 us  [moved(): return lax.ppermute(value, ('res', 'nbr'), pairs)]
    pallas_call x1, Pallas kernels: 55.3 us -> 46.5 us  [message_backward(): pl.pallas_call(functools.partial(message_backward_kernel, local_first), n...]
    all_gather x1, waiting for transfers between devices: 16.3 us -> 8.4 us  [early_parts(): lax.all_gather(value, 'res', axis_index_groups=planes(size), tiled=True)]
  transfers between devices with their start and end apart: 8 -> 23, of which waited for: 5 -> 7; matrix products, arithmetic and copies ran while one was open for 2% -> 3% of each run, Pallas kernels for 15% -> 29%
where the time goes in v2:
time: 358 us; the launch traced here: 357 us
  Pallas kernels  276 us (77%)
  waiting for transfers between devices  25.7 us (7%)
  starting transfers between devices  18.8 us (5%)
  local copies, waits for them, and re-layouts  17.6 us (5%)
  between operations  13.9 us (4%)
  other arithmetic  4.89 us (1%)
    pallas_call x1, Pallas kernels, edge_layer(): pl.pallas_call(functools.partial(edge_kernel, local_first), name='edge_la...  80.5 us
    pallas_call x1, Pallas kernels, message_forward(): pl.pallas_call(functools.partial(message_forward_kernel, local_first), na...  53.1 us
    pallas_call x1, Pallas kernels, message_backward(): pl.pallas_call(functools.partial(message_backward_kernel, local_first), n...  46.5 us
    pallas_call x5, Pallas kernels, edge_gradient(): pl.pallas_call(edge_gradient_kernel, name='edge_gradient', grid=(count,),...  42.9 us
    pallas_call x1, Pallas kernels, node_backward(): pl.pallas_call(node_backward_kernel, name='node_backward', grid=(rows //...  16.8 us
    ppermute x12, starting transfers between devices, moved(): return lax.ppermute(value, ('res', 'nbr'), pairs)  16.7 us
    pallas_call x1, Pallas kernels, node_forward(): pl.pallas_call(node_forward_kernel, name='node_forward', grid=(rows // ch...  15.3 us
    unnamed x43, local copies, waits for them, and re-layouts  10.6 us
  transfers between devices with their start and end apart: 23, of which 7 were waited for; matrix products, arithmetic and copies ran while one was open for 3% of the time, Pallas kernels for 29%

profile of v2, /device:TPU:0, one launch (start us, length us, event | category | flops | bytes accessed | tf_op | source)
XLA Modules:
  0.0 357.1 jit_solution(15312184175930171186)
XLA Ops:
  7.2 0.5 collective-permute-start
  7.8 1.3 fusion
  9.0 1.2 stack.27.meta
  10.3 0.8 copy-done.6
  11.1 53.1 %message_forward.1 = (bf16[1024,512]{1,0:T(8,128)(2,1)}, bf16[30,512,1024]{2,1,0:T(8,128)(2,1)}, bf16[528,1024]{1,0:T(8,128)(2,1)}) custom-call(s32[8]{0:T(128)} %stack.27.meta, bf16[512,512]{1,0:T(8,128)(2,1)} %own.1, bf16[512,512]{1,0:T(8,128)(2,1)} %copy-done.6, s32[30,1024]{1,0:T(8,128)} %bitcast.34, bf16[30,192,1024]{2,1,0:T(8,128)(2,1)} %bitcast.30, ...), custom_call_target="tpu_custom_call" | custom-call | tf_op jit(solution)/shard_map/message_forward/pallas_call | solution.py:180
  64.3 0.7 fusion.1
  64.9 0.7 copy.48.out_weight
  65.7 1.4 collective-permute-done.1.theirs
  67.0 1.0 copy-done.2
  68.0 15.3 %node_forward.1 = (bf16[1024,512]{1,0:T(8,128)(2,1)}, bf16[1024,512]{1,0:T(8,128)(2,1)}, bf16[1024,2048]{1,0:T(8,128)(2,1)}, bf16[1024,2048]{1,0:T(8,128)(2,1)},...) custom-call(bf16[1024,512]{1,0:T(8,128)(2,1)} %get-tuple-element.101.nodes.table, ...), custom_call_target="tpu_custom_call" | custom-call | tf_op jit(solution)/shard_map/node_forward/pallas_call | solution.py:276
  83.4 0.7 broadcast_in_dim.35.bias
  84.1 0.7 broadcast_in_dim.36.gain
  84.8 80.5 %edge_layer.1 = (bf16[30,192,1024]{2,1,0:T(8,128)(2,1)}, f32[30,192,1024]{2,1,0:T(8,128)}, bf16[1024,512]{1,0:T(8,128)(2,1)}, f32[576,512]{1,0:T(8,128)}, f32[8,512]{1,0:T(8,128)}) custom-call(s32[8]{0:T(128)} %stack.27.meta, bf16[1024,512]{1,0:T(8,128)(2,1)} %get-tuple-element.103.states, s32[30,1024]{1,0:T(8,128)} %bitcast.35, ...), custom_call_target="tpu_custom_call" | custom-call | tf_op jit(solution)/shard_map/edge_layer/pallas_call | solution.py:444
  165.3 0.2 collective-permute-start.3
  165.5 0.4 collective-permute-start.2
  165.9 2.9 collective-permute-done.2.other_cot
  168.8 0.8 copy-done.7
  169.6 0.4 copy-done.3
  170.0 16.8 %node_backward.1 = (f32[1024,512]{1,0:T(8,128)}, bf16[1024,512]{1,0:T(8,128)(2,1)}, bf16[2304,512]{1,0:T(8,128)(2,1)}, f32[8,512]{1,0:T(8,128)}) custom-call(s32[8]{0:T(128)} %stack.27.meta, bf16[512,512]{1,0:T(8,128)(2,1)} %own_cot.1, bf16[512,512]{1,0:T(8,128)(2,1)} %copy-done.7, bf16[1024,512]{1,0:T(8,128)(2,1)} %get-tuple-element.105.mine, ...), custom_call_target="tpu_custom_call" | custom-call | tf_op jit(solution)/shard_map/node_backward/pallas_call | solution.py:606
  186.8 46.5 %message_backward.1 = (f32[512,512]{1,0:T(8,128)}, bf16[512,512]{1,0:T(8,128)(2,1)}, f32[1024,512]{1,0:T(8,128)}, bf16[1024,512]{1,0:T(8,128)(2,1)}, f32[512,1024]{1,0:T(8,128)}) custom-call(s32[8]{0:T(128)} %stack.27.meta, bf16[1024,512]{1,0:T(8,128)(2,1)} %get-tuple-element.101.nodes.table, bf16[1024,512]{1,0:T(8,128)(2,1)} %get-tuple-element.114.cot, ...), custom_call_target="tpu_custom_call" | custom-call | tf_op jit(solution)/shard_map/message_backward/pallas_call | solution.py:760
  233.4 0.2 collective-permute-start.5
  233.7 8.7 %edge_gradient.5.partial = f32[30,192,1024]{2,1,0:T(8,128)} custom-call(f32[30,192,1024]{2,1,0:T(8,128)} %get-tuple-element.121.partial, bf16[30,512,1024]{2,1,0:T(8,128)(2,1)} %get-tuple-element.115.slope, f32[512,1024]{1,0:T(8,128)} %get-tuple-element.122.spread, bf16[192,512]{1,0:T(8,128)(2,1)} %edge_weight.13), custom_call_target="tpu_custom_call", output_to_operand_aliasing={{}: (0, {})} | custom-call | tf_op jit(solution)/shard_map/edge_gradient/pallas_call | solution.py:825
  242.4 1.0 copy-done.4
  243.4 3.3 sum_to_slots.2
  246.6 2.9 collective-permute-start.6
  249.5 1.5 collective-permute-start.7
  251.0 8.5 %edge_gradient.6.partial = f32[30,192,1024]{2,1,0:T(8,128)} custom-call(f32[30,192,1024]{2,1,0:T(8,128)} %edge_gradient.5.partial, bf16[30,512,1024]{2,1,0:T(8,128)(2,1)} %get-tuple-element.115.slope, f32[512,1024]{1,0:T(8,128)} %get-tuple-element.122.spread, bf16[192,512]{1,0:T(8,128)(2,1)} %edge_weight.13), custom_call_target="tpu_custom_call", output_to_operand_aliasing={{}: (0, {})} | custom-call | tf_op jit(solution)/shard_map/edge_gradient/pallas_call | solution.py:825
  259.6 3.8 %collective-permute-done.7.refs_2_ = bf16[256,512]{1,0:T(8,128)(2,1)S(1)} collective-permute-done((bf16[256,512]{1,0:T(8,128)(2,1)}, bf16[256,512]{1,0:T(8,128)(2,1)S(1)}, u32[]{:S(2)}, u32[]{:S(2)}) %collective-permute-start.7) | collective-permute-done | bytes 262176 | tf_op jit(solution)/shard_map/ppermute | solution.py:914
  263.4 0.7 copy-done.9
  264.1 0.7 copy-done.10
  264.8 2.2 sum_to_slots.3
  267.0 1.6 collective-permute-start.9
  268.5 2.6 collective-permute-start.10
  271.1 0.2 collective-permute-start.11
  271.3 8.5 %edge_gradient.7.partial = f32[30,192,1024]{2,1,0:T(8,128)} custom-call(f32[30,192,1024]{2,1,0:T(8,128)} %edge_gradient.6.partial, bf16[30,512,1024]{2,1,0:T(8,128)(2,1)} %get-tuple-element.115.slope, f32[512,1024]{1,0:T(8,128)} %get-tuple-element.122.spread, bf16[192,512]{1,0:T(8,128)(2,1)} %edge_weight.13), custom_call_target="tpu_custom_call", output_to_operand_aliasing={{}: (0, {})} | custom-call | tf_op jit(solution)/shard_map/edge_gradient/pallas_call | solution.py:825
  279.9 0.6 copy-done.15
  280.5 0.6 copy-done.17
  281.1 1.6 sum_parts.1.refs_0_
  282.8 0.7 collective-permute-start.12
  283.5 3.5 collective-permute-start.13
  287.0 0.2 collective-permute-start.14
  287.2 8.6 %edge_gradient.8.partial = f32[30,192,1024]{2,1,0:T(8,128)} custom-call(f32[30,192,1024]{2,1,0:T(8,128)} %edge_gradient.7.partial, bf16[30,512,1024]{2,1,0:T(8,128)(2,1)} %get-tuple-element.115.slope, f32[512,1024]{1,0:T(8,128)} %get-tuple-element.122.spread, bf16[192,512]{1,0:T(8,128)(2,1)} %edge_weight.13), custom_call_target="tpu_custom_call", output_to_operand_aliasing={{}: (0, {})} | custom-call | tf_op jit(solution)/shard_map/edge_gradient/pallas_call | solution.py:825
  295.9 0.6 copy-done.12
  296.5 0.6 copy-done.14
  297.2 1.7 assemble.2.refs_0_
  298.8 1.2 collective-permute-start.15
  300.0 0.9 collective-permute-start.16
  300.9 1.4 collective-permute-start.17
  302.3 8.6 %edge_gradient.9 = f32[30,192,1024]{2,1,0:T(8,128)} custom-call(f32[30,192,1024]{2,1,0:T(8,128)} %edge_gradient.8.partial, bf16[30,512,1024]{2,1,0:T(8,128)(2,1)} %get-tuple-element.115.slope, f32[512,1024]{1,0:T(8,128)} %get-tuple-element.122.spread, bf16[192,512]{1,0:T(8,128)(2,1)} %edge_weight.13), custom_call_target="tpu_custom_call", output_to_operand_aliasing={{}: (0, {})} | custom-call | tf_op jit(solution)/shard_map/edge_gradient/pallas_call | solution.py:825
  310.9 0.3 collective-permute-done.16.refs_2_
  311.2 5.3 %collective-permute-done.17.refs_3_ = bf16[256,512]{1,0:T(8,128)(2,1)} collective-permute-done((bf16[256,512]{1,0:T(8,128)(2,1)}, bf16[256,512]{1,0:T(8,128)(2,1)}, u32[]{:S(2)}, u32[]{:S(2)}) %collective-permute-start.17) | collective-permute-done | bytes 262176 | tf_op jit(solution)/shard_map/ppermute | solution.py:914
  316.5 8.4 %all-gather.2.cloned.1.call-done.own = bf16[2304,512]{1,0:T(8,128)(2,1)} async-done(((bf16[576,512]{1,0:T(8,128)(2,1)}), bf16[2304,512]{1,0:T(8,128)(2,1)}) %all-gather.2.cloned.1.call-update) | async-done | bytes 2359312 | tf_op jit(solution)/shard_map/all_gather | solution.py:1006
  325.0 2.2 assemble.3.own
  327.2 0.5 collective-permute-start.18
  327.7 0.8 constant_dynamic-slice_fusion
  328.6 3.5 collective-permute-done.4
  332.1 2.9 add_add_fusion
  335.0 3.6 %unpack_late.1 = (f32[512,512]{1,0:T(8,128)}, f32[512,512]{1,0:T(8,128)}, f32[192,512]{1,0:T(8,128)}, f32[192,512]{1,0:T(8,128)}, f32[192,512]{1,0:T(8,128)}, /*...) custom-call(s32[8]{0:T(128)} %stack.27.meta, bf16[1024,512]{1,0:T(8,128)(2,1)} %assemble.3.own, ...), custom_call_target="tpu_custom_call" | custom-call | tf_op jit(solution)/shard_map/unpack_late/pallas_call | solution.py:973
  338.6 0.7 slice_bitcast_fusion
  339.3 0.6 copy.49
  339.9 1.3 fusion.2
  341.3 1.4 fusion.3
  342.7 1.4 copy-done.1
  344.1 6.5 %unpack_early.1 = (f32[2048,512]{1,0:T(8,128)}, f32[512,2048]{1,0:T(8,128)}, f32[512,512]{1,0:T(8,128)}) custom-call(s32[8]{0:T(128)} %stack.27.meta, bf16[2304,512]{1,0:T(8,128)(2,1)} %all-gather.2.cloned.1.call-done.own, bf16[2304,512]{1,0:T(8,128)(2,1)} %copy-done.1), custom_call_target="tpu_custom_call" | custom-call | tf_op jit(solution)/shard_map/unpack_early/pallas_call | solution.py:935
  (56 shorter events, 0.6 us)
Async XLA Ops:
  7.2 226.2 %reduce-scatter.2.cloned.1.call-start = ((), (), s32[]{:S(2)}) async-start(), calls=%async_computation.1 | async-start | bytes 2949120 | tf_op jit(solution)/shard_map/reduce_scatter | solution.py:1004
  7.2 3.0 collective-permute-start
  10.3 0.8 copy-start.6
  11.1 53.1 %copy-start.11 = (bf16[192,192]{1,0:T(8,128)(2,1)S(1)}, bf16[192,192]{1,0:T(8,128)(2,1)}, u32[]{:S(2)}) copy-start(bf16[192,192]{1,0:T(8,128)(2,1)} %param.40) | copy-start | bytes 221188
  64.1 2.9 collective-permute-start.1
  67.0 1.0 copy-start.2
  68.0 15.3 %copy-start.18 = (f32[192]{0:T(256)S(1)}, f32[192]{0:T(256)}, u32[]{:S(2)}) copy-start(f32[192]{0:T(256)} %param.39) | copy-start | bytes 2308
  68.0 16.1 %copy-start.19 = (f32[192]{0:T(256)S(1)}, f32[192]{0:T(256)}, u32[]{:S(2)}) copy-start(f32[192]{0:T(256)} %param.41) | copy-start | bytes 2308
  84.8 80.7 %copy-start.5 = (bf16[512,512]{1,0:T(8,128)(2,1)S(1)}, bf16[512,512]{1,0:T(8,128)(2,1)}, u32[]{:S(2)}) copy-start(bf16[512,512]{1,0:T(8,128)(2,1)} %own_cot.1) | copy-start | bytes 1572868
  165.3 3.5 collective-permute-start.3
  165.5 3.3 collective-permute-start.2
  168.8 0.8 copy-start.7
  168.8 1.2 copy-start.3
  186.8 96.0 %all-reduce.2.cloned.1.call-start = ((), (), s32[]{:S(2)}) async-start(), calls=%async_computation.2 | async-start | bytes 1179648 | tf_op jit(solution)/shard_map/psum | solution.py:1005
  233.4 9.0 %collective-permute-start.5 = (bf16[1024,512]{1,0:T(8,128)(2,1)}, bf16[1024,512]{1,0:T(8,128)(2,1)S(1)}, u32[]{:S(2)}, u32[]{:S(2)}) collective-permute-start(bf16[1024,512]{1,0:T(8,128)(2,1)} %get-tuple-element.126), channel_id=1, source_target_pairs={{0,1},{1,0},{2,3},{3,2},{4,5},{5,4},{6,7},{7,6},{8,9},{9,8},{10,11... | collective-permute-start | bytes 3145736 | tf_op jit(solution)/shard_map/ppermute | solution.py:28
  233.6 91.3 %all-gather.2.cloned.1.call-start = ((), (), s32[]{:S(2)}) async-start(), calls=%async_computation.3 | async-start | bytes 2949120 | tf_op jit(solution)/shard_map/all_gather | solution.py:1006
  242.4 1.0 copy-start.4
  246.6 12.9 %collective-permute-start.6 = (bf16[256,512]{1,0:T(8,128)(2,1)}, bf16[256,512]{1,0:T(8,128)(2,1)S(1)}, u32[]{:S(2)}, u32[]{:S(2)}) collective-permute-start(bf16[256,512]{1,0:T(8,128)(2,1)} %get-tuple-element.135), channel_id=1, source_target_pairs={{0,2},{1,3},{2,0},{3,1},{4,6},{5,7},{6,4},{7,5},{8,10},{9,11},{10,... | collective-permute-start | bytes 786440 | tf_op jit(solution)/shard_map/ppermute | solution.py:914
  249.5 13.9 %collective-permute-start.7 = (bf16[256,512]{1,0:T(8,128)(2,1)}, bf16[256,512]{1,0:T(8,128)(2,1)S(1)}, u32[]{:S(2)}, u32[]{:S(2)}) collective-permute-start(bf16[256,512]{1,0:T(8,128)(2,1)} %get-tuple-element.136), channel_id=1, source_target_pairs={{0,4},{1,5},{2,6},{3,7},{4,0},{5,1},{6,2},{7,3},{8,12},{9,13},{10,... | collective-permute-start | bytes 786440 | tf_op jit(solution)/shard_map/ppermute | solution.py:914
  251.0 12.4 %collective-permute-start.8 = (bf16[256,512]{1,0:T(8,128)(2,1)}, bf16[256,512]{1,0:T(8,128)(2,1)S(1)}, u32[]{:S(2)}, u32[]{:S(2)}) collective-permute-start(bf16[256,512]{1,0:T(8,128)(2,1)} %get-tuple-element.137), channel_id=1, source_target_pairs={{0,6},{1,7},{2,4},{3,5},{4,2},{5,3},{6,0},{7,1},{8,14},{9,15},{10,... | collective-permute-start | bytes 786440 | tf_op jit(solution)/shard_map/ppermute | solution.py:914
  259.5 3.8 %copy-start.8 = (bf16[256,512]{1,0:T(8,128)(2,1)}, bf16[256,512]{1,0:T(8,128)(2,1)S(1)}, u32[]{:S(2)}) copy-start(bf16[256,512]{1,0:T(8,128)(2,1)S(1)} %collective-permute-done.6.refs_1_) | copy-start | bytes 786436
  263.4 0.7 copy-start.9
  264.1 0.7 copy-start.10
  267.0 12.9 %collective-permute-start.9 = (bf16[64,512]{1,0:T(8,128)(2,1)}, bf16[64,512]{1,0:T(8,128)(2,1)S(1)}, u32[]{:S(2)}, u32[]{:S(2)}) collective-permute-start(bf16[64,512]{1,0:T(8,128)(2,1)} %get-tuple-element.148), channel_id=1, source_target_pairs={{0,8},{1,9},{2,10},{3,11},{4,12},{5,13},{6,14},{7,15},{8,0},{9,1},... | collective-permute-start | bytes 196616 | tf_op jit(solution)/shard_map/ppermute | solution.py:914
  268.5 11.3 %collective-permute-start.10 = (bf16[64,512]{1,0:T(8,128)(2,1)}, bf16[64,512]{1,0:T(8,128)(2,1)S(1)}, u32[]{:S(2)}, u32[]{:S(2)}) collective-permute-start(bf16[64,512]{1,0:T(8,128)(2,1)} %get-tuple-element.149), channel_id=1, source_target_pairs={{0,16},{1,17},{2,18},{3,19},{4,20},{5,21},{6,22},{7,23},{8,24},{9,... | collective-permute-start | bytes 196616 | tf_op jit(solution)/shard_map/ppermute | solution.py:914
  271.1 8.8 %collective-permute-start.11 = (bf16[64,512]{1,0:T(8,128)(2,1)}, bf16[64,512]{1,0:T(8,128)(2,1)S(1)}, u32[]{:S(2)}, u32[]{:S(2)}) collective-permute-start(bf16[64,512]{1,0:T(8,128)(2,1)} %get-tuple-element.150), channel_id=1, source_target_pairs={{0,24},{1,25},{2,26},{3,27},{4,28},{5,29},{6,30},{7,31},{8,16},{9,... | collective-permute-start | bytes 196616 | tf_op jit(solution)/shard_map/ppermute | solution.py:914
  279.8 0.6 copy-start.15
  279.8 0.6 copy-start.16
  280.5 0.6 copy-start.17
  282.8 13.1 %collective-permute-start.12 = (bf16[64,512]{1,0:T(8,128)(2,1)}, bf16[64,512]{1,0:T(8,128)(2,1)S(1)}, u32[]{:S(2)}, u32[]{:S(2)}) collective-permute-start(bf16[64,512]{1,0:T(8,128)(2,1)} %sum_parts.1.refs_0_), channel_id=1, source_target_pairs={{0,8},{1,9},{2,10},{3,11},{4,12},{5,13},{6,14},{7,15},{8,0},{9,1},... | collective-permute-start | bytes 196616 | tf_op jit(solution)/shard_map/ppermute | solution.py:914
  283.5 12.4 %collective-permute-start.13 = (bf16[64,512]{1,0:T(8,128)(2,1)}, bf16[64,512]{1,0:T(8,128)(2,1)S(1)}, u32[]{:S(2)}, u32[]{:S(2)}) collective-permute-start(bf16[64,512]{1,0:T(8,128)(2,1)} %sum_parts.1.refs_0_), channel_id=1, source_target_pairs={{0,16},{1,17},{2,18},{3,19},{4,20},{5,21},{6,22},{7,23},{8,24},{9,... | collective-permute-start | bytes 196616 | tf_op jit(solution)/shard_map/ppermute | solution.py:914
  287.0 8.9 %collective-permute-start.14 = (bf16[64,512]{1,0:T(8,128)(2,1)}, bf16[64,512]{1,0:T(8,128)(2,1)S(1)}, u32[]{:S(2)}, u32[]{:S(2)}) collective-permute-start(bf16[64,512]{1,0:T(8,128)(2,1)} %sum_parts.1.refs_0_), channel_id=1, source_target_pairs={{0,24},{1,25},{2,26},{3,27},{4,28},{5,29},{6,30},{7,31},{8,16},{9,... | collective-permute-start | bytes 196616 | tf_op jit(solution)/shard_map/ppermute | solution.py:914
  295.9 0.6 copy-start.12
  295.9 0.6 copy-start.13
  296.5 0.6 copy-start.14
  298.8 12.1 %collective-permute-start.15 = (bf16[256,512]{1,0:T(8,128)(2,1)}, bf16[256,512]{1,0:T(8,128)(2,1)}, u32[]{:S(2)}, u32[]{:S(2)}) collective-permute-start(bf16[256,512]{1,0:T(8,128)(2,1)} %assemble.2.refs_0_), channel_id=1, source_target_pairs={{0,2},{1,3},{2,0},{3,1},{4,6},{5,7},{6,4},{7,5},{8,10},{9,11},{10,... | collective-permute-start | bytes 786440 | tf_op jit(solution)/shard_map/ppermute | solution.py:914
  300.0 11.2 %collective-permute-start.16 = (bf16[256,512]{1,0:T(8,128)(2,1)}, bf16[256,512]{1,0:T(8,128)(2,1)}, u32[]{:S(2)}, u32[]{:S(2)}) collective-permute-start(bf16[256,512]{1,0:T(8,128)(2,1)} %assemble.2.refs_0_), channel_id=1, source_target_pairs={{0,4},{1,5},{2,6},{3,7},{4,0},{5,1},{6,2},{7,3},{8,12},{9,13},{10,... | collective-permute-start | bytes 786440 | tf_op jit(solution)/shard_map/ppermute | solution.py:914
  300.9 15.6 %collective-permute-start.17 = (bf16[256,512]{1,0:T(8,128)(2,1)}, bf16[256,512]{1,0:T(8,128)(2,1)}, u32[]{:S(2)}, u32[]{:S(2)}) collective-permute-start(bf16[256,512]{1,0:T(8,128)(2,1)} %assemble.2.refs_0_), channel_id=1, source_target_pairs={{0,6},{1,7},{2,4},{3,5},{4,2},{5,3},{6,0},{7,1},{8,14},{9,15},{10,... | collective-permute-start | bytes 786440 | tf_op jit(solution)/shard_map/ppermute | solution.py:914
  310.9 16.9 %copy-start = (bf16[1024,512]{1,0:T(8,128)(2,1)S(1)}, bf16[1024,512]{1,0:T(8,128)(2,1)}, u32[]{:S(2)}) copy-start(bf16[1024,512]{1,0:T(8,128)(2,1)} %get-tuple-element.103.states) | copy-start | bytes 3145732
  324.9 17.7 %collective-permute-start.19 = (bf16[2304,512]{1,0:T(8,128)(2,1)}, bf16[2304,512]{1,0:T(8,128)(2,1)S(1)}, u32[]{:S(2)}, u32[]{:S(2)}) collective-permute-start(bf16[2304,512]{1,0:T(8,128)(2,1)} %all-gather.2.cloned.1.call-done.own), channel_id=1, source_target_pairs={{0,1},{1,0},{2,3},{3,2},{4,5},{5,4},{6,7},{7,6},{8,9},{9,8},{10,11... | collective-permute-start | bytes 7077896 | tf_op jit(solution)/shard_map/ppermute | solution.py:28
  327.2 7.8 %collective-permute-start.18 = (bf16[1024,512]{1,0:T(8,128)(2,1)}, bf16[1024,512]{1,0:T(8,128)(2,1)}, u32[]{:S(2)}, u32[]{:S(2)}) collective-permute-start(bf16[1024,512]{1,0:T(8,128)(2,1)} %assemble.3.own), channel_id=1, source_target_pairs={{0,1},{1,0},{2,3},{3,2},{4,5},{5,4},{6,7},{7,6},{8,9},{9,8},{10,11... | collective-permute-start | bytes 3145736 | tf_op jit(solution)/shard_map/ppermute | solution.py:28
  327.7 4.4 %collective-permute-start.4 = (bf16[512,512]{1,0:T(8,128)(2,1)}, bf16[512,512]{1,0:T(8,128)(2,1)}, u32[]{:S(2)}, u32[]{:S(2)}) collective-permute-start(bf16[512,512]{1,0:T(8,128)(2,1)} %get-tuple-element.120), channel_id=1, source_target_pairs={{0,1},{1,0},{2,3},{3,2},{4,5},{5,4},{6,7},{7,6},{8,9},{9,8},{10,11... | collective-permute-start | bytes 1572872 | tf_op jit(solution)/shard_map/ppermute | solution.py:28
  342.7 1.4 copy-start.1
Sparse Core Ops, SparseCore 0:
  186.9 39.8 reduce-scatter.1
  233.7 46.4 all-reduce.1
  282.9 42.0 all-gather.1

commit v3 on v2

v3 whole, which is shorter than its diff:
```python
import functools

import jax
import jax.numpy as jnp
from jax import lax
from jax.experimental import pallas as pl
from jax.experimental.pallas import tpu as pltpu
from jax.sharding import PartitionSpec as P

SPAN = 1024
REACH = 32
MASKED = -16384.0
FORWARD_GROUP = 2
EDGE_GROUP = 6
MSG_GROUP = 6
NODE_CHUNK = 256

epsilon = 1e-05
root_half = 0.7071067811865476
inv_root_two_pi = 0.3989422804014327
half_log2_e = 0.7213475204444817

bf16 = jnp.bfloat16
f32 = jnp.float32


def swapped(value, level):
    mask = 2**level
    devices = lax.axis_size("res") * lax.axis_size("nbr")
    pairs = [(source, source ^ mask) for source in range(devices)]
    return lax.ppermute(value, ("res", "nbr"), pairs)


def nn(left_op, right_op):
    return jnp.dot(left_op, right_op, preferred_element_type=f32)


def nt(left_op, right_op):
    return lax.dot_general(
        left_op, right_op, (((1,), (1,)), ((), ())), preferred_element_type=f32
    )


def tn(left_op, right_op):
    return lax.dot_general(
        left_op, right_op, (((0,), (0,)), ((), ())), preferred_element_type=f32
    )


def split(values):
    high = values.astype(bf16)
    return high, (values - high.astype(f32)).astype(bf16)


def twice_gelu_and_slope(values):
    below = 1.0 + lax.erf(values * root_half)
    density = jnp.exp2(values * values * -half_log2_e)
    return values * below, below + values * density * (2.0 * inv_root_two_pi)


def selector(rows, ids):
    places = lax.broadcasted_iota(jnp.int16, (rows, ids.shape[1]), 0)
    return jnp.where(places == ids.astype(jnp.int16), bf16(1), bf16(0))


def group_of(count, wanted):
    return wanted if count % wanted == 0 else 2


def tile_of(rows):
    return min(rows, 256)


def window_of(rows):
    return tile_of(rows) + 2 * REACH


def far_rows(ids, edge):
    return jnp.concatenate([selector(SPAN, ids), edge], axis=0)


def near_rows(ids, edge, first):
    return jnp.concatenate([selector(ids.shape[1] + 2 * REACH, ids - (first - REACH)), edge], axis=0)


def beside(parts):
    return parts[0] if len(parts) == 1 else jnp.concatenate(parts, axis=1)


def tiles(rows):
    width = tile_of(rows)
    return [(tile, slice(tile * width, (tile + 1) * width)) for tile in range(rows // width)]


def window_rows(local_first, rows, tile):
    start = local_first + tile * tile_of(rows)
    if not isinstance(start, int):
        start = pl.multiple_of(start, 128)
    return pl.ds(start, window_of(rows))


def repeat_lanes(column, width):
    return jnp.concatenate([column] * (width // column.shape[1]), axis=1)


def whole(shape):
    return pl.BlockSpec(shape, lambda *_: (0,) * len(shape))


def params(mebibytes=60):
    return pltpu.CompilerParams(vmem_limit_bytes=mebibytes * 2**20)


smem = pl.BlockSpec(memory_space=pltpu.SMEM)


def message_forward_kernel(
    static_first,
    meta,
    lengths,
    own,
    other,
    ids,
    edges,
    receiver,
    neighbour,
    edge_weight,
    bias,
    table,
    slope,
    packed,
    padded,
    far_table,
    near_table,
    base,
    sums,
    counts,
):
    step = pl.program_id(0)
    rows = base.shape[1]
    half = own.shape[0]
    length = lengths[meta[3]]
    local_first = pl.multiple_of(meta[1], 128) if static_first is None else static_first

    @pl.when(step == 0)
    def _():
        high = meta[0]
        table[pl.ds(pl.multiple_of(high * half, half), half), :] = own[...]
        table[pl.ds(pl.multiple_of((1 - high) * half, half), half), :] = other[...]
        places = lax.broadcasted_iota(jnp.int32, (SPAN, 1), 0)
        hidden = jnp.where(places < length, 0.0, MASKED)
        projected = (nn(table[...], neighbour[...]) + hidden).astype(bf16)
        far_table[...] = jnp.concatenate([projected, edge_weight[...]], axis=0).T
        padded[...] = jnp.zeros_like(padded)
        padded[REACH : REACH + SPAN, :] = projected
        for tile, _ in tiles(rows):
            window = padded[window_rows(local_first, rows, tile), :]
            near_table[tile] = jnp.concatenate([window, edge_weight[...]], axis=0).T
        block = table[pl.ds(local_first, rows), :]
        places = lax.broadcasted_iota(jnp.int32, (rows, 1), 0) + local_first
        hidden = jnp.where(places < length, 0.0, MASKED)
        base[...] = (nn(block, receiver[...]) + (bias[...] + hidden)).T
        sums[...] = jnp.zeros_like(sums)
        counts[...] = jnp.zeros_like(counts)

    positions = lax.broadcasted_iota(jnp.int32, (1, rows), 1) + local_first
    group = edges.shape[0]
    near = [ids[pl.ds(group * step + k, 1), :] - meta[2] for k in range(group)]
    counts[...] += jnp.where(positions < length, 1.0, 0.0) * sum(
        jnp.where(place < length, 1.0, 0.0) for place in near
    )
    for tile, lanes in tiles(rows):
        for k in range(0, group, 2):
            near_part = near_rows(near[k][:, lanes], edges[k, :, lanes], local_first + lanes.start)
            far_part = far_rows(near[k + 1][:, lanes], edges[k + 1, :, lanes])
            far_value = nn(far_table[...], far_part)
            near_value = nn(near_table[tile], near_part)
            far_act, far_slope = twice_gelu_and_slope(far_value + base[:, lanes])
            slope[k + 1, :, lanes] = far_slope.astype(bf16)
            near_act, near_slope = twice_gelu_and_slope(near_value + base[:, lanes])
            slope[k, :, lanes] = near_slope.astype(bf16)
            sums[:, lanes] += far_act + near_act

    @pl.when(step == pl.num_programs(0) - 1)
    def _():
        width = sums.shape[0]
        packed[:width, :] = (0.5 * sums[...]).astype(bf16)
        packed[width:, :] = jnp.broadcast_to(counts[...], (16, rows)).astype(bf16)


def message_forward(meta, lengths, own, other, ids, edges, receiver, neighbour, edge_weight, bias, local_first):
    columns_in = edges.shape[0]
    group = group_of(columns_in, FORWARD_GROUP)
    width, rows = edges.shape[1:]
    model = own.shape[1]
    return pl.pallas_call(
        functools.partial(message_forward_kernel, local_first),
        name="message_forward",
        grid=(columns_in // group,),
        in_specs=[
            smem,
            smem,
            whole(own.shape),
            whole(other.shape),
            whole(ids.shape),
            pl.BlockSpec((group, width, rows), lambda i: (i, 0, 0)),
            whole(receiver.shape),
            whole(neighbour.shape),
            whole(edge_weight.shape),
            whole((1, model)),
        ],
        out_specs=[
            whole((SPAN, model)),
            pl.BlockSpec((group, model, rows), lambda i: (i, 0, 0)),
            whole((model + 16, rows)),
        ],
        out_shape=[
            jax.ShapeDtypeStruct((SPAN, model), bf16),
            jax.ShapeDtypeStruct((columns_in, model, rows), bf16),
            jax.ShapeDtypeStruct((model + 16, rows), bf16),
        ],
        scratch_shapes=[
            pltpu.VMEM((SPAN + 2 * REACH, model), bf16),
            pltpu.VMEM((model, SPAN + width), bf16),
            pltpu.VMEM((rows // tile_of(rows), model, window_of(rows) + width), bf16),
            pltpu.VMEM((model, rows), f32),
            pltpu.VMEM((model, rows), f32),
            pltpu.VMEM((1, rows), f32),
        ],
        compiler_params=params(),
    )(meta, lengths, own, other, ids, edges, receiver, neighbour, edge_weight, bias[None])


def normed(values):
    mean_val = jnp.mean(values, -1, keepdims=True)
    centered = values - mean_val
    inv_std = lax.rsqrt(jnp.mean(centered * centered, -1, keepdims=True) + epsilon)
    return centered * inv_std, inv_std


def node_forward_kernel(
    meta,
    nodes,
    mine,
    theirs,
    out_weight,
    gain_one,
    ffn_in,
    ffn_bias,
    ffn_out,
    gain_two,
    state,
    ffn_input,
    act,
    slope,
    first,
    second,
    stats,
    sums,
    own_state,
):
    step = pl.program_id(0)
    rows, width = nodes.shape
    total = mine[...].astype(f32) + theirs[...].astype(f32)
    count = jnp.maximum(total[width : width + 1, :], 1.0)
    ratio = 1.0 / jnp.broadcast_to(count, (128, rows)).T
    high, low = split(total[:width, :])
    sums[...] = high
    message = tn(high, out_weight[...]) + tn(low, out_weight[...])
    first_sum = nodes[...].astype(f32) + message * repeat_lanes(ratio, width)
    first_unit, first_inv = normed(first_sum)
    first[...] = first_unit.astype(bf16)
    first_norm = first_unit * gain_one[...]
    low = first_norm.astype(bf16)
    ffn_input[...] = low
    hidden, grad = twice_gelu_and_slope(nn(low, ffn_in[...]) + ffn_bias[...])
    hidden = (0.5 * hidden).astype(bf16)
    act[...] = hidden
    slope[...] = (0.5 * grad).astype(bf16)
    second_unit, second_inv = normed(first_norm + nn(hidden, ffn_out[...]))
    second[...] = second_unit.astype(bf16)
    out = (second_unit * gain_two[...]).astype(bf16)
    state[...] = out
    store_own_rows(own_state, out, step, meta[4])
    lane = lax.broadcasted_iota(jnp.int32, ratio.shape, 1)
    stats[...] = jnp.where(lane == 0, ratio, jnp.where(lane == 1, first_inv, second_inv))


def store_own_rows(own, values, step, core):
    half, chunk = own.shape[0], values.shape[0]
    if chunk > half:
        own[...] = jnp.where(core == 0, values[:half, :], values[half:, :])
        return
    place = step * chunk

    @pl.when(place // half == core)
    def _():
        own[pl.ds(pl.multiple_of(lax.rem(place, half), chunk), chunk), :] = values


def node_forward(meta, nodes, mine, theirs, out_weight, gain_one, ffn_in, ffn_bias, ffn_out, gain_two):
    rows, model = nodes.shape
    hidden = ffn_in.shape[1]
    chunk = min(rows, NODE_CHUNK)

    def by_rows(width):
        return pl.BlockSpec((chunk, width), lambda i: (i, 0))

    return pl.pallas_call(
        node_forward_kernel,
        name="node_forward",
        grid=(rows // chunk,),
        in_specs=[
            smem,
            by_rows(model),
            pl.BlockSpec((model + 16, chunk), lambda i: (0, i)),
            pl.BlockSpec((model + 16, chunk), lambda i: (0, i)),
            whole(out_weight.shape),
            whole((1, model)),
            whole(ffn_in.shape),
            whole((1, hidden)),
            whole(ffn_out.shape),
            whole((1, model)),
        ],
        out_specs=[
            by_rows(model),
            by_rows(model),
            by_rows(hidden),
            by_rows(hidden),
            by_rows(model),
            by_rows(model),
            by_rows(128),
            pl.BlockSpec((model, chunk), lambda i: (0, i)),
            whole((rows // 2, model)),
        ],
        out_shape=[
            jax.ShapeDtypeStruct((rows, model), bf16),
            jax.ShapeDtypeStruct((rows, model), bf16),
            jax.ShapeDtypeStruct((rows, hidden), bf16),
            jax.ShapeDtypeStruct((rows, hidden), bf16),
            jax.ShapeDtypeStruct((rows, model), bf16),
            jax.ShapeDtypeStruct((rows, model), bf16),
            jax.ShapeDtypeStruct((rows, 128), f32),
            jax.ShapeDtypeStruct((model, rows), bf16),
            jax.ShapeDtypeStruct((rows // 2, model), bf16),
        ],
        compiler_params=params(),
    )(
        meta, nodes, mine, theirs, out_weight, gain_one[None], ffn_in, ffn_bias[None], ffn_out, gain_two[None]
    )


def edge_kernel(
    static_first,
    meta,
    states,
    ids,
    edges,
    cots,
    residue_t,
    neighbour_t,
    edge_weight,
    bias,
    out_weight,
    out_weight_t,
    gain,
    new_edges,
    partial,
    back_table,
    grads,
    squares,
    vectors,
    padded,
    far_table,
    near_table,
    base,
    gains,
    far_sum,
    near_sum,
    own_sum,
    gain_sum,
    grad_edge,
    grad_out,
):
    step = pl.program_id(0)
    width, rows = base.shape
    window = window_of(rows)
    local_first = pl.multiple_of(meta[1], 128) if static_first is None else static_first

    @pl.when(step == 0)
    def _():
        fill = jnp.zeros((width, 256 - width), bf16)
        weight = jnp.concatenate([edge_weight[...], fill], axis=1)
        projected = nt(states[...], neighbour_t[...]).astype(bf16)
        projected = jnp.concatenate([projected, jnp.zeros((SPAN, 256 - width), bf16)], axis=1)
        far_table[...] = jnp.concatenate([projected, weight], axis=0).T[:width, :]
        padded[...] = jnp.zeros_like(padded)
        padded[REACH : REACH + SPAN, :] = projected
        for tile, _ in tiles(rows):
            part = padded[window_rows(local_first, rows, tile), :]
            near_table[tile] = jnp.concatenate([part, weight], axis=0).T[:width, :]
        block = states[pl.ds(local_first, rows), :]
        base[...] = nt(residue_t[...], block) + repeat_lanes(bias[...], rows)
        gains[...] = repeat_lanes(gain[...], rows)
        for total in (far_sum, near_sum, own_sum, gain_sum, grad_edge, grad_out):
            total[...] = jnp.zeros_like(total)

    group = edges.shape[0]
    order = list(range(1, group, 2)) + list(range(0, group, 2))
    found_rows, found_grads = {}, {}
    for side in order:
        near = ids[pl.ds(group * step + side, 1), :] - meta[2]
        edge = edges[side]
        if side % 2 == 0:
            chosen = [
                near_rows(near[:, lanes], edges[side, :, lanes], local_first + lanes.start)
                for _, lanes in tiles(rows)
            ]
            value = jnp.concatenate(
                [nn(near_table[tile], part) for tile, part in enumerate(chosen)], axis=1
            )
        else:
            chosen = far_rows(near, edge)
            value = nn(far_table[...], chosen)
        act, slope = twice_gelu_and_slope(value + base[...])
        act = act.astype(bf16)
        third = edge.astype(f32) + nn(out_weight_t[...], act)
        centered = third - jnp.mean(third, 0, keepdims=True)
        inv_std = lax.rsqrt(jnp.mean(centered * centered, 0, keepdims=True) + epsilon)
        unit = centered * inv_std
        new_edges[side] = (unit * gains[...]).astype(bf16)
        cot = cots[side].astype(f32)
        gain_sum[...] += cot * unit
        scaled = cot * gains[...]
        grad_third = inv_std * (
            scaled
            - jnp.mean(scaled, 0, keepdims=True)
            - unit * jnp.mean(scaled * unit, 0, keepdims=True)
        )
        branch = grad_third.astype(bf16)
        grad_out[...] += nt(act, branch)
        grad_wide = nn(out_weight[...], branch) * slope
        own_sum[...] += grad_wide
        grad_value = grad_wide.astype(bf16)
        partial[side] = (grad_third + nn(edge_weight[...], grad_value)).astype(bf16)
        found_rows[side], found_grads[side] = chosen, grad_value
        if side == order[group // 2 - 1]:
            far_sum[...] += nt(
                beside([found_rows[k] for k in order[: group // 2]]),
                beside([found_grads[k] for k in order[: group // 2]]),
            )
    for tile, lanes in tiles(rows):
        found = nt(
            beside([found_rows[k][tile] for k in range(0, group, 2)]),
            beside([found_grads[k][:, lanes] for k in range(0, group, 2)]),
        )
        near_sum[window_rows(local_first, rows, tile), :] += found[:window, :]
        grad_edge[...] += found[window:, :]

    @pl.when(step == pl.num_programs(0) - 1)
    def _():
        table_high, table_low = split(far_sum[:SPAN, :] + near_sum[REACH : REACH + SPAN, :])
        own_high, own_low = split(own_sum[...])
        back = nn(table_high, neighbour_t[...]) + nn(table_low, neighbour_t[...])
        own_back = tn(own_high, residue_t[...]) + tn(own_low, residue_t[...])
        if rows == SPAN:
            back_table[...] = (back + own_back).astype(bf16)
        else:
            own_rows = pl.ds(local_first, rows)
            back_table[...] = back.astype(bf16)
            back_table[own_rows, :] = (back_table[own_rows, :].astype(f32) + own_back).astype(bf16)
        block = states[pl.ds(local_first, rows), :]
        grad_self = nn(own_high, block) + nn(own_low, block)
        grad_near = tn(table_high, states[...]) + tn(table_low, states[...])
        grads[:width, :] = grad_self
        grads[width:, :] = grad_near
        squares[...] = jnp.zeros_like(squares)
        squares[:, :width] = grad_edge[...] + far_sum[SPAN:, :]
        squares[:, 256 : 256 + width] = 0.5 * grad_out[...]
        vectors[...] = jnp.zeros_like(vectors)
        ones = jnp.ones((16, rows), bf16)
        gain_high, gain_low = split(gain_sum[...])
        vectors[0:1, :width] = (nt(ones, own_high) + nt(ones, own_low))[:1]
        vectors[1:2, :width] = (nt(ones, gain_high) + nt(ones, gain_low))[:1]


def edge_layer(
    meta, states, ids, edges, cots, residue, neighbour, edge_weight, bias, out_weight, out_weight_t, gain, local_first
):
    group = group_of(edges.shape[0], EDGE_GROUP)
    width, rows = edges.shape[1:]
    model = states.shape[1]
    by_pair = pl.BlockSpec((group, width, rows), lambda i: (i, 0, 0))
    square = whole((width, width))
    return pl.pallas_call(
        functools.partial(edge_kernel, local_first),
        name="edge_layer",
        grid=(edges.shape[0] // group,),
        in_specs=[
            smem,
            whole(states.shape),
            whole(ids.shape),
            by_pair,
            by_pair,
            whole((width, model)),
            whole((width, model)),
            square,
            whole((width, 128)),
            square,
            square,
            whole((width, 128)),
        ],
        out_specs=[
            by_pair,
            by_pair,
            whole((SPAN, model)),
            whole((2 * width, model)),
            whole((width, model)),
            whole((8, model)),
        ],
        out_shape=[
            jax.ShapeDtypeStruct(edges.shape, bf16),
            jax.ShapeDtypeStruct(edges.shape, bf16),
            jax.ShapeDtypeStruct((SPAN, model), bf16),
            jax.ShapeDtypeStruct((2 * width, model), f32),
            jax.ShapeDtypeStruct((width, model), f32),
            jax.ShapeDtypeStruct((8, model), f32),
        ],
        scratch_shapes=[
            pltpu.VMEM((SPAN + 2 * REACH, 256), bf16),
            pltpu.VMEM((width, SPAN + width), bf16),
            pltpu.VMEM((rows // tile_of(rows), width, window_of(rows) + width), bf16),
            pltpu.VMEM((width, rows), f32),
            pltpu.VMEM((width, rows), f32),
            pltpu.VMEM((SPAN + width, width), f32),
            pltpu.VMEM((SPAN + 2 * REACH, width), f32),
            pltpu.VMEM((width, rows), f32),
            pltpu.VMEM((width, rows), f32),
            pltpu.VMEM((width, width), f32),
            pltpu.VMEM((width, width), f32),
        ],
        compiler_params=params(),
    )(
        meta,
        states,
        ids,
        edges,
        cots,
        residue.T,
        neighbour.T,
        edge_weight,
        bias,
        out_weight,
        out_weight_t,
        gain,
    )


def norm_back(unit, inv_std, gain, grad_out):
    grad_gain = jnp.sum(grad_out * unit, axis=0, keepdims=True)
    scaled = grad_out * gain
    grad_in = inv_std * (
        scaled
        - jnp.mean(scaled, -1, keepdims=True)
        - unit * jnp.mean(scaled * unit, -1, keepdims=True)
    )
    return grad_in, grad_gain


def node_backward_kernel(
    meta,
    own_cot,
    other_cot,
    mine,
    theirs,
    first,
    second,
    stats,
    ffn_input,
    act,
    slope,
    sums,
    gain_one,
    ffn_in,
    ffn_out,
    gain_two,
    out_weight,
    own_grad,
    spread,
    weights,
    message_out,
    vectors,
    sum_out,
    sum_in,
    sum_message,
):
    step = pl.program_id(0)
    chunk, model = first.shape
    hidden = act.shape[1]
    core = meta[4]
    half = own_cot.shape[0]

    @pl.when(step == 0)
    def _():
        vectors[...] = jnp.zeros_like(vectors)
        sum_out[...] = jnp.zeros_like(sum_out)
        sum_in[...] = jnp.zeros_like(sum_in)
        sum_message[...] = jnp.zeros_like(sum_message)

    if chunk > half:
        mine_first = core == 0
        lower = jnp.where(mine_first, own_cot[...], other_cot[...])
        cot = jnp.concatenate([lower, jnp.where(mine_first, other_cot[...], own_cot[...])], axis=0)
    else:
        row = step * chunk
        inside = pl.ds(pl.multiple_of(lax.rem(row, half), chunk), chunk)
        cot = jnp.where(row // half == core, own_cot[inside, :], other_cot[inside, :])
    total = cot.astype(f32) + (mine[...].astype(f32) + theirs[...].astype(f32))
    second_inv = stats[:, 2:3]
    first_inv = stats[:, 1:2]
    grad_second, gain_two_part = norm_back(second[...].astype(f32), second_inv, gain_two[...], total)
    top = grad_second.astype(bf16)
    grad_hidden = (nt(top, ffn_out[...]) * slope[...].astype(f32)).astype(bf16)
    out_columns = pl.ds(pl.multiple_of(core * (hidden // 2), 128), hidden // 2)
    in_columns = pl.ds(pl.multiple_of(core * (model // 2), 128), model // 2)
    sum_out[...] += tn(act[:, out_columns], top)
    sum_in[...] += tn(ffn_input[:, in_columns], grad_hidden)
    bias_part = jnp.sum(grad_hidden.astype(f32), axis=0, keepdims=True)
    grad_norm = grad_second + nt(grad_hidden, ffn_in[...])
    grad_first, gain_one_part = norm_back(first[...].astype(f32), first_inv, gain_one[...], grad_norm)
    store_own_rows(own_grad, grad_first, step, core)
    message_cot = (grad_first * stats[:, :1]).astype(bf16)
    spread[...] = (0.5 * nt(out_weight[...], message_cot)).astype(bf16)
    sum_message[...] += nn(sums[pl.ds(pl.multiple_of(core * (model // 2), 16), model // 2), :], message_cot)
    vectors[0:1, :] += gain_one_part
    vectors[1:2, :] += gain_two_part
    for part in range(hidden // model):
        vectors[2 + part : 3 + part, :] += bias_part[:, part * model : (part + 1) * model]

    @pl.when(step == pl.num_programs(0) - 1)
    def _():
        weights[: hidden // 2, :] = sum_out[...].astype(bf16)
        for part in range(hidden // model):
            start = hidden // 2 + part * (model // 2)
            weights[start : start + model // 2, :] = sum_in[
                :, part * model : (part + 1) * model
            ].astype(bf16)
        message_out[...] = sum_message[...]


def node_backward(
    meta,
    own_cot,
    other_cot,
    mine,
    theirs,
    first,
    second,
    stats,
    ffn_input,
    act,
    slope,
    sums,
    gain_one,
    ffn_in,
    ffn_out,
    gain_two,
    out_weight,
):
    rows, model = first.shape
    hidden = act.shape[1]
    chunk = min(rows, NODE_CHUNK)

    def by_rows(width):
        return pl.BlockSpec((chunk, width), lambda i: (i, 0))

    by_lanes = pl.BlockSpec((model, chunk), lambda i: (0, i))
    return pl.pallas_call(
        node_backward_kernel,
        name="node_backward",
        grid=(rows // chunk,),
        in_specs=[
            smem,
            whole(own_cot.shape),
            whole(other_cot.shape),
            by_rows(model),
            by_rows(model),
            by_rows(model),
            by_rows(model),
            by_rows(128),
            by_rows(model),
            by_rows(hidden),
            by_rows(hidden),
            by_lanes,
            whole((1, model)),
            whole(ffn_in.shape),
            whole(ffn_out.shape),
            whole((1, model)),
            whole(out_weight.shape),
        ],
        out_specs=[
            whole(own_cot.shape),
            by_lanes,
            whole((hidden, model)),
            whole((model // 2, model)),
            whole((8, model)),
        ],
        out_shape=[
            jax.ShapeDtypeStruct(own_cot.shape, f32),
            jax.ShapeDtypeStruct((model, rows), bf16),
            jax.ShapeDtypeStruct((hidden, model), bf16),
            jax.ShapeDtypeStruct((model // 2, model), f32),
            jax.ShapeDtypeStruct((8, model), f32),
        ],
        scratch_shapes=[
            pltpu.VMEM((hidden // 2, model), f32),
            pltpu.VMEM((model // 2, hidden), f32),
            pltpu.VMEM((model // 2, model), f32),
        ],
        compiler_params=params(),
    )(
        meta,
        own_cot,
        other_cot,
        mine,
        theirs,
        first,
        second,
        stats,
        ffn_input,
        act,
        slope,
        sums,
        gain_one[None],
        ffn_in,
        ffn_out,
        gain_two[None],
        out_weight,
    )


def message_backward_kernel(
    static_first,
    meta,
    table,
    spread,
    ids,
    edges,
    slope,
    receiver,
    neighbour,
    edge_grads,
    squares,
    message_out,
    edge_vectors,
    node_vectors,
    own_grad,
    keep,
    send,
    keep_weights,
    send_weights,
    far_sum,
    near_sum,
    own_sum,
    edge_sum,
    weights,
):
    step = pl.program_id(0)
    model, rows = spread.shape
    group, width = edges.shape[:2]
    half = keep.shape[0]
    window = window_of(rows)
    local_first = pl.multiple_of(meta[1], 128) if static_first is None else static_first

    @pl.when(step == 0)
    def _():
        for total in (far_sum, near_sum, own_sum, edge_sum):
            total[...] = jnp.zeros_like(total)

    near = [ids[pl.ds(group * step + k, 1), :] - meta[2] for k in range(group)]
    grads = [spread[...] * slope[k] for k in range(group)]
    own_sum[...] += sum(grad.astype(f32) for grad in grads)
    far_sum[...] += nt(
        beside([far_rows(near[k], edges[k]) for k in range(1, group, 2)]), beside(grads[1::2])
    )
    for tile, lanes in tiles(rows):
        first = local_first + lanes.start
        part = beside([near_rows(near[k][:, lanes], edges[k, :, lanes], first) for k in range(0, group, 2)])
        found = nt(part, beside([grad[:, lanes] for grad in grads[::2]]))
        near_sum[window_rows(local_first, rows, tile), :] += found[:window, :]
        edge_sum[...] += found[window:, :]

    @pl.when(step == pl.num_programs(0) - 1)
    def _():
        table_sum = (far_sum[:SPAN, :] + near_sum[REACH : REACH + SPAN, :]).astype(bf16)
        own_rows = own_sum[...].T
        own_low = own_rows.astype(bf16)
        nodes_t = table[...].T
        block_t = nodes_t
        if rows < SPAN:
            block_t = table[pl.ds(local_first, rows), :].T
        split_rows = keep_weights.shape[0]
        for core, start in enumerate((0, split_rows)):
            if core == 0:
                weights[:model, :] = nn(block_t, own_low)
                third = edge_sum[...] + far_sum[SPAN:, :]
            else:
                weights[start : start + model, :] = nn(nodes_t, table_sum)
                third = squares[...]
            start += model
            weights[start : start + width, :] = third
            start += width
            weights[start : start + width, :] = edge_grads[core * width : (core + 1) * width, :]
            start += width
            weights[start : start + model // 2, :] = jnp.where(meta[4] == core, message_out[...], 0.0)
            start += model // 2
            if core == 0:
                weights[start:split_rows, :] = jnp.zeros((split_rows - start, model), f32)
        weights[start : start + 8, :] = edge_vectors[...]
        weights[start + 8 : start + 16, :] = 0.5 * node_vectors[...]
        weights[start + 16 :, :] = jnp.broadcast_to(
            jnp.sum(own_rows, axis=0, keepdims=True), (2 * split_rows - start - 16, model)
        )
        mine = pl.multiple_of(meta[4] * split_rows, split_rows)
        keep_weights[...] = weights[pl.ds(mine, split_rows), :]
        send_weights[...] = weights[pl.ds(split_rows - mine, split_rows), :].astype(bf16)
        back = nt(table_sum, neighbour[...])
        own_back = nt(own_low, receiver[...])
        if rows == SPAN:
            far_sum[:SPAN, :] = back + own_back
        else:
            far_sum[:SPAN, :] = back
            far_sum[pl.ds(local_first, rows), :] += own_back
        high = meta[0]
        kept = far_sum[pl.ds(pl.multiple_of(high * half, half), half), :]
        keep[...] = kept + own_grad[...] if own_grad.shape[0] == half else kept
        send[...] = far_sum[pl.ds(pl.multiple_of((1 - high) * half, half), half), :].astype(bf16)


def message_backward(
    meta,
    table,
    spread,
    ids,
    edges,
    slope,
    receiver,
    neighbour,
    edge_grads,
    squares,
    message_out,
    edge_vectors,
    node_vectors,
    own_grad,
    local_first,
):
    group = group_of(edges.shape[0], MSG_GROUP)
    width, rows = edges.shape[1:]
    model = table.shape[1]
    square = whole((model, model))
    split_rows = -(-(model + 2 * width + model // 2 + 24) // 256) * 256
    return pl.pallas_call(
        functools.partial(message_backward_kernel, local_first),
        name="message_backward",
        grid=(edges.shape[0] // group,),
        in_specs=[
            smem,
            whole(table.shape),
            whole(spread.shape),
            whole(ids.shape),
            pl.BlockSpec((group, width, rows), lambda i: (i, 0, 0)),
            pl.BlockSpec((group, model, rows), lambda i: (i, 0, 0)),
            square,
            square,
            whole(edge_grads.shape),
            whole(squares.shape),
            whole(message_out.shape),
            whole(edge_vectors.shape),
            whole(node_vectors.shape),
            whole(own_grad.shape),
        ],
        out_specs=[
            whole((SPAN // 2, model)),
            whole((SPAN // 2, model)),
            whole((split_rows, model)),
            whole((split_rows, model)),
        ],
        out_shape=[
            jax.ShapeDtypeStruct((SPAN // 2, model), f32),
            jax.ShapeDtypeStruct((SPAN // 2, model), bf16),
            jax.ShapeDtypeStruct((split_rows, model), f32),
            jax.ShapeDtypeStruct((split_rows, model), bf16),
        ],
        scratch_shapes=[
            pltpu.VMEM((SPAN + width, model), f32),
            pltpu.VMEM((SPAN + 2 * REACH, model), f32),
            pltpu.VMEM((model, rows), f32),
            pltpu.VMEM((width, model), f32),
            pltpu.VMEM((2 * split_rows, model), f32),
        ],
        compiler_params=params(),
    )(
        meta,
        table,
        spread,
        ids,
        edges,
        slope,
        receiver,
        neighbour,
        edge_grads,
        squares,
        message_out,
        edge_vectors,
        node_vectors,
        own_grad,
    )


def edge_gradient_kernel(partial, slope, spread, edge_weight, *rest):
    out = rest[-1]
    for k in range(out.shape[0]):
        grad_value = spread[...] * slope[k]
        out[k] = partial[k].astype(f32) + nn(edge_weight[...], grad_value)


def edge_gradient(first, count, filled, partial, slope, spread, edge_weight):
    width, rows = partial.shape[1:]
    model = spread.shape[0]

    def pair(size):
        return pl.BlockSpec((2, size, rows), lambda i: (first + i, 0, 0))

    before = [] if filled is None else [filled]
    return pl.pallas_call(
        edge_gradient_kernel,
        name="edge_gradient",
        grid=(count,),
        in_specs=[pair(width), pair(model), whole(spread.shape), whole(edge_weight.shape)]
        + [pl.BlockSpec(memory_space=pl.ANY)] * len(before),
        out_specs=pair(width),
        out_shape=jax.ShapeDtypeStruct(partial.shape, f32),
        input_output_aliases={4: 0} if before else {},
        compiler_params=params(54),
    )(partial, slope, spread, edge_weight, *before)


def sum_to_slots_kernel(shift, meta, *refs):
    parts, outs, total = refs[:-5], refs[-5:-1], refs[-1]
    total[...] = parts[0][...].astype(f32)
    for part in parts[1:]:
        total[...] += part[...].astype(f32)
    place = meta[5] >> shift & 3
    rows = outs[0].shape[0]
    for slot, out in enumerate(outs):
        start = pl.multiple_of((place ^ slot) * rows, rows)
        out[...] = total[pl.ds(start, rows), :].astype(out.dtype)


def sum_to_slots(meta, shift, parts):
    rows, width = parts[0].shape
    out_types = (f32, bf16, bf16, bf16)
    return pl.pallas_call(
        functools.partial(sum_to_slots_kernel, shift),
        name="sum_to_slots",
        in_specs=[smem] + [whole(part.shape) for part in parts],
        out_specs=[whole((rows // 4, width))] * 4,
        out_shape=[jax.ShapeDtypeStruct((rows // 4, width), kind) for kind in out_types],
        scratch_shapes=[pltpu.VMEM((rows, width), f32)],
        compiler_params=params(12),
    )(meta, *parts)


def sum_parts_kernel(*refs):
    total = refs[0][...].astype(f32)
    for part in refs[1:-1]:
        total = total + part[...].astype(f32)
    refs[-1][...] = total.astype(bf16)


def sum_parts(parts):
    return pl.pallas_call(
        sum_parts_kernel,
        name="sum_parts",
        in_specs=[whole(part.shape) for part in parts],
        out_specs=whole(parts[0].shape),
        out_shape=jax.ShapeDtypeStruct(parts[0].shape, bf16),
        compiler_params=params(12),
    )(*parts)


def assemble_kernel(shift, meta, *refs):
    place = meta[5] >> shift & 3
    rows = refs[0].shape[0]
    for slot, part in enumerate(refs[:-1]):
        start = pl.multiple_of((place ^ slot) * rows, rows)
        refs[-1][pl.ds(start, rows), :] = part[...]


def assemble(meta, shift, parts):
    rows, width = parts[0].shape
    return pl.pallas_call(
        functools.partial(assemble_kernel, shift),
        name="assemble",
        in_specs=[smem] + [whole(part.shape) for part in parts],
        out_specs=whole((4 * rows, width)),
        out_shape=jax.ShapeDtypeStruct((4 * rows, width), bf16),
        compiler_params=params(12),
    )(meta, *parts)


def sent_each_way(shift, slots):
    return [moved(slot, place << shift) for place, slot in enumerate(slots) if place > 0]


def moved(value, mask):
    devices = lax.axis_size("res") * lax.axis_size("nbr")
    cores = lax.axis_size("nbr")
    pairs = [(source, source ^ (mask * cores)) for source in range(devices)]
    return lax.ppermute(value, ("res", "nbr"), pairs)


def unpack_early_kernel(side, meta, source, *rest):
    grad_out, grad_in, wide, out_sem, in_sem = rest[-5:]
    place = meta[4] if side == 0 else 1 - meta[4]
    model, hidden = grad_in.shape
    wide[...] = source[...].astype(f32)
    half, quarter = hidden // 2, model // 2
    copies = [
        pltpu.make_async_copy(
            wide.at[:half], grad_out.at[pl.ds(pl.multiple_of(place * half, half), half)], out_sem
        )
    ]
    for part in range(hidden // model):
        start = half + part * quarter
        copies.append(
            pltpu.make_async_copy(
                wide.at[start : start + quarter],
                grad_in.at[
                    pl.ds(pl.multiple_of(place * quarter, quarter), quarter),
                    part * model : (part + 1) * model,
                ],
                in_sem.at[part],
            )
        )
    for copy in copies:
        copy.start()
    for copy in copies:
        copy.wait()


def unpack_early(meta, side, source, before):
    rows, model = source.shape
    anywhere = pl.BlockSpec(memory_space=pl.ANY)
    return pl.pallas_call(
        functools.partial(unpack_early_kernel, side),
        name="unpack_early",
        in_specs=[smem, whole(source.shape)] + [anywhere] * len(before),
        out_specs=[anywhere, anywhere],
        out_shape=[
            jax.ShapeDtypeStruct((rows, model), f32),
            jax.ShapeDtypeStruct((model, rows), f32),
        ],
        scratch_shapes=[
            pltpu.VMEM((rows, model), f32),
            pltpu.SemaphoreType.DMA,
            pltpu.SemaphoreType.DMA((rows // model,)),
        ],
        input_output_aliases={2: 0, 3: 1} if before else {},
        compiler_params=params(),
    )(meta, source, *before)


def unpack_late_kernel(
    meta, own, other, grad_self, grad_near, grad_edge, edge_edge, edge_out, edge_self, edge_near, message_out, *vectors
):
    lower = meta[4] == 0
    model = own.shape[1]
    width = edge_edge.shape[0]
    first = jnp.where(lower, own[...], other[...]).astype(f32)
    second = jnp.where(lower, other[...], own[...]).astype(f32)
    grad_self[...] = first[:model, :]
    grad_near[...] = second[:model, :]
    start = model + width
    grad_edge[...] = first[model:start, :]
    edge_edge[...] = second[model:start, :width]
    edge_out[...] = second[model:start, 256 : 256 + width]
    edge_self[...] = first[start : start + width, :]
    edge_near[...] = second[start : start + width, :]
    start += width
    half = model // 2
    message_out[:half, :] = first[start : start + half, :]
    message_out[half:, :] = second[start : start + half, :]
    start += half
    edge_bias, gain_three, gain_one, gain_two, message_bias, ffn_bias = vectors
    edge_bias[...] = second[start : start + 1, :width]
    gain_three[...] = second[start + 1 : start + 2, :width]
    gain_one[...] = second[start + 8 : start + 9, :]
    gain_two[...] = second[start + 9 : start + 10, :]
    message_bias[...] = second[start + 16 : start + 17, :]
    for part in range(ffn_bias.shape[1] // model):
        row = start + 10 + part
        ffn_bias[:, part * model : (part + 1) * model] = second[row : row + 1, :]


def unpack_late(meta, own, other, width, hidden):
    model = own.shape[1]
    shapes = [(model, model)] * 2 + [(width, model)] + [(width, width)] * 2 + [(width, model)] * 2
    shapes += [(model, model)] + [(1, size) for size in (width, width, model, model, model, hidden)]
    return pl.pallas_call(
        unpack_late_kernel,
        name="unpack_late",
        in_specs=[smem, whole(own.shape), whole(other.shape)],
        out_specs=[whole(shape) for shape in shapes],
        out_shape=[jax.ShapeDtypeStruct(shape, f32) for shape in shapes],
        compiler_params=params(),
    )(meta, own, other)


def planes(size):
    return [[4 * block + place for place in range(4)] for block in range(size // 4)]


def columns(size):
    return [[4 * block + place for block in range(size // 4)] for place in range(4)]


def tied(*arrays):
    return lax.optimization_barrier(arrays)


def weight_sums(meta, early, kept, sent, kept_nodes, nodes, size, pieces):
    received = swapped(sent, 0)
    early = lax.psum(early, "res", axis_index_groups=columns(size))
    value, received, given = tied(pieces[0](None), received, swapped(nodes, 0))
    node_grad = kept_nodes + given.astype(f32)
    value, kept, *slots = tied(value, *sum_to_slots(meta, 0, [kept, received]))
    value, node_grad, *received = tied(pieces[1](value), node_grad, *sent_each_way(0, [kept, *slots]))
    value, kept, *slots = tied(value, *sum_to_slots(meta, 2, [kept, *received]))
    value, *received = tied(pieces[2](value), *sent_each_way(2, [kept, *slots]))
    value, early, late = tied(value, early, sum_parts([kept, *received]))
    early = lax.all_gather(early, "res", axis_index_groups=planes(size), tiled=True)
    value, *received = tied(pieces[3](value), *sent_each_way(2, [late] * 4))
    value, late = tied(value, assemble(meta, 2, [late, *received]))
    value, early, *received = tied(pieces[4](value), early, *sent_each_way(0, [late] * 4))
    return early, assemble(meta, 0, [late, *received]), value, node_grad


def joined(table, other, high_side):
    return jnp.where(
        high_side, jnp.concatenate([other, table], axis=0), jnp.concatenate([table, other], axis=0)
    )


def halves(table, high_side):
    half = table.shape[0] // 2
    lower, upper = (table[:half], table[half:])
    return (jnp.where(high_side, upper, lower), jnp.where(high_side, lower, upper))


def sum_blocks(table, device, level):
    keep, send = halves(table, device >> level & 1 == 1)
    return keep + swapped(send.astype(bf16), level).astype(keep.dtype)


def on_device(
    nodes,
    edges,
    neighbours,
    lengths,
    message_receiver_weight,
    message_neighbour_weight,
    message_edge_weight,
    message_hidden_bias,
    message_output_weight,
    gain_one,
    ffn_in,
    ffn_bias,
    ffn_out,
    gain_two,
    edge_update_residue_weight,
    edge_update_neighbour_weight,
    edge_update_edge_weight,
    edge_update_bias,
    edge_out,
    gain_three,
    node_cot,
    edge_cot,
):
    rows, half_k, edge_width = edges.shape
    own_rows, model = nodes.shape
    hidden = ffn_in.shape[1]
    levels = (SPAN // own_rows).bit_length() - 1
    core = lax.axis_index("nbr")
    device = lax.axis_index("res") * lax.axis_size("nbr") + core
    first_row = lax.axis_index("res") * rows
    bucket = first_row // SPAN
    group_start = bucket * SPAN
    local_first = 0 if rows == SPAN else None
    top = device >> (levels - 1) & 1
    meta = jnp.stack(
        [top, first_row - group_start, group_start, bucket, core, lax.axis_index("res"), 0, 0]
    ).astype(jnp.int32)

    ids = neighbours.T
    edges_t = edges.transpose(1, 2, 0)
    cot_t = edge_cot.transpose(1, 2, 0)

    table = nodes
    for level in range(levels - 1):
        table = joined(table, swapped(table, level), device >> level & 1 == 1)
    other_table = swapped(table, levels - 1)
    other_cot = swapped(node_cot, 0)

    node_table, slope, packed = message_forward(
        meta,
        lengths,
        table,
        other_table,
        ids,
        edges_t,
        message_receiver_weight,
        message_neighbour_weight,
        message_edge_weight,
        message_hidden_bias,
        local_first,
    )
    packed, *edge_parts = tied(
        packed,
        jnp.broadcast_to(edge_update_bias[:, None], (edge_width, 128)),
        edge_out * 0.5,
        edge_out.T * 0.5,
        jnp.broadcast_to(gain_three[:, None], (edge_width, 128)),
    )
    block = node_table
    if rows < SPAN:
        block = lax.dynamic_slice_in_dim(node_table, first_row - group_start, rows, 0)
    state, ffn_input, act, ffn_slope, first, second, stats, sums, node_out = node_forward(
        meta,
        block,
        packed,
        swapped(packed, 0),
        message_output_weight,
        gain_one,
        ffn_in,
        ffn_bias,
        ffn_out,
        gain_two,
    )
    states = state
    for level in range(1, levels):
        states = joined(states, swapped(states, level), device >> level & 1 == 1)
    new_edges, partial, back, edge_grads, squares, edge_vectors = edge_layer(
        meta,
        states,
        ids,
        edges_t,
        cot_t,
        edge_update_residue_weight,
        edge_update_neighbour_weight,
        edge_update_edge_weight,
        *edge_parts,
        local_first,
    )
    for level in reversed(range(1, levels)):
        back = sum_blocks(back, device, level)
    own_grad, spread, early, message_out, node_vectors = node_backward(
        meta,
        node_cot,
        other_cot,
        back,
        swapped(back, 0),
        first,
        second,
        stats,
        ffn_input,
        act,
        ffn_slope,
        sums,
        gain_one,
        ffn_in,
        ffn_out,
        gain_two,
        message_output_weight,
    )
    size = lax.axis_size("res")
    if size == 16:
        early = lax.psum_scatter(early, "res", axis_index_groups=planes(size), tiled=True)
    else:
        early = lax.psum(early.astype(f32), "res").astype(bf16)
    keep, send, kept_weights, sent_weights = message_backward(
        meta,
        node_table,
        spread,
        ids,
        edges_t,
        slope,
        message_receiver_weight,
        message_neighbour_weight,
        edge_grads,
        squares,
        message_out,
        edge_vectors,
        node_vectors,
        own_grad,
        local_first,
    )
    early, kept_weights, sent_weights = tied(early, kept_weights, sent_weights)
    counts = [1, 6, 1, 1, 6] if half_k == 30 else [half_k // 2]
    starts = [sum(counts[:index]) for index in range(len(counts))]

    def piece(start, count):
        return lambda filled: edge_gradient(
            start, count, filled, partial, slope, spread, message_edge_weight
        )

    spans = [piece(*span) for span in zip(starts, counts)]
    if size == 16:
        early, late, edge_grad, node_grad = weight_sums(
            meta, early, kept_weights, sent_weights, keep, send, size, spans
        )
    else:
        late = lax.psum(kept_weights + swapped(sent_weights, 0).astype(f32), "res").astype(bf16)
        edge_grad = None
        for span in spans:
            edge_grad = span(edge_grad)
        node_grad = keep + swapped(send, levels - 1).astype(f32)
        for level in reversed(range(levels - 1)):
            node_grad = sum_blocks(node_grad, device, level)
        if levels > 1:
            node_grad = own_grad + node_grad
    late_other = swapped(late, 0)
    early_other = swapped(early, 0)
    late_other, *halves_out = tied(late_other, *unpack_early(meta, 0, early, []))
    (
        grad_msg_self,
        grad_msg_nbr,
        grad_msg_edge,
        grad_edge_edge,
        grad_edge_out,
        grad_edge_self,
        grad_edge_nbr,
        grad_msg_out,
        grad_edge_bias,
        grad_gain_three,
        grad_gain_one,
        grad_gain_two,
        grad_msg_bias,
        grad_ffn_bias,
    ) = unpack_late(meta, late, late_other, edge_width, hidden)
    grad_msg_out, early_other = tied(grad_msg_out, early_other)
    grad_ffn_out, grad_ffn_in = unpack_early(meta, 1, early_other, halves_out)
    return (
        node_out,
        new_edges.transpose(2, 0, 1),
        node_grad,
        edge_grad.transpose(2, 0, 1),
        grad_msg_self,
        grad_msg_nbr,
        grad_msg_edge,
        grad_msg_bias[0],
        grad_msg_out,
        grad_gain_one[0],
        grad_ffn_in,
        grad_ffn_bias[0],
        grad_ffn_out,
        grad_gain_two[0],
        grad_edge_self.T,
        grad_edge_nbr.T,
        grad_edge_edge,
        grad_edge_bias[0],
        grad_edge_out,
        grad_gain_three[0],
    )


def solution(mesh):
    rows = P(("res", "nbr"), None)
    pairs = P("res", "nbr", None)
    placed = (rows, pairs, P("res", "nbr")) + (P(),) * 17 + (rows, pairs)
    return jax.shard_map(
        on_device,
        mesh=mesh,
        in_specs=placed,
        out_specs=(rows, pairs, rows, pairs) + (P(),) * 16,
        check_vma=False,
    )
```

time: 358 us -> 339 us (0.947); the launches traced: 357 us -> 333 us
  Pallas kernels: 276 us -> 252 us
  waiting for transfers between devices: 25.7 us -> 38.3 us
  local copies, waits for them, and re-layouts: 17.6 us -> 7.81 us
    pallas_call x5, Pallas kernels: 42.9 us -> 35.8 us  [edge_gradient(): pl.pallas_call(edge_gradient_kernel, name='edge_gradient', grid=(count,),...]
    pallas_call x1, Pallas kernels: 80.5 us -> 73.5 us  [edge_layer(): pl.pallas_call(functools.partial(edge_kernel, local_first), name='edge_la...]
    psum x1, waiting for transfers between devices: 0.01 us -> 6.38 us  [weight_sums(): early = lax.psum(early, 'res', axis_index_groups=columns(size))]
    ppermute x12, waiting for transfers between devices: 9.51 us -> 15.9 us  [moved(): return lax.ppermute(value, ('res', 'nbr'), pairs)]
    unnamed x43 -> x25, local copies, waits for them, and re-layouts: 10.6 us -> 4.98 us
    pallas_call x1, Pallas kernels: 46.5 us -> 41.1 us  [message_backward(): pl.pallas_call(functools.partial(message_backward_kernel, local_first), n...]
    pallas_call x1 -> x2, Pallas kernels: 6.47 us -> 7.83 us  [unpack_early(): pl.pallas_call(functools.partial(unpack_early_kernel, side), name='unpack...]
  transfers between devices with their start and end apart: 23 -> 23, of which waited for: 7 -> 11; matrix products, arithmetic and copies ran while one was open for 3% -> 1% of each run, Pallas kernels for 29% -> 26%
where the time goes in v3:
time: 339 us; the launch traced here: 333 us
  Pallas kernels  252 us (74%)
  waiting for transfers between devices  38.3 us (11%)
  starting transfers between devices  19.1 us (6%)
  between operations  14.4 us (4%)
  local copies, waits for them, and re-layouts  7.81 us (2%)
    pallas_call x1, Pallas kernels, edge_layer(): pl.pallas_call(functools.partial(edge_kernel, local_first), name='edge_la...  73.5 us
    pallas_call x1, Pallas kernels, message_forward(): pl.pallas_call(functools.partial(message_forward_kernel, local_first), na...  52.1 us
    pallas_call x1, Pallas kernels, message_backward(): pl.pallas_call(functools.partial(message_backward_kernel, local_first), n...  41.1 us
    pallas_call x5, Pallas kernels, edge_gradient(): pl.pallas_call(edge_gradient_kernel, name='edge_gradient', grid=(count,),...  35.8 us
    pallas_call x1, Pallas kernels, node_backward(): pl.pallas_call(node_backward_kernel, name='node_backward', grid=(rows //...  18.2 us
    ppermute x12, starting transfers between devices, moved(): return lax.ppermute(value, ('res', 'nbr'), pairs)  16.5 us
    pallas_call x1, Pallas kernels, node_forward(): pl.pallas_call(node_forward_kernel, name='node_forward', grid=(rows // ch...  15.9 us
    ppermute x12, waiting for transfers between devices, moved(): return lax.ppermute(value, ('res', 'nbr'), pairs)  15.9 us
  transfers between devices with their start and end apart: 23, of which 11 were waited for; matrix products, arithmetic and copies ran while one was open for 1% of the time, Pallas kernels for 26%

profile of v3, /device:TPU:0, one launch (start us, length us, event | category | flops | bytes accessed | tf_op | source)
XLA Modules:
  0.0 333.2 jit_solution(8111788203136900690)
XLA Ops:
  7.2 0.0 reduce-scatter.2.cloned.1.call-start
  7.2 0.5 collective-permute-start
  7.8 1.0 copy.48
  8.8 0.6 stack.27.meta
  9.4 0.7 fusion
  10.0 0.8 copy-done.9
  10.8 52.1 %message_forward.1 = (bf16[1024,512]{1,0:T(8,128)(2,1)}, bf16[30,512,1024]{2,1,0:T(8,128)(2,1)}, bf16[528,1024]{1,0:T(8,128)(2,1)}) custom-call(s32[8]{0:T(128)} %stack.27.meta, s32[16]{0:T(128)} %lengths.1, bf16[512,512]{1,0:T(8,128)(2,1)} %own.1, bf16[512,512]{1,0:T(8,128)(2,1)} %copy-done.9, s32[30,1024]{1,0:T(8,128)} %bitcast.32, ...), custom_call_target="tpu_custom_call" | custom-call | tf_op jit(solution)/shard_map/message_forward/pallas_call | solution.py:196
  63.0 0.7 broadcast_in_dim.13.bias
  63.7 0.7 broadcast_in_dim.28.gain
  64.4 0.1 collective-permute-start.1
  64.5 0.7 copy.49.out_weight
  65.2 2.1 collective-permute-done.1.theirs
  67.4 1.0 copy-done.4
  68.3 15.9 %node_forward.1 = (bf16[1024,512]{1,0:T(8,128)(2,1)}, bf16[1024,512]{1,0:T(8,128)(2,1)}, bf16[1024,2048]{1,0:T(8,128)(2,1)}, bf16[1024,2048]{1,0:T(8,128)(2,1)},...) custom-call(s32[8]{0:T(128)} %stack.27.meta, ...), custom_call_target="tpu_custom_call" | custom-call | tf_op jit(solution)/shard_map/node_forward/pallas_call | solution.py:309
  84.3 73.5 %edge_layer.1 = (bf16[30,192,1024]{2,1,0:T(8,128)(2,1)}, bf16[30,192,1024]{2,1,0:T(8,128)(2,1)}, bf16[1024,512]{1,0:T(8,128)(2,1)}, f32[384,512]{1,0:T(8,128)}, f32[192,512]{1,0:T(8,128)}, /*index=5*/f32[8,512]{1,0:T(8,128)}) custom-call(s32[8]{0:T(128)} %stack.27.meta, bf16[1024,512]{1,0:T(8,128)(2,1)} %get-tuple-element.126.states, s32[30,1024]{1,0:T(8,128)} %bitcast.33, ...), custom_call_target="tpu_custom_call" | custom-call | tf_op jit(solution)/shard_map/edge_layer/pallas_call | solution.py:495
  157.8 0.2 collective-permute-start.3
  158.0 0.4 collective-permute-start.2
  158.4 2.9 collective-permute-done.2.other_cot
  161.3 0.8 copy-done.8
  162.1 0.3 copy-done.5
  162.4 18.2 %node_backward.1 = (f32[512,512]{1,0:T(8,128)}, bf16[512,1024]{1,0:T(8,128)(2,1)}, bf16[2048,512]{1,0:T(8,128)(2,1)}, f32[256,512]{1,0:T(8,128)}, f32[8,512]{1,0:T(8,128)}) custom-call(s32[8]{0:T(128)} %stack.27.meta, bf16[512,512]{1,0:T(8,128)(2,1)} %own_cot.1, bf16[512,512]{1,0:T(8,128)(2,1)} %copy-done.8, bf16[1024,512]{1,0:T(8,128)(2,1)} %get-tuple-element.134.mine, ...), custom_call_target="tpu_custom_call" | custom-call | tf_op jit(solution)/shard_map/node_backward/pallas_call | solution.py:678
  180.6 0.0 reduce-scatter.2.cloned.1.call-update
  180.6 0.0 all-reduce.2.cloned.1.call-start
  180.7 41.1 %message_backward.1 = (f32[512,512]{1,0:T(8,128)}, bf16[512,512]{1,0:T(8,128)(2,1)}, f32[1280,512]{1,0:T(8,128)}, bf16[1280,512]{1,0:T(8,128)(2,1)}) custom-call(s32[8]{0:T(128)} %stack.27.meta, bf16[1024,512]{1,0:T(8,128)(2,1)} %get-tuple-element.122.nodes.table, bf16[512,1024]{1,0:T(8,128)(2,1)} %get-tuple-element.142.spread, s32[30,1024]{1,0:T(8,128)} %bitcast.34, ...), custom_call_target="tpu_custom_call" | custom-call | tf_op jit(solution)/shard_map/message_backward/pallas_call | solution.py:862
  221.8 0.2 collective-permute-start.4
  222.0 0.4 collective-permute-start.5
  222.4 0.3 all-gather.2.cloned.1.call-start
  222.7 4.0 %edge_gradient.5.rest_0_ = f32[30,192,1024]{2,1,0:T(8,128)} custom-call(bf16[30,192,1024]{2,1,0:T(8,128)(2,1)} %get-tuple-element.132.partial, bf16[30,512,1024]{2,1,0:T(8,128)(2,1)} %get-tuple-element.133.slope, bf16[512,1024]{1,0:T(8,128)(2,1)} %get-tuple-element.142.spread, bf16[192,512]{1,0:T(8,128)(2,1)} %edge_weight.13), custom_call_target="tpu_custom_call" | custom-call | tf_op jit(solution)/shard_map/edge_gradient/pallas_call | solution.py:935
  226.7 1.3 sum_to_slots.2
  228.0 2.7 collective-permute-start.6
  230.7 1.5 collective-permute-start.7
  232.2 0.0 collective-permute-start.8
  232.3 12.1 %edge_gradient.6.rest_0_ = f32[30,192,1024]{2,1,0:T(8,128)} custom-call(bf16[30,192,1024]{2,1,0:T(8,128)(2,1)} %get-tuple-element.132.partial, bf16[30,512,1024]{2,1,0:T(8,128)(2,1)} %get-tuple-element.133.slope, bf16[512,1024]{1,0:T(8,128)(2,1)} %get-tuple-element.142.spread, bf16[192,512]{1,0:T(8,128)(2,1)} %edge_weight.13, ...), custom_call_target="tpu_custom_call", output_to_operand_aliasing={{}: (4, {})} | custom-call | tf_op jit(solution)/shard_map/edge_gradient/pallas_call | solution.py:935
  244.3 1.1 convert_add_fusion
  245.5 2.0 collective-permute-done.7.refs_2_
  247.4 0.8 sum_to_slots.3
  248.2 2.6 collective-permute-start.10
  250.9 1.3 collective-permute-start.11
  252.2 0.2 collective-permute-start.9
  252.5 3.9 %edge_gradient.7.rest_0_ = f32[30,192,1024]{2,1,0:T(8,128)} custom-call(bf16[30,192,1024]{2,1,0:T(8,128)(2,1)} %get-tuple-element.132.partial, bf16[30,512,1024]{2,1,0:T(8,128)(2,1)} %get-tuple-element.133.slope, bf16[512,1024]{1,0:T(8,128)(2,1)} %get-tuple-element.142.spread, bf16[192,512]{1,0:T(8,128)(2,1)} %edge_weight.13, ...), custom_call_target="tpu_custom_call", output_to_operand_aliasing={{}: (4, {})} | custom-call | tf_op jit(solution)/shard_map/edge_gradient/pallas_call | solution.py:935
  256.3 3.8 %collective-permute-done.10.refs_2_ = bf16[80,512]{1,0:T(8,128)(2,1)S(1)} collective-permute-done((bf16[80,512]{1,0:T(8,128)(2,1)S(1)}, bf16[80,512]{1,0:T(8,128)(2,1)S(1)}, u32[]{:S(2)}, u32[]{:S(2)}) %collective-permute-start.10) | collective-permute-done | bytes 81952 | tf_op jit(solution)/shard_map/ppermute | solution.py:1020
  260.1 0.1 collective-permute-done.11.refs_3_
  260.2 1.2 collective-permute-done.9.refs_1_
  261.4 6.4 %all-reduce.2.cloned.1.call-done = bf16[512,512]{1,0:T(8,128)(2,1)} async-done(((bf16[512,512]{1,0:T(8,128)(2,1)}), bf16[512,512]{1,0:T(8,128)(2,1)}) %all-reduce.2.cloned.1.call-update) | async-done | bytes 524304 | tf_op jit(solution)/shard_map/psum | solution.py:1134
  267.8 1.2 collective-permute-start.12
  269.0 1.8 collective-permute-start.13
  270.8 1.5 collective-permute-start.14
  272.3 3.8 %edge_gradient.8.rest_0_ = f32[30,192,1024]{2,1,0:T(8,128)} custom-call(bf16[30,192,1024]{2,1,0:T(8,128)(2,1)} %get-tuple-element.132.partial, bf16[30,512,1024]{2,1,0:T(8,128)(2,1)} %get-tuple-element.133.slope, bf16[512,1024]{1,0:T(8,128)(2,1)} %get-tuple-element.142.spread, bf16[192,512]{1,0:T(8,128)(2,1)} %edge_weight.13, ...), custom_call_target="tpu_custom_call", output_to_operand_aliasing={{}: (4, {})} | custom-call | tf_op jit(solution)/shard_map/edge_gradient/pallas_call | solution.py:935
  276.1 1.5 collective-permute-done.13.refs_2_
  277.6 0.6 assemble.2.refs_0_
  278.2 1.7 collective-permute-start.15
  279.9 0.7 collective-permute-start.16
  280.5 1.2 collective-permute-start.17
  281.7 12.0 %edge_gradient.9 = f32[30,192,1024]{2,1,0:T(8,128)} custom-call(bf16[30,192,1024]{2,1,0:T(8,128)(2,1)} %get-tuple-element.132.partial, bf16[30,512,1024]{2,1,0:T(8,128)(2,1)} %get-tuple-element.133.slope, bf16[512,1024]{1,0:T(8,128)(2,1)} %get-tuple-element.142.spread, bf16[192,512]{1,0:T(8,128)(2,1)} %edge_weight.13, ...), custom_call_target="tpu_custom_call", output_to_operand_aliasing={{}: (4, {})} | custom-call | tf_op jit(solution)/shard_map/edge_gradient/pallas_call | solution.py:935
  293.8 7.4 %collective-permute-done.17.refs_3_ = bf16[320,512]{1,0:T(8,128)(2,1)S(1)} collective-permute-done((bf16[320,512]{1,0:T(8,128)(2,1)S(1)}, bf16[320,512]{1,0:T(8,128)(2,1)S(1)}, u32[]{:S(2)}, u32[]{:S(2)}) %collective-permute-start.17) | collective-permute-done | bytes 327712 | tf_op jit(solution)/shard_map/ppermute | solution.py:1020
  301.1 10.1 %all-gather.2.cloned.1.call-done.source = bf16[2048,512]{1,0:T(8,128)(2,1)} async-done(((bf16[512,512]{1,0:T(8,128)(2,1)}), bf16[2048,512]{1,0:T(8,128)(2,1)}) %all-gather.2.cloned.1.call-update) | async-done | bytes 2097168 | tf_op jit(solution)/shard_map/all_gather | solution.py:1142
  311.2 0.1 collective-permute-start.19
  311.3 0.6 assemble.3.own
  311.9 0.5 collective-permute-start.18
  312.4 3.9 %unpack_early.2 = (f32[2048,512]{1,0:T(8,128)}, f32[512,2048]{1,0:T(8,128)}) custom-call(s32[8]{0:T(128)} %stack.27.meta, bf16[2048,512]{1,0:T(8,128)(2,1)} %all-gather.2.cloned.1.call-done.source), custom_call_target="tpu_custom_call" | custom-call | tf_op jit(solution)/shard_map/unpack_early/pallas_call | solution.py:1055
  316.3 0.9 collective-permute-done.18.other
  317.2 1.0 copy-done.3
  318.3 4.0 %unpack_late.1 = (f32[512,512]{1,0:T(8,128)}, f32[512,512]{1,0:T(8,128)}, f32[192,512]{1,0:T(8,128)}, f32[192,192]{1,0:T(8,128)}, f32[192,192]{1,0:T(8,128)}, /*...) custom-call(s32[8]{0:T(128)} %stack.27.meta, ...), custom_call_target="tpu_custom_call" | custom-call | tf_op jit(solution)/shard_map/unpack_late/pallas_call | solution.py:1110
  322.3 3.9 %unpack_early.3 = (f32[2048,512]{1,0:T(8,128)}, f32[512,2048]{1,0:T(8,128)}) custom-call(s32[8]{0:T(128)} %stack.27.meta, bf16[2048,512]{1,0:T(8,128)(2,1)} %collective-permute-done.19.source, f32[2048,512]{1,0:T(8,128)} %get-tuple-element.212.rest_0_, f32[512,2048]{1,0:T(8,128)} %get-tuple-element.213.rest_1_), custom_call_target="tpu_custom_call", output_to_operand_aliasing={{0}: (2, {}), {1}: (3, {})} | custom-call | tf_op jit(solution)/shard_map/unpack_early/pallas_call | solution.py:1055
  (35 shorter events, 0.2 us)
Async XLA Ops:
  7.2 214.6 %reduce-scatter.2.cloned.1.call-start = ((), (), s32[]{:S(2)}) async-start(), calls=%async_computation.1 | async-start | bytes 2621440 | tf_op jit(solution)/shard_map/reduce_scatter | solution.py:1288
  7.2 2.8 collective-permute-start
  10.0 0.8 copy-start.9
  10.8 52.1 %copy-start.10 = (f32[192]{0:T(256)S(1)}, f32[192]{0:T(256)}, u32[]{:S(2)}) copy-start(f32[192]{0:T(256)} %param.39) | copy-start | bytes 2308
  10.8 52.9 %copy-start.11 = (f32[192]{0:T(256)S(1)}, f32[192]{0:T(256)}, u32[]{:S(2)}) copy-start(f32[192]{0:T(256)} %param.41) | copy-start | bytes 2308
  64.4 2.9 collective-permute-start.1
  67.4 1.0 copy-start.4
  84.3 73.7 %copy-start.7 = (bf16[512,512]{1,0:T(8,128)(2,1)S(1)}, bf16[512,512]{1,0:T(8,128)(2,1)}, u32[]{:S(2)}) copy-start(bf16[512,512]{1,0:T(8,128)(2,1)} %own_cot.1) | copy-start | bytes 1572868
  157.8 3.5 %collective-permute-start.3 = (bf16[1024,512]{1,0:T(8,128)(2,1)}, bf16[1024,512]{1,0:T(8,128)(2,1)S(1)}, u32[]{:S(2)}, u32[]{:S(2)}) collective-permute-start(bf16[1024,512]{1,0:T(8,128)(2,1)} %get-tuple-element.134.mine), channel_id=1, source_target_pairs={{0,1},{1,0},{2,3},{3,2},{4,5},{5,4},{6,7},{7,6},{8,9},{9,8},{10,11... | collective-permute-start | bytes 3145736 | tf_op jit(solution)/shard_map/ppermute | solution.py:31
  158.0 3.3 collective-permute-start.2
  161.3 0.8 copy-start.8
  161.3 1.1 copy-start.5
  180.6 87.2 %all-reduce.2.cloned.1.call-start = ((), (), s32[]{:S(2)}) async-start(), calls=%async_computation.2 | async-start | bytes 1048576 | tf_op jit(solution)/shard_map/psum | solution.py:1134
  221.8 4.9 %collective-permute-start.4 = (bf16[1280,512]{1,0:T(8,128)(2,1)}, bf16[1280,512]{1,0:T(8,128)(2,1)S(1)}, u32[]{:S(2)}, u32[]{:S(2)}) collective-permute-start(bf16[1280,512]{1,0:T(8,128)(2,1)} %get-tuple-element.152), channel_id=1, source_target_pairs={{0,1},{1,0},{2,3},{3,2},{4,5},{5,4},{6,7},{7,6},{8,9},{9,8},{10,11... | collective-permute-start | bytes 3932168 | tf_op jit(solution)/shard_map/ppermute | solution.py:31
  222.0 4.7 %collective-permute-start.5 = (bf16[512,512]{1,0:T(8,128)(2,1)}, bf16[512,512]{1,0:T(8,128)(2,1)S(1)}, u32[]{:S(2)}, u32[]{:S(2)}) collective-permute-start(bf16[512,512]{1,0:T(8,128)(2,1)} %get-tuple-element.153), channel_id=1, source_target_pairs={{0,1},{1,0},{2,3},{3,2},{4,5},{5,4},{6,7},{7,6},{8,9},{9,8},{10,11... | collective-permute-start | bytes 1572872 | tf_op jit(solution)/shard_map/ppermute | solution.py:31
  222.4 88.8 %all-gather.2.cloned.1.call-start = ((), (), s32[]{:S(2)}) async-start(), calls=%async_computation.3 | async-start | bytes 2621440 | tf_op jit(solution)/shard_map/all_gather | solution.py:1142
  222.7 4.0 %copy-start.1 = (f32[1280,512]{1,0:T(8,128)S(1)}, f32[1280,512]{1,0:T(8,128)}, u32[]{:S(2)}) copy-start(f32[1280,512]{1,0:T(8,128)} %get-tuple-element.155.refs_0_) | copy-start | bytes 7864324
  222.7 4.0 %copy-start.2 = (s32[8]{0:T(128)S(1)}, s32[8]{0:T(128)}, u32[]{:S(2)}) copy-start(s32[8]{0:T(128)} %stack.27.meta) | copy-start | bytes 100
  228.0 16.3 %copy-start.6 = (f32[512,512]{1,0:T(8,128)S(1)}, f32[512,512]{1,0:T(8,128)}, u32[]{:S(2)}) copy-start(f32[512,512]{1,0:T(8,128)} %get-tuple-element.162) | copy-start | bytes 3145732
  228.0 17.5 %collective-permute-start.6 = (bf16[320,512]{1,0:T(8,128)(2,1)S(1)}, bf16[320,512]{1,0:T(8,128)(2,1)S(1)}, u32[]{:S(2)}, u32[]{:S(2)}) collective-permute-start(bf16[320,512]{1,0:T(8,128)(2,1)S(1)} %get-tuple-element.164), channel_id=1, source_target_pairs={{0,2},{1,3},{2,0},{3,1},{4,6},{5,7},{6,4},{7,5},{8,10},{9,11},{10,... | collective-permute-start | bytes 983048 | tf_op jit(solution)/shard_map/ppermute | solution.py:1020
  230.7 16.7 %collective-permute-start.7 = (bf16[320,512]{1,0:T(8,128)(2,1)S(1)}, bf16[320,512]{1,0:T(8,128)(2,1)S(1)}, u32[]{:S(2)}, u32[]{:S(2)}) collective-permute-start(bf16[320,512]{1,0:T(8,128)(2,1)S(1)} %get-tuple-element.165), channel_id=1, source_target_pairs={{0,4},{1,5},{2,6},{3,7},{4,0},{5,1},{6,2},{7,3},{8,12},{9,13},{10,... | collective-permute-start | bytes 983048 | tf_op jit(solution)/shard_map/ppermute | solution.py:1020
  232.2 15.2 %collective-permute-start.8 = (bf16[320,512]{1,0:T(8,128)(2,1)S(1)}, bf16[320,512]{1,0:T(8,128)(2,1)S(1)}, u32[]{:S(2)}, u32[]{:S(2)}) collective-permute-start(bf16[320,512]{1,0:T(8,128)(2,1)S(1)} %get-tuple-element.166), channel_id=1, source_target_pairs={{0,6},{1,7},{2,4},{3,5},{4,2},{5,3},{6,0},{7,1},{8,14},{9,15},{10,... | collective-permute-start | bytes 983048 | tf_op jit(solution)/shard_map/ppermute | solution.py:1020
  248.2 11.8 %collective-permute-start.10 = (bf16[80,512]{1,0:T(8,128)(2,1)S(1)}, bf16[80,512]{1,0:T(8,128)(2,1)S(1)}, u32[]{:S(2)}, u32[]{:S(2)}) collective-permute-start(bf16[80,512]{1,0:T(8,128)(2,1)S(1)} %get-tuple-element.179), channel_id=1, source_target_pairs={{0,16},{1,17},{2,18},{3,19},{4,20},{5,21},{6,22},{7,23},{8,24},{9,... | collective-permute-start | bytes 245768 | tf_op jit(solution)/shard_map/ppermute | solution.py:1020
  250.9 9.3 %collective-permute-start.11 = (bf16[80,512]{1,0:T(8,128)(2,1)S(1)}, bf16[80,512]{1,0:T(8,128)(2,1)S(1)}, u32[]{:S(2)}, u32[]{:S(2)}) collective-permute-start(bf16[80,512]{1,0:T(8,128)(2,1)S(1)} %get-tuple-element.180), channel_id=1, source_target_pairs={{0,24},{1,25},{2,26},{3,27},{4,28},{5,29},{6,30},{7,31},{8,16},{9,... | collective-permute-start | bytes 245768 | tf_op jit(solution)/shard_map/ppermute | solution.py:1020
  252.2 9.1 %collective-permute-start.9 = (bf16[80,512]{1,0:T(8,128)(2,1)S(1)}, bf16[80,512]{1,0:T(8,128)(2,1)S(1)}, u32[]{:S(2)}, u32[]{:S(2)}) collective-permute-start(bf16[80,512]{1,0:T(8,128)(2,1)S(1)} %get-tuple-element.178), channel_id=1, source_target_pairs={{0,8},{1,9},{2,10},{3,11},{4,12},{5,13},{6,14},{7,15},{8,0},{9,1},... | collective-permute-start | bytes 245768 | tf_op jit(solution)/shard_map/ppermute | solution.py:1020
  267.8 8.3 %collective-permute-start.12 = (bf16[80,512]{1,0:T(8,128)(2,1)S(1)}, bf16[80,512]{1,0:T(8,128)(2,1)S(1)}, u32[]{:S(2)}, u32[]{:S(2)}) collective-permute-start(bf16[80,512]{1,0:T(8,128)(2,1)S(1)} %sum_parts.1.refs_0_), channel_id=1, source_target_pairs={{0,8},{1,9},{2,10},{3,11},{4,12},{5,13},{6,14},{7,15},{8,0},{9,1},... | collective-permute-start | bytes 245768 | tf_op jit(solution)/shard_map/ppermute | solution.py:1020
  269.0 8.6 %collective-permute-start.13 = (bf16[80,512]{1,0:T(8,128)(2,1)S(1)}, bf16[80,512]{1,0:T(8,128)(2,1)S(1)}, u32[]{:S(2)}, u32[]{:S(2)}) collective-permute-start(bf16[80,512]{1,0:T(8,128)(2,1)S(1)} %sum_parts.1.refs_0_), channel_id=1, source_target_pairs={{0,16},{1,17},{2,18},{3,19},{4,20},{5,21},{6,22},{7,23},{8,24},{9,... | collective-permute-start | bytes 245768 | tf_op jit(solution)/shard_map/ppermute | solution.py:1020
  270.8 6.8 %collective-permute-start.14 = (bf16[80,512]{1,0:T(8,128)(2,1)S(1)}, bf16[80,512]{1,0:T(8,128)(2,1)S(1)}, u32[]{:S(2)}, u32[]{:S(2)}) collective-permute-start(bf16[80,512]{1,0:T(8,128)(2,1)S(1)} %sum_parts.1.refs_0_), channel_id=1, source_target_pairs={{0,24},{1,25},{2,26},{3,27},{4,28},{5,29},{6,30},{7,31},{8,16},{9,... | collective-permute-start | bytes 245768 | tf_op jit(solution)/shard_map/ppermute | solution.py:1020
  278.2 15.6 %collective-permute-start.15 = (bf16[320,512]{1,0:T(8,128)(2,1)S(1)}, bf16[320,512]{1,0:T(8,128)(2,1)S(1)}, u32[]{:S(2)}, u32[]{:S(2)}) collective-permute-start(bf16[320,512]{1,0:T(8,128)(2,1)S(1)} %assemble.2.refs_0_), channel_id=1, source_target_pairs={{0,2},{1,3},{2,0},{3,1},{4,6},{5,7},{6,4},{7,5},{8,10},{9,11},{10,... | collective-permute-start | bytes 983048 | tf_op jit(solution)/shard_map/ppermute | solution.py:1020
  279.9 13.9 %collective-permute-start.16 = (bf16[320,512]{1,0:T(8,128)(2,1)S(1)}, bf16[320,512]{1,0:T(8,128)(2,1)S(1)}, u32[]{:S(2)}, u32[]{:S(2)}) collective-permute-start(bf16[320,512]{1,0:T(8,128)(2,1)S(1)} %assemble.2.refs_0_), channel_id=1, source_target_pairs={{0,4},{1,5},{2,6},{3,7},{4,0},{5,1},{6,2},{7,3},{8,12},{9,13},{10,... | collective-permute-start | bytes 983048 | tf_op jit(solution)/shard_map/ppermute | solution.py:1020
  280.5 20.6 %collective-permute-start.17 = (bf16[320,512]{1,0:T(8,128)(2,1)S(1)}, bf16[320,512]{1,0:T(8,128)(2,1)S(1)}, u32[]{:S(2)}, u32[]{:S(2)}) collective-permute-start(bf16[320,512]{1,0:T(8,128)(2,1)S(1)} %assemble.2.refs_0_), channel_id=1, source_target_pairs={{0,6},{1,7},{2,4},{3,5},{4,2},{5,3},{6,0},{7,1},{8,14},{9,15},{10,... | collective-permute-start | bytes 983048 | tf_op jit(solution)/shard_map/ppermute | solution.py:1020
  311.2 11.1 %collective-permute-start.19 = (bf16[2048,512]{1,0:T(8,128)(2,1)}, bf16[2048,512]{1,0:T(8,128)(2,1)}, u32[]{:S(2)}, u32[]{:S(2)}) collective-permute-start(bf16[2048,512]{1,0:T(8,128)(2,1)} %all-gather.2.cloned.1.call-done.source), channel_id=1, source_target_pairs={{0,1},{1,0},{2,3},{3,2},{4,5},{5,4},{6,7},{7,6},{8,9},{9,8},{10,11... | collective-permute-start | bytes 6291464 | tf_op jit(solution)/shard_map/ppermute | solution.py:31
  311.9 5.3 %copy-start = (bf16[1280,512]{1,0:T(8,128)(2,1)}, bf16[1280,512]{1,0:T(8,128)(2,1)S(1)}, u32[]{:S(2)}) copy-start(bf16[1280,512]{1,0:T(8,128)(2,1)S(1)} %assemble.3.own) | copy-start | bytes 3932164
  311.9 5.3 %collective-permute-start.18 = (bf16[1280,512]{1,0:T(8,128)(2,1)S(1)}, bf16[1280,512]{1,0:T(8,128)(2,1)S(1)}, u32[]{:S(2)}, u32[]{:S(2)}) collective-permute-start(bf16[1280,512]{1,0:T(8,128)(2,1)S(1)} %assemble.3.own), channel_id=1, source_target_pairs={{0,1},{1,0},{2,3},{3,2},{4,5},{5,4},{6,7},{7,6},{8,9},{9,8},{10,11... | collective-permute-start | bytes 3932168 | tf_op jit(solution)/shard_map/ppermute | solution.py:31
  317.2 1.1 copy-start.3
Sparse Core Ops, SparseCore 0:
  180.7 37.5 reduce-scatter.1
  222.5 45.2 all-reduce.1
  269.8 41.3 all-gather.1
